TPU v7x, 512 devices: a whole 4x8x8 slice. The times are simulated.
512 devices in a mesh: gx: 64 (over z, x, core), gy: 8 (over y).
Axes of the slice: x: 4, y: 8, z: 8, core: 2. Of those that a mesh axis runs over, the one named last changes fastest.
Arguments:
- right_side: float32 [9, 1024, 4096], P(None, 'gx', 'gy'), may hold values from -6 to 6
- guess: float32 [9, 1024, 4096], P(None, 'gx', 'gy'), may hold values from -3 to 3
- vertical_coef: float32 [1024, 4096], P('gx', 'gy'), may hold values from 0.005 to 0.1
- breaking: int32 [1024, 4096], P('gx', 'gy'), may hold values 0 or 1
Outputs:
- updated: float32 [9, 1024, 4096], P(None, 'gx', 'gy')
- new_defect: float32 [9, 1024, 4096], P(None, 'gx', 'gy')
All inputs are finite; a program needn't handle non-finite values. No bound on the sum of `breaking` on one device may be relied on, other than what follows from the above.
Results may differ from a plain program's by a relative error of at most 0.0003.
Values sent between devices are 32-bit elements; how exact they have to be, the bound alone decides.
No kernel may reach another device: no remote copies, remote signals or barrier semaphores. Data moves between devices by JAX's collectives and lax.ppermute only.
A program may use at most 128 MiB of HBM per device.

v0:
```python
import jax
import jax.numpy as jnp
from jax import lax
from jax.sharding import PartitionSpec as P

LEVELS = 5
POST = 2
COARSE = 8


damping = 0.8
break_gain = 0.05


def extended(cells, sides, width):
    for axis, dim in sides:
        count = lax.axis_size(axis)
        ends = count - 1
        head = lax.slice_in_dim(cells, 0, width, axis=dim)
        tail = lax.slice_in_dim(cells, cells.shape[dim] - width, cells.shape[dim], axis=dim)
        cells = jnp.concatenate(
            [
                lax.ppermute(tail, axis, [(i, (i + 1) % count) for i in range(ends)]),
                cells,
                lax.ppermute(head, axis, [((i + 1) % count, i) for i in range(ends)]),
            ],
            axis=dim,
        )
    return cells


def coarsen(field):
    row_count, col_count = field.shape
    return field.reshape(row_count // 2, 2, col_count // 2, 2).mean(axis=(1, 3))


def fold_pairs(padded, axis):
    count = (padded.shape[axis] - 2) // 2

    def pick_rows(start):
        return lax.slice_in_dim(padded, start, start + 2 * count - 1, 2, axis)

    return (pick_rows(0) + 3.0 * pick_rows(1) + 3.0 * pick_rows(2) + pick_rows(3)) * 0.125


def prolong(coarse):
    depth, row_count, col_count = coarse.shape
    wide = jnp.broadcast_to(coarse[:, :, None, :, None], (depth, row_count, 2, col_count, 2))
    return wide.reshape(depth, 2 * row_count, 2 * col_count)


def local_apply(field, padded, vert_coef, center, scale):
    horizontal = (
        padded[:, 2:, 1:-1] + padded[:, :-2, 1:-1] + padded[:, 1:-1, 2:] + padded[:, 1:-1, :-2]
    )
    stacked = jnp.pad(field, ((1, 1), (0, 0), (0, 0)))
    vertical = stacked[2:] + stacked[:-2]
    return center * field - scale * horizontal - vert_coef * vertical


def restrict(residual):
    padded = extended(residual, (("gx", 1), ("gy", 2)), 1)
    result = fold_pairs(fold_pairs(padded, 1), 2)
    return result


def shards(right_side, guess, vertical_coef, breaking):
    vert_list = [vertical_coef]
    break_list = [break_gain * breaking.astype(jnp.float32)]
    for level in range(1, LEVELS):
        vert_list.append(coarsen(vert_list[-1]))
        break_list.append(coarsen(break_list[-1]))
    center_list = [
        4.0 * 0.25**level + 2.0 * vert_list[level] + break_list[level] for level in range(LEVELS)
    ]

    def operate(field, level):
        padded = extended(field, (("gx", 1), ("gy", 2)), 1)
        return local_apply(field, padded, vert_list[level], center_list[level], 0.25**level)

    def coarse_solve(source, level):
        center = center_list[level]
        scale = 0.25**level
        iterate = damping * source / center
        for sweep in range(1, COARSE):
            padded = extended(iterate, (("gx", 1), ("gy", 2)), 1)
            applied = local_apply(iterate, padded, vert_list[level], center, scale)
            iterate = iterate + damping * (source - applied) / center
        return iterate

    def cycle(source, level):
        if level == LEVELS - 1:
            return coarse_solve(source, level)
        center = center_list[level]
        iterate = damping * source / center
        iterate = iterate + damping * (source - operate(iterate, level)) / center
        residual = source - operate(iterate, level)
        iterate = iterate + prolong(cycle(restrict(residual), level + 1))
        for sweep in range(POST):
            iterate = iterate + damping * (source - operate(iterate, level)) / center
        return iterate

    defect = right_side - operate(guess, 0)
    updated = guess + cycle(defect, 0)
    new_defect = right_side - operate(updated, 0)
    return (updated, new_defect)


def solution(mesh):
    in_specs = (P(None, "gx", "gy"), P(None, "gx", "gy"), P("gx", "gy"), P("gx", "gy"))
    out_specs = (P(None, "gx", "gy"), P(None, "gx", "gy"))
    return jax.shard_map(shards, mesh=mesh, in_specs=in_specs, out_specs=out_specs, check_vma=False)
```

profile of v0, /device:TPU:231, one launch (start us, length us, event | category | flops | bytes accessed | tf_op | source)
XLA Modules:
  0.0 630.7 jit_solution(17844921491838680667)
XLA Ops:
  1.9 5.7 collective-permute-start.1
  10.7 5.5 collective-permute-done
  31.3 6.6 %collective-permute-done.4 = f32[9,1,512]{2,0,1:T(8,128)S(1)} collective-permute-done((f32[9,1,512]{2,0,1:T(8,128)S(1)}, f32[9,1,512]{2,0,1:T(8,128)S(1)}, u32[]{:S(2)}, u32[]{:S(2)}) %collective-permute-start.4) | collective-permute-done | bytes 18464 | tf_op jit(solution)/shard_map/ppermute | solution.py:25
  52.6 6.6 %collective-permute-done.8 = f32[9,1,512]{2,0,1:T(8,128)S(1)} collective-permute-done((f32[9,1,512]{2,0,1:T(8,128)S(1)}, f32[9,1,512]{2,0,1:T(8,128)S(1)}, u32[]{:S(2)}, u32[]{:S(2)}) %collective-permute-start.8) | collective-permute-done | bytes 18464 | tf_op jit(solution)/shard_map/ppermute | solution.py:25
  105.5 6.7 %collective-permute-start.17 = (f32[9,1,256]{2,0,1:T(8,128)S(1)}, f32[9,1,256]{2,0,1:T(8,128)S(1)}, u32[]{:S(2)}, u32[]{:S(2)}) collective-permute-start(f32[9,1,256]{2,0,1:T(8,128)S(1)} %get-tuple-element.60), channel_id=1, source_target_pairs={{0,8},{8,16},{16,24},{24,32},{32,40},{40,48},{48,56},{56,64},{64,7... | collective-permute-start | bytes 27656 | tf_op jit(solution)/shard_map/ppermute | solution.py:23
  114.1 6.4 %collective-permute-done.16 = f32[9,1,256]{2,0,1:T(8,128)S(1)} collective-permute-done((f32[9,1,256]{2,0,1:T(8,128)S(1)}, f32[9,1,256]{2,0,1:T(8,128)S(1)}, u32[]{:S(2)}, u32[]{:S(2)}) %collective-permute-start.16) | collective-permute-done | bytes 9248 | tf_op jit(solution)/shard_map/ppermute | solution.py:25
  120.7 5.3 collective-permute-start.18
  138.0 6.3 collective-permute-done.20
  159.2 5.2 collective-permute-done.25
  180.7 6.4 %collective-permute-done.28 = f32[9,1,128]{2,0,1:T(8,128)S(1)} collective-permute-done((f32[9,1,128]{2,0,1:T(8,128)S(1)}, f32[9,1,128]{2,0,1:T(8,128)S(1)}, u32[]{:S(2)}, u32[]{:S(2)}) %collective-permute-start.28) | collective-permute-done | bytes 4640 | tf_op jit(solution)/shard_map/ppermute | solution.py:25
  187.1 5.2 collective-permute-start.30
  203.8 6.4 %collective-permute-done.32 = f32[9,1,128]{2,0,1:T(8,128)S(1)} collective-permute-done((f32[9,1,128]{2,0,1:T(8,128)S(1)}, f32[9,1,128]{2,0,1:T(8,128)S(1)}, u32[]{:S(2)}, u32[]{:S(2)}) %collective-permute-start.32) | collective-permute-done | bytes 4640 | tf_op jit(solution)/shard_map/ppermute | solution.py:25
  223.9 5.9 collective-permute-done.37
  243.8 6.4 %collective-permute-done.40 = f32[9,1,64]{2,0,1:T(8,128)S(1)} collective-permute-done((f32[9,1,64]{2,0,1:T(8,128)S(1)}, f32[9,1,64]{2,0,1:T(8,128)S(1)}, u32[]{:S(2)}, u32[]{:S(2)}) %collective-permute-start.40) | collective-permute-done | bytes 2336 | tf_op jit(solution)/shard_map/ppermute | solution.py:25
  266.7 6.4 %collective-permute-done.44 = f32[9,1,64]{2,0,1:T(8,128)S(1)} collective-permute-done((f32[9,1,64]{2,0,1:T(8,128)S(1)}, f32[9,1,64]{2,0,1:T(8,128)S(1)}, u32[]{:S(2)}, u32[]{:S(2)}) %collective-permute-start.44) | collective-permute-done | bytes 2336 | tf_op jit(solution)/shard_map/ppermute | solution.py:25
  286.5 5.9 collective-permute-done.49
  305.7 6.4 %collective-permute-done.52 = f32[9,1,32]{2,0,1:T(8,128)S(1)} collective-permute-done((f32[9,1,32]{2,0,1:T(8,128)S(1)}, f32[9,1,32]{2,0,1:T(8,128)S(1)}, u32[]{:S(2)}, u32[]{:S(2)}) %collective-permute-start.52) | collective-permute-done | bytes 1184 | tf_op jit(solution)/shard_map/ppermute | solution.py:25
  328.5 6.4 %collective-permute-done.56 = f32[9,1,32]{2,0,1:T(8,128)S(1)} collective-permute-done((f32[9,1,32]{2,0,1:T(8,128)S(1)}, f32[9,1,32]{2,0,1:T(8,128)S(1)}, u32[]{:S(2)}, u32[]{:S(2)}) %collective-permute-start.56) | collective-permute-done | bytes 1184 | tf_op jit(solution)/shard_map/ppermute | solution.py:25
  347.8 6.4 %collective-permute-done.60 = f32[9,1,32]{2,0,1:T(8,128)S(1)} collective-permute-done((f32[9,1,32]{2,0,1:T(8,128)S(1)}, f32[9,1,32]{2,0,1:T(8,128)S(1)}, u32[]{:S(2)}, u32[]{:S(2)}) %collective-permute-start.60) | collective-permute-done | bytes 1184 | tf_op jit(solution)/shard_map/ppermute | solution.py:25
  367.1 6.4 %collective-permute-done.64 = f32[9,1,32]{2,0,1:T(8,128)S(1)} collective-permute-done((f32[9,1,32]{2,0,1:T(8,128)S(1)}, f32[9,1,32]{2,0,1:T(8,128)S(1)}, u32[]{:S(2)}, u32[]{:S(2)}) %collective-permute-start.64) | collective-permute-done | bytes 1184 | tf_op jit(solution)/shard_map/ppermute | solution.py:25
  386.3 6.4 %collective-permute-done.68 = f32[9,1,32]{2,0,1:T(8,128)S(1)} collective-permute-done((f32[9,1,32]{2,0,1:T(8,128)S(1)}, f32[9,1,32]{2,0,1:T(8,128)S(1)}, u32[]{:S(2)}, u32[]{:S(2)}) %collective-permute-start.68) | collective-permute-done | bytes 1184 | tf_op jit(solution)/shard_map/ppermute | solution.py:25
  405.6 6.4 %collective-permute-done.72 = f32[9,1,32]{2,0,1:T(8,128)S(1)} collective-permute-done((f32[9,1,32]{2,0,1:T(8,128)S(1)}, f32[9,1,32]{2,0,1:T(8,128)S(1)}, u32[]{:S(2)}, u32[]{:S(2)}) %collective-permute-start.72) | collective-permute-done | bytes 1184 | tf_op jit(solution)/shard_map/ppermute | solution.py:25
  424.9 6.4 %collective-permute-done.76 = f32[9,1,32]{2,0,1:T(8,128)S(1)} collective-permute-done((f32[9,1,32]{2,0,1:T(8,128)S(1)}, f32[9,1,32]{2,0,1:T(8,128)S(1)}, u32[]{:S(2)}, u32[]{:S(2)}) %collective-permute-start.76) | collective-permute-done | bytes 1184 | tf_op jit(solution)/shard_map/ppermute | solution.py:25
  444.3 6.4 %collective-permute-done.80 = f32[9,1,64]{2,0,1:T(8,128)S(1)} collective-permute-done((f32[9,1,64]{2,0,1:T(8,128)S(1)}, f32[9,1,64]{2,0,1:T(8,128)S(1)}, u32[]{:S(2)}, u32[]{:S(2)}) %collective-permute-start.80) | collective-permute-done | bytes 2336 | tf_op jit(solution)/shard_map/ppermute | solution.py:25
  463.7 6.4 %collective-permute-done.84 = f32[9,1,64]{2,0,1:T(8,128)S(1)} collective-permute-done((f32[9,1,64]{2,0,1:T(8,128)S(1)}, f32[9,1,64]{2,0,1:T(8,128)S(1)}, u32[]{:S(2)}, u32[]{:S(2)}) %collective-permute-start.84) | collective-permute-done | bytes 2336 | tf_op jit(solution)/shard_map/ppermute | solution.py:25
  483.4 6.4 %collective-permute-done.88 = f32[9,1,128]{2,0,1:T(8,128)S(1)} collective-permute-done((f32[9,1,128]{2,0,1:T(8,128)S(1)}, f32[9,1,128]{2,0,1:T(8,128)S(1)}, u32[]{:S(2)}, u32[]{:S(2)}) %collective-permute-start.88) | collective-permute-done | bytes 4640 | tf_op jit(solution)/shard_map/ppermute | solution.py:25
  502.9 6.4 %collective-permute-done.92 = f32[9,1,128]{2,0,1:T(8,128)S(1)} collective-permute-done((f32[9,1,128]{2,0,1:T(8,128)S(1)}, f32[9,1,128]{2,0,1:T(8,128)S(1)}, u32[]{:S(2)}, u32[]{:S(2)}) %collective-permute-start.92) | collective-permute-done | bytes 4640 | tf_op jit(solution)/shard_map/ppermute | solution.py:25
  523.5 6.4 %collective-permute-done.96 = f32[9,1,256]{2,0,1:T(8,128)S(1)} collective-permute-done((f32[9,1,256]{2,0,1:T(8,128)S(1)}, f32[9,1,256]{2,0,1:T(8,128)S(1)}, u32[]{:S(2)}, u32[]{:S(2)}) %collective-permute-start.96) | collective-permute-done | bytes 9248 | tf_op jit(solution)/shard_map/ppermute | solution.py:25
  543.6 6.4 %collective-permute-done.100 = f32[9,1,256]{2,0,1:T(8,128)S(1)} collective-permute-done((f32[9,1,256]{2,0,1:T(8,128)S(1)}, f32[9,1,256]{2,0,1:T(8,128)S(1)}, u32[]{:S(2)}, u32[]{:S(2)}) %collective-permute-start.100) | collective-permute-done | bytes 9248 | tf_op jit(solution)/shard_map/ppermute | solution.py:25
  570.8 6.6 %collective-permute-done.104 = f32[9,1,512]{2,0,1:T(8,128)S(1)} collective-permute-done((f32[9,1,512]{2,0,1:T(8,128)S(1)}, f32[9,1,512]{2,0,1:T(8,128)S(1)}, u32[]{:S(2)}, u32[]{:S(2)}) %collective-permute-start.104) | collective-permute-done | bytes 18464 | tf_op jit(solution)/shard_map/ppermute | solution.py:25
  592.1 6.6 %collective-permute-done.108 = f32[9,1,512]{2,0,1:T(8,128)S(1)} collective-permute-done((f32[9,1,512]{2,0,1:T(8,128)S(1)}, f32[9,1,512]{2,0,1:T(8,128)S(1)}, u32[]{:S(2)}, u32[]{:S(2)}) %collective-permute-start.108) | collective-permute-done | bytes 18464 | tf_op jit(solution)/shard_map/ppermute | solution.py:25
  613.5 6.6 %collective-permute-done.112 = f32[9,1,512]{2,0,1:T(8,128)S(1)} collective-permute-done((f32[9,1,512]{2,0,1:T(8,128)S(1)}, f32[9,1,512]{2,0,1:T(8,128)S(1)}, u32[]{:S(2)}, u32[]{:S(2)}) %collective-permute-start.112) | collective-permute-done | bytes 18464 | tf_op jit(solution)/shard_map/ppermute | solution.py:25
  (379 shorter events, 428.8 us)
Async XLA Ops:
  7.6 8.6 %collective-permute-start = (f32[9,1,512]{2,0,1:T(8,128)S(1)}, f32[9,1,512]{2,0,1:T(8,128)S(1)}, u32[]{:S(2)}, u32[]{:S(2)}) collective-permute-start(f32[9,1,512]{2,0,1:T(8,128)S(1)} %get-tuple-element.40), channel_id=1, source_target_pairs={{8,0},{16,8},{24,16},{32,24},{40,32},{48,40},{56,48},{64,56},{72,6... | collective-permute-start | bytes 55304 | tf_op jit(solution)/shard_map/ppermute | solution.py:25
  29.4 8.6 %collective-permute-start.4 = (f32[9,1,512]{2,0,1:T(8,128)S(1)}, f32[9,1,512]{2,0,1:T(8,128)S(1)}, u32[]{:S(2)}, u32[]{:S(2)}) collective-permute-start(f32[9,1,512]{2,0,1:T(8,128)S(1)} %get-tuple-element.39), channel_id=1, source_target_pairs={{8,0},{16,8},{24,16},{32,24},{40,32},{48,40},{56,48},{64,56},{72,6... | collective-permute-start | bytes 55304 | tf_op jit(solution)/shard_map/ppermute | solution.py:25
  50.7 8.6 %collective-permute-start.8 = (f32[9,1,512]{2,0,1:T(8,128)S(1)}, f32[9,1,512]{2,0,1:T(8,128)S(1)}, u32[]{:S(2)}, u32[]{:S(2)}) collective-permute-start(f32[9,1,512]{2,0,1:T(8,128)S(1)} %get-tuple-element.37), channel_id=1, source_target_pairs={{8,0},{16,8},{24,16},{32,24},{40,32},{48,40},{56,48},{64,56},{72,6... | collective-permute-start | bytes 55304 | tf_op jit(solution)/shard_map/ppermute | solution.py:25
  69.5 12.8 %collective-permute-start.12 = (f32[9,1,512]{2,0,1:T(8,128)}, f32[9,1,512]{2,0,1:T(8,128)}, u32[]{:S(2)}, u32[]{:S(2)}) collective-permute-start(f32[9,1,512]{2,0,1:T(8,128)} %get-tuple-element.34), channel_id=1, source_target_pairs={{0,8},{8,16},{16,24},{24,32},{32,40},{40,48},{48,56},{56,64},{64,7... | collective-permute-start | bytes 55304 | tf_op jit(solution)/shard_map/ppermute | solution.py:23
  72.6 9.7 %collective-permute-start.13 = (f32[9,1,512]{2,0,1:T(8,128)}, f32[9,1,512]{2,0,1:T(8,128)}, u32[]{:S(2)}, u32[]{:S(2)}) collective-permute-start(f32[9,1,512]{2,0,1:T(8,128)} %get-tuple-element.35), channel_id=1, source_target_pairs={{8,0},{16,8},{24,16},{32,24},{40,32},{48,40},{56,48},{64,56},{72,6... | collective-permute-start | bytes 55304 | tf_op jit(solution)/shard_map/ppermute | solution.py:25
  83.4 8.6 %collective-permute-start.14 = (f32[9,18,1]{2,0,1:T(8,128)S(1)}, f32[9,18,1]{2,0,1:T(8,128)S(1)}, u32[]{:S(2)}, u32[]{:S(2)}) collective-permute-start(f32[9,18,1]{2,0,1:T(8,128)S(1)} %get-tuple-element.20), channel_id=1, source_target_pairs={{0,1},{1,2},{2,3},{3,4},{4,5},{5,6},{6,7},{8,9},{9,10},{10,11},{11... | collective-permute-start | bytes 1952 | tf_op jit(solution)/shard_map/ppermute | solution.py:23
  105.5 8.6 %collective-permute-start.17 = (f32[9,1,256]{2,0,1:T(8,128)S(1)}, f32[9,1,256]{2,0,1:T(8,128)S(1)}, u32[]{:S(2)}, u32[]{:S(2)}) collective-permute-start(f32[9,1,256]{2,0,1:T(8,128)S(1)} %get-tuple-element.60), channel_id=1, source_target_pairs={{0,8},{8,16},{16,24},{24,32},{32,40},{40,48},{48,56},{56,64},{64,7... | collective-permute-start | bytes 27656 | tf_op jit(solution)/shard_map/ppermute | solution.py:23
  112.2 8.4 %collective-permute-start.16 = (f32[9,1,256]{2,0,1:T(8,128)S(1)}, f32[9,1,256]{2,0,1:T(8,128)S(1)}, u32[]{:S(2)}, u32[]{:S(2)}) collective-permute-start(f32[9,1,256]{2,0,1:T(8,128)S(1)} %get-tuple-element.61), channel_id=1, source_target_pairs={{8,0},{16,8},{24,16},{32,24},{40,32},{48,40},{56,48},{64,56},{72,6... | collective-permute-start | bytes 27656 | tf_op jit(solution)/shard_map/ppermute | solution.py:25
  135.9 8.4 %collective-permute-start.20 = (f32[9,1,256]{2,0,1:T(8,128)S(1)}, f32[9,1,256]{2,0,1:T(8,128)S(1)}, u32[]{:S(2)}, u32[]{:S(2)}) collective-permute-start(f32[9,1,256]{2,0,1:T(8,128)S(1)} %get-tuple-element.59), channel_id=1, source_target_pairs={{8,0},{16,8},{24,16},{32,24},{40,32},{48,40},{56,48},{64,56},{72,6... | collective-permute-start | bytes 27656 | tf_op jit(solution)/shard_map/ppermute | solution.py:25
  156.0 8.4 %collective-permute-start.25 = (f32[9,1,256]{2,0,1:T(8,128)S(1)}, f32[9,1,256]{2,0,1:T(8,128)S(1)}, u32[]{:S(2)}, u32[]{:S(2)}) collective-permute-start(f32[9,1,256]{2,0,1:T(8,128)S(1)} %get-tuple-element.57), channel_id=1, source_target_pairs={{8,0},{16,8},{24,16},{32,24},{40,32},{48,40},{56,48},{64,56},{72,6... | collective-permute-start | bytes 27656 | tf_op jit(solution)/shard_map/ppermute | solution.py:25
  178.8 8.3 %collective-permute-start.28 = (f32[9,1,128]{2,0,1:T(8,128)S(1)}, f32[9,1,128]{2,0,1:T(8,128)S(1)}, u32[]{:S(2)}, u32[]{:S(2)}) collective-permute-start(f32[9,1,128]{2,0,1:T(8,128)S(1)} %get-tuple-element.91), channel_id=1, source_target_pairs={{8,0},{16,8},{24,16},{32,24},{40,32},{48,40},{56,48},{64,56},{72,6... | collective-permute-start | bytes 13832 | tf_op jit(solution)/shard_map/ppermute | solution.py:25
  201.9 8.3 %collective-permute-start.32 = (f32[9,1,128]{2,0,1:T(8,128)S(1)}, f32[9,1,128]{2,0,1:T(8,128)S(1)}, u32[]{:S(2)}, u32[]{:S(2)}) collective-permute-start(f32[9,1,128]{2,0,1:T(8,128)S(1)} %get-tuple-element.89), channel_id=1, source_target_pairs={{8,0},{16,8},{24,16},{32,24},{40,32},{48,40},{56,48},{64,56},{72,6... | collective-permute-start | bytes 13832 | tf_op jit(solution)/shard_map/ppermute | solution.py:25
  221.5 8.3 %collective-permute-start.37 = (f32[9,1,128]{2,0,1:T(8,128)S(1)}, f32[9,1,128]{2,0,1:T(8,128)S(1)}, u32[]{:S(2)}, u32[]{:S(2)}) collective-permute-start(f32[9,1,128]{2,0,1:T(8,128)S(1)} %get-tuple-element.87), channel_id=1, source_target_pairs={{8,0},{16,8},{24,16},{32,24},{40,32},{48,40},{56,48},{64,56},{72,6... | collective-permute-start | bytes 13832 | tf_op jit(solution)/shard_map/ppermute | solution.py:25
  241.9 8.3 %collective-permute-start.40 = (f32[9,1,64]{2,0,1:T(8,128)S(1)}, f32[9,1,64]{2,0,1:T(8,128)S(1)}, u32[]{:S(2)}, u32[]{:S(2)}) collective-permute-start(f32[9,1,64]{2,0,1:T(8,128)S(1)} %get-tuple-element.117), channel_id=1, source_target_pairs={{8,0},{16,8},{24,16},{32,24},{40,32},{48,40},{56,48},{64,56},{72,6... | collective-permute-start | bytes 6920 | tf_op jit(solution)/shard_map/ppermute | solution.py:25
  264.8 8.3 %collective-permute-start.44 = (f32[9,1,64]{2,0,1:T(8,128)S(1)}, f32[9,1,64]{2,0,1:T(8,128)S(1)}, u32[]{:S(2)}, u32[]{:S(2)}) collective-permute-start(f32[9,1,64]{2,0,1:T(8,128)S(1)} %get-tuple-element.115), channel_id=1, source_target_pairs={{8,0},{16,8},{24,16},{32,24},{40,32},{48,40},{56,48},{64,56},{72,6... | collective-permute-start | bytes 6920 | tf_op jit(solution)/shard_map/ppermute | solution.py:25
  284.2 8.3 %collective-permute-start.49 = (f32[9,1,64]{2,0,1:T(8,128)S(1)}, f32[9,1,64]{2,0,1:T(8,128)S(1)}, u32[]{:S(2)}, u32[]{:S(2)}) collective-permute-start(f32[9,1,64]{2,0,1:T(8,128)S(1)} %get-tuple-element.113), channel_id=1, source_target_pairs={{8,0},{16,8},{24,16},{32,24},{40,32},{48,40},{56,48},{64,56},{72,6... | collective-permute-start | bytes 6920 | tf_op jit(solution)/shard_map/ppermute | solution.py:25
  303.8 8.3 %collective-permute-start.52 = (f32[9,1,32]{2,0,1:T(8,128)S(1)}, f32[9,1,32]{2,0,1:T(8,128)S(1)}, u32[]{:S(2)}, u32[]{:S(2)}) collective-permute-start(f32[9,1,32]{2,0,1:T(8,128)S(1)} %get-tuple-element.4), channel_id=1, source_target_pairs={{8,0},{16,8},{24,16},{32,24},{40,32},{48,40},{56,48},{64,56},{72,6... | collective-permute-start | bytes 3464 | tf_op jit(solution)/shard_map/ppermute | solution.py:25
  326.6 8.3 %collective-permute-start.56 = (f32[9,1,32]{2,0,1:T(8,128)S(1)}, f32[9,1,32]{2,0,1:T(8,128)S(1)}, u32[]{:S(2)}, u32[]{:S(2)}) collective-permute-start(f32[9,1,32]{2,0,1:T(8,128)S(1)} %fusion.216), channel_id=1, source_target_pairs={{8,0},{16,8},{24,16},{32,24},{40,32},{48,40},{56,48},{64,56},{72,6... | collective-permute-start | bytes 3464 | tf_op jit(solution)/shard_map/ppermute | solution.py:25
  345.9 8.3 %collective-permute-start.60 = (f32[9,1,32]{2,0,1:T(8,128)S(1)}, f32[9,1,32]{2,0,1:T(8,128)S(1)}, u32[]{:S(2)}, u32[]{:S(2)}) collective-permute-start(f32[9,1,32]{2,0,1:T(8,128)S(1)} %fusion.207), channel_id=1, source_target_pairs={{8,0},{16,8},{24,16},{32,24},{40,32},{48,40},{56,48},{64,56},{72,6... | collective-permute-start | bytes 3464 | tf_op jit(solution)/shard_map/ppermute | solution.py:25
  365.1 8.3 %collective-permute-start.64 = (f32[9,1,32]{2,0,1:T(8,128)S(1)}, f32[9,1,32]{2,0,1:T(8,128)S(1)}, u32[]{:S(2)}, u32[]{:S(2)}) collective-permute-start(f32[9,1,32]{2,0,1:T(8,128)S(1)} %fusion.198), channel_id=1, source_target_pairs={{8,0},{16,8},{24,16},{32,24},{40,32},{48,40},{56,48},{64,56},{72,6... | collective-permute-start | bytes 3464 | tf_op jit(solution)/shard_map/ppermute | solution.py:25
  384.4 8.3 %collective-permute-start.68 = (f32[9,1,32]{2,0,1:T(8,128)S(1)}, f32[9,1,32]{2,0,1:T(8,128)S(1)}, u32[]{:S(2)}, u32[]{:S(2)}) collective-permute-start(f32[9,1,32]{2,0,1:T(8,128)S(1)} %fusion.189), channel_id=1, source_target_pairs={{8,0},{16,8},{24,16},{32,24},{40,32},{48,40},{56,48},{64,56},{72,6... | collective-permute-start | bytes 3464 | tf_op jit(solution)/shard_map/ppermute | solution.py:25
  403.7 8.3 %collective-permute-start.72 = (f32[9,1,32]{2,0,1:T(8,128)S(1)}, f32[9,1,32]{2,0,1:T(8,128)S(1)}, u32[]{:S(2)}, u32[]{:S(2)}) collective-permute-start(f32[9,1,32]{2,0,1:T(8,128)S(1)} %fusion.180), channel_id=1, source_target_pairs={{8,0},{16,8},{24,16},{32,24},{40,32},{48,40},{56,48},{64,56},{72,6... | collective-permute-start | bytes 3464 | tf_op jit(solution)/shard_map/ppermute | solution.py:25
  422.9 8.3 %collective-permute-start.76 = (f32[9,1,32]{2,0,1:T(8,128)S(1)}, f32[9,1,32]{2,0,1:T(8,128)S(1)}, u32[]{:S(2)}, u32[]{:S(2)}) collective-permute-start(f32[9,1,32]{2,0,1:T(8,128)S(1)} %fusion.171), channel_id=1, source_target_pairs={{8,0},{16,8},{24,16},{32,24},{40,32},{48,40},{56,48},{64,56},{72,6... | collective-permute-start | bytes 3464 | tf_op jit(solution)/shard_map/ppermute | solution.py:25
  442.4 8.3 %collective-permute-start.80 = (f32[9,1,64]{2,0,1:T(8,128)S(1)}, f32[9,1,64]{2,0,1:T(8,128)S(1)}, u32[]{:S(2)}, u32[]{:S(2)}) collective-permute-start(f32[9,1,64]{2,0,1:T(8,128)S(1)} %get-tuple-element.111), channel_id=1, source_target_pairs={{8,0},{16,8},{24,16},{32,24},{40,32},{48,40},{56,48},{64,56},{72,6... | collective-permute-start | bytes 6920 | tf_op jit(solution)/shard_map/ppermute | solution.py:25
  461.8 8.3 %collective-permute-start.84 = (f32[9,1,64]{2,0,1:T(8,128)S(1)}, f32[9,1,64]{2,0,1:T(8,128)S(1)}, u32[]{:S(2)}, u32[]{:S(2)}) collective-permute-start(f32[9,1,64]{2,0,1:T(8,128)S(1)} %get-tuple-element.109), channel_id=1, source_target_pairs={{8,0},{16,8},{24,16},{32,24},{40,32},{48,40},{56,48},{64,56},{72,6... | collective-permute-start | bytes 6920 | tf_op jit(solution)/shard_map/ppermute | solution.py:25
  481.4 8.3 %collective-permute-start.88 = (f32[9,1,128]{2,0,1:T(8,128)S(1)}, f32[9,1,128]{2,0,1:T(8,128)S(1)}, u32[]{:S(2)}, u32[]{:S(2)}) collective-permute-start(f32[9,1,128]{2,0,1:T(8,128)S(1)} %get-tuple-element.75), channel_id=1, source_target_pairs={{8,0},{16,8},{24,16},{32,24},{40,32},{48,40},{56,48},{64,56},{72,6... | collective-permute-start | bytes 13832 | tf_op jit(solution)/shard_map/ppermute | solution.py:25
  501.0 8.3 %collective-permute-start.92 = (f32[9,1,128]{2,0,1:T(8,128)S(1)}, f32[9,1,128]{2,0,1:T(8,128)S(1)}, u32[]{:S(2)}, u32[]{:S(2)}) collective-permute-start(f32[9,1,128]{2,0,1:T(8,128)S(1)} %get-tuple-element.73), channel_id=1, source_target_pairs={{8,0},{16,8},{24,16},{32,24},{40,32},{48,40},{56,48},{64,56},{72,6... | collective-permute-start | bytes 13832 | tf_op jit(solution)/shard_map/ppermute | solution.py:25
  521.6 8.4 %collective-permute-start.96 = (f32[9,1,256]{2,0,1:T(8,128)S(1)}, f32[9,1,256]{2,0,1:T(8,128)S(1)}, u32[]{:S(2)}, u32[]{:S(2)}) collective-permute-start(f32[9,1,256]{2,0,1:T(8,128)S(1)} %get-tuple-element.55), channel_id=1, source_target_pairs={{8,0},{16,8},{24,16},{32,24},{40,32},{48,40},{56,48},{64,56},{72,6... | collective-permute-start | bytes 27656 | tf_op jit(solution)/shard_map/ppermute | solution.py:25
  541.7 8.4 %collective-permute-start.100 = (f32[9,1,256]{2,0,1:T(8,128)S(1)}, f32[9,1,256]{2,0,1:T(8,128)S(1)}, u32[]{:S(2)}, u32[]{:S(2)}) collective-permute-start(f32[9,1,256]{2,0,1:T(8,128)S(1)} %get-tuple-element.53), channel_id=1, source_target_pairs={{8,0},{16,8},{24,16},{32,24},{40,32},{48,40},{56,48},{64,56},{72,6... | collective-permute-start | bytes 27656 | tf_op jit(solution)/shard_map/ppermute | solution.py:25
  568.9 8.6 %collective-permute-start.104 = (f32[9,1,512]{2,0,1:T(8,128)S(1)}, f32[9,1,512]{2,0,1:T(8,128)S(1)}, u32[]{:S(2)}, u32[]{:S(2)}) collective-permute-start(f32[9,1,512]{2,0,1:T(8,128)S(1)} %get-tuple-element.33), channel_id=1, source_target_pairs={{8,0},{16,8},{24,16},{32,24},{40,32},{48,40},{56,48},{64,56},{72,6... | collective-permute-start | bytes 55304 | tf_op jit(solution)/shard_map/ppermute | solution.py:25
  590.2 8.6 %collective-permute-start.108 = (f32[9,1,512]{2,0,1:T(8,128)S(1)}, f32[9,1,512]{2,0,1:T(8,128)S(1)}, u32[]{:S(2)}, u32[]{:S(2)}) collective-permute-start(f32[9,1,512]{2,0,1:T(8,128)S(1)} %get-tuple-element.31), channel_id=1, source_target_pairs={{8,0},{16,8},{24,16},{32,24},{40,32},{48,40},{56,48},{64,56},{72,6... | collective-permute-start | bytes 55304 | tf_op jit(solution)/shard_map/ppermute | solution.py:25
  611.6 8.6 %collective-permute-start.112 = (f32[9,1,512]{2,0,1:T(8,128)S(1)}, f32[9,1,512]{2,0,1:T(8,128)S(1)}, u32[]{:S(2)}, u32[]{:S(2)}) collective-permute-start(f32[9,1,512]{2,0,1:T(8,128)S(1)} %get-tuple-element.29), channel_id=1, source_target_pairs={{8,0},{16,8},{24,16},{32,24},{40,32},{48,40},{56,48},{64,56},{72,6... | collective-permute-start | bytes 55304 | tf_op jit(solution)/shard_map/ppermute | solution.py:25
  (89 other events, 597.9 us)
where the time goes:
time: 634 us; the launch traced here: 631 us
  starting transfers between devices  319 us (50%)
  waiting for transfers between devices  260 us (41%)
  local copies, waits for them, and re-layouts  36.9 us (6%)
  other arithmetic  12.2 us (2%)
    ppermute x58, starting transfers between devices, extended(): lax.ppermute(tail, axis, [(i, (i + 1) % count) for i in range(ends)])  185 us
    ppermute x58, waiting for transfers between devices, extended(): lax.ppermute(head, axis, [((i + 1) % count, i) for i in range(ends)])  184 us
    ppermute x58, starting transfers between devices, extended(): lax.ppermute(head, axis, [((i + 1) % count, i) for i in range(ends)])  133 us
    ppermute x58, waiting for transfers between devices, extended(): lax.ppermute(tail, axis, [(i, (i + 1) % count) for i in range(ends)])  76.1 us
    slice x16, local copies, waits for them, and re-layouts, pick_rows(): return lax.slice_in_dim(padded, start, start + 2 * count - 1, 2, axis)  15.2 us
  transfers between devices with their start and end apart: 116, of which 63 were waited for; matrix products, arithmetic and copies ran while one was open for 2% of the time, Pallas kernels for 0%

commit v1 on v0

v1 whole, which is shorter than its diff:
```python
import jax
import jax.numpy as jnp
from jax import lax
from jax.experimental import pallas as pl
from jax.experimental.pallas import tpu as pltpu
from jax.sharding import PartitionSpec as P

K = 9
PLANES = K + 2
VC, BT = K, K + 1
TILES = 23
SIDE = TILES // 2
damping = 0.8
keep = 0.2
break_gain = 0.05
F32 = jnp.float32
BF16 = jnp.bfloat16

COLS_AT = 24 * PLANES
TOP_AT = COLS_AT + 16
BOTTOM_AT = TOP_AT + 16
FAR_AT = BOTTOM_AT + 16
Y_ROWS = FAR_AT + 16


def lanes(rows):
    return lax.broadcasted_iota(jnp.int32, (rows, 128), 1)


def shifted(chunks):
    lane = lanes(chunks[0].shape[0])
    right = [pltpu.roll(v, 1, 1) for v in chunks]
    left = [pltpu.roll(v, 127, 1) for v in chunks]
    n = len(chunks)
    before = [jnp.where(lane == 0, right[c - 1], right[c]) if c else right[c] for c in range(n)]
    after = [jnp.where(lane == 127, left[c + 1], left[c]) if c < n - 1 else left[c] for c in range(n)]
    return before, after


def stencil(x, k, rows, at):
    count = x.shape[1]
    here = pl.ds(at, rows)
    v = [x[k + 1, c, here, :] for c in range(count)]
    before, after = shifted(v)
    out = []
    for c in range(count):
        hs = (x[k + 1, c, pl.ds(at - 1, rows), :] + x[k + 1, c, pl.ds(at + 1, rows), :]) + (before[c] + after[c])
        vs = x[k, c, here, :] + x[k + 2, c, here, :]
        out.append((v[c], hs, vs))
    return out


def each_plane(body, unrolled=False):
    if unrolled:
        for k in range(K):
            body(k)
    else:

        def step(k, carry):
            body(k)
            return carry

        lax.fori_loop(0, K, step, 0)


def clear_edges(x, rows):
    count, total = x.shape[1], x.shape[2]
    for k in (0, K + 1):
        x[k] = jnp.zeros((count, total, 128), F32)
    for k in range(1, K + 1):
        x[k, :, 0:8, :] = jnp.zeros((count, 8, 128), F32)
        x[k, :, 8 + rows : total, :] = jnp.zeros((count, total - 8 - rows, 128), F32)


def scales(f, inv, h):
    for c in range(f.shape[1]):
        vc = f[VC, c]
        center = 4.0 * h + 2.0 * vc + f[BT, c]
        inv[c] = jnp.where(vc > 0.0, damping / center, 0.0)


def first_sweep(x, f, inv, rows, unrolled=False):
    def body(k):
        for c in range(f.shape[1]):
            x[k + 1, c, pl.ds(8, rows), :] = inv[c] * f[k, c]

    each_plane(body, unrolled)


def sweep(x, y, f, inv, rows, h, unrolled=False):
    def body(k):
        for c, (v, hs, vs) in enumerate(stencil(x, k, rows, 8)):
            y[k + 1, c, pl.ds(8, rows), :] = keep * v + inv[c] * (f[k, c] + h * hs + f[VC, c] * vs)

    each_plane(body, unrolled)


def pair_matrix(inputs):
    i = lax.broadcasted_iota(jnp.int32, (inputs, 128), 0)
    j = lax.broadcasted_iota(jnp.int32, (inputs, 128), 1)
    return jnp.where((i == 2 * j) | (i == 2 * j + 1), 0.125, 0.0).astype(BF16)


def copy_matrix(outputs):
    i = lax.broadcasted_iota(jnp.int32, (128, outputs), 0)
    j = lax.broadcasted_iota(jnp.int32, (128, outputs), 1)
    return jnp.where((j == 2 * i) | (j == 2 * i + 1), 1.0, 0.0).astype(BF16)


def exact_dot(values, matrix):
    total = None
    for _ in range(3):
        part = values.astype(BF16)
        values = values - part.astype(F32)
        product = jnp.dot(part, matrix, preferred_element_type=F32)
        total = product if total is None else total + product
    return total


def restrict(x, f, rs, gs, rows, h, base, n, unrolled=False):
    count = f.shape[1]
    pairs = max(count // 2, 1)
    even = lanes(n) % 2 == 0
    rs[:, 0:8, :] = jnp.zeros((count, 8, 128), F32)
    rs[:, 8 + rows : 16 + rows, :] = jnp.zeros((count, 8, 128), F32)

    def put(k, c, value):
        at = pl.multiple_of((k * pairs + c // 2) * n, 8)
        gs[pl.ds(at, n), 128 * (c % 2) : 128 * (c % 2) + 128] = value

    def body(k):
        for c, (v, hs, vs) in enumerate(stencil(x, k, rows, 8)):
            vc = f[VC, c]
            center = 4.0 * h + 2.0 * vc + f[BT, c]
            rs[c, 8 : 8 + rows, :] = jnp.where(vc > 0.0, f[k, c] - center * v + h * hs + vc * vs, 0.0)
        folded = []
        for c in range(count):

            def pick(start):
                return rs[c, pl.ds(8 + base + start, n, stride=2), :]

            folded.append((pick(-1) + 3.0 * (pick(0) + pick(1)) + pick(2)) * 0.125)
        before, after = shifted(folded)
        for c in range(count):
            put(k, c, 3.0 * folded[c] + jnp.where(even, before[c], after[c]))

    each_plane(body, unrolled)
    for k in (VC, BT):
        for c in range(count):
            put(k, c, 2.0 * (f[k, c, pl.ds(base, n, stride=2), :] + f[k, c, pl.ds(base + 1, n, stride=2), :]))


def parity_copy(even, on, off, assemble):
    @pl.when(even)
    def _():
        assemble(off, on)

    @pl.when(jnp.logical_not(even))
    def _():
        assemble(on, off)


def pack_kernel(right_side, guess, vertical, breaking, f_out, to_left, to_right):
    shape = (16, 512)
    row = lax.broadcasted_iota(jnp.int32, shape, 0)
    col = lax.broadcasted_iota(jnp.int32, shape, 1)
    lane = lanes(16)
    lane8 = lanes(8)
    vc = vertical[...]
    bt = break_gain * breaking[...].astype(F32)
    center = 4.0 + 2.0 * vc + bt

    def pack(plane, field):
        near, far = field[:, 0:128], field[:, 128:256]
        to_left[24 * plane : 24 * plane + 16, :] = near
        to_left[24 * plane + 16 : 24 * plane + 24, :] = jnp.where(
            lane8 < 64, far[0:8], pltpu.roll(far[8:16], 64, 1)
        )
        near, far = field[:, 384:512], field[:, 256:384]
        to_right[24 * plane : 24 * plane + 16, :] = near
        to_right[24 * plane + 16 : 24 * plane + 24, :] = jnp.where(
            lane8 >= 64, far[0:8], pltpu.roll(far[8:16], 64, 1)
        )

    first = jnp.zeros((16, 128), F32)
    last = jnp.zeros((16, 128), F32)
    to_left[TOP_AT:Y_ROWS, :] = jnp.zeros((Y_ROWS - TOP_AT, 128), F32)
    to_right[TOP_AT:Y_ROWS, :] = jnp.zeros((Y_ROWS - TOP_AT, 128), F32)
    lane1 = lanes(1)
    for k in range(K):
        v = guess[k]
        hs = jnp.where(row > 0, pltpu.roll(v, 1, 0), 0.0) + jnp.where(row < 15, pltpu.roll(v, 15, 0), 0.0)
        hs = hs + jnp.where(col > 0, pltpu.roll(v, 1, 1), 0.0) + jnp.where(col < 511, pltpu.roll(v, 511, 1), 0.0)
        f = right_side[k] - center * v + hs
        if k == 0:
            f = f + vc * guess[1]
        elif k == K - 1:
            f = f + vc * guess[K - 2]
        else:
            f = f + vc * (guess[k - 1] + guess[k + 1])
        for c in range(4):
            f_out[k, c] = f[:, 128 * c : 128 * c + 128]
        pack(k, f)
        first = jnp.where(lane == k, jnp.broadcast_to(v[:, 0:1], (16, 128)), first)
        last = jnp.where(lane == k, jnp.broadcast_to(v[:, 511:512], (16, 128)), last)
        top, bottom = v[0:1], v[15:16]
        to_left[TOP_AT + k : TOP_AT + k + 1, :] = top[:, 0:128]
        to_left[BOTTOM_AT + k : BOTTOM_AT + k + 1, :] = bottom[:, 0:128]
        to_left[FAR_AT + k : FAR_AT + k + 1, :] = jnp.where(
            lane1 < 64, top[:, 128:256], pltpu.roll(bottom[:, 128:256], 64, 1)
        )
        to_right[TOP_AT + k : TOP_AT + k + 1, :] = top[:, 384:512]
        to_right[BOTTOM_AT + k : BOTTOM_AT + k + 1, :] = bottom[:, 384:512]
        to_right[FAR_AT + k : FAR_AT + k + 1, :] = jnp.where(
            lane1 >= 64, top[:, 256:384], pltpu.roll(bottom[:, 256:384], 64, 1)
        )
    pack(VC, vc)
    pack(BT, bt)
    to_left[COLS_AT : COLS_AT + 16, :] = first
    to_right[COLS_AT : COLS_AT + 16, :] = last


def widen_kernel(f_own, guess, vertical, breaking, from_left, from_right, q):
    lane = lanes(16)
    lane8 = lanes(8)
    lane1 = lanes(1)
    left_cols = from_left[COLS_AT : COLS_AT + 16, :]
    right_cols = from_right[COLS_AT : COLS_AT + 16, :]
    for k in range(PLANES):
        far = from_left[24 * k + 16 : 24 * k + 24, :]
        q[k, 0, 0:8, :] = jnp.where(lane8 >= 64, far, 0.0)
        q[k, 0, 8:16, :] = jnp.where(lane8 >= 64, pltpu.roll(far, 64, 1), 0.0)
        far = from_right[24 * k + 16 : 24 * k + 24, :]
        q[k, 7, 0:8, :] = jnp.where(lane8 < 64, far, 0.0)
        q[k, 7, 8:16, :] = jnp.where(lane8 < 64, pltpu.roll(far, 64, 1), 0.0)
        near_left = from_left[24 * k : 24 * k + 16, :]
        near_right = from_right[24 * k : 24 * k + 16, :]
        if k < K:
            v = guess[k]
            first = jnp.broadcast_to(v[:, 0:1], (16, 128))
            last = jnp.broadcast_to(v[:, 511:512], (16, 128))
            q[k, 1] = near_left + jnp.where(lane == 127, first, 0.0)
            q[k, 6] = near_right + jnp.where(lane == 0, last, 0.0)
            left = jnp.broadcast_to(left_cols[:, k : k + 1], (16, 128))
            right = jnp.broadcast_to(right_cols[:, k : k + 1], (16, 128))
            q[k, 2] = f_own[k, 0] + jnp.where(lane == 0, left, 0.0)
            q[k, 3] = f_own[k, 1]
            q[k, 4] = f_own[k, 2]
            q[k, 5] = f_own[k, 3] + jnp.where(lane == 127, right, 0.0)
        else:
            q[k, 1] = near_left
            q[k, 6] = near_right
            own = vertical[...] if k == VC else break_gain * breaking[...].astype(F32)
            for c in range(4):
                q[k, 2 + c] = own[:, 128 * c : 128 * c + 128]
    for plane, row, near_at in ((PLANES, 0, TOP_AT), (PLANES + 1, 15, BOTTOM_AT)):
        for c in range(8):
            q[plane, c] = jnp.zeros((16, 128), F32)
        for k in range(K):
            at = slice(k, k + 1)
            v = guess[k, row : row + 1, :]
            for c in range(4):
                q[plane, 2 + c, at, :] = v[:, 128 * c : 128 * c + 128]
            q[plane, 1, at, :] = from_left[near_at + k : near_at + k + 1, :]
            q[plane, 6, at, :] = from_right[near_at + k : near_at + k + 1, :]
            far_left = from_left[FAR_AT + k : FAR_AT + k + 1, :]
            far_right = from_right[FAR_AT + k : FAR_AT + k + 1, :]
            if plane == PLANES + 1:
                far_left = pltpu.roll(far_left, 64, 1)
                far_right = pltpu.roll(far_right, 64, 1)
            q[plane, 0, at, :] = jnp.where(lane1 >= 64, far_left, 0.0)
            q[plane, 7, at, :] = jnp.where(lane1 < 64, far_right, 0.0)


def fine_kernel(q, on, off, x0_out, f0_out, x1_out, f1_out, f2_out, f, xa, xb, inv, rs, gs, f1, xc, xd, inv1, rs1, gs1):
    even = lax.axis_index("gx") % 2 == 0

    def assemble(up, down):
        for k in range(PLANES):
            f[k, :, 0:16, :] = up[k]
            f[k, :, 16:32, :] = q[k]
            f[k, :, 32:48, :] = down[k]
        for k in range(K):
            row = slice(k, k + 1)
            f[k, :, 15:16, :] += q[PLANES, :, row, :]
            f[k, :, 16:17, :] += up[PLANES + 1, :, row, :]
            f[k, :, 31:32, :] += down[PLANES, :, row, :]
            f[k, :, 32:33, :] += q[PLANES + 1, :, row, :]

    parity_copy(even, on, off, assemble)
    clear_edges(xa, 48)
    clear_edges(xb, 48)
    scales(f, inv, 1.0)
    first_sweep(xa, f, inv, 48)
    sweep(xa, xb, f, inv, 48, 1.0)
    restrict(xb, f, rs, gs, 48, 1.0, 0, 24)
    for k in range(K):
        x0_out[k] = xb[k + 1, 1:7, 20:44, :]
    for k in range(PLANES):
        f0_out[k] = f[k, 1:7, 12:36, :]
    pairs = exact_dot(gs[...], pair_matrix(256))
    for k in range(PLANES):
        for c in range(4):
            at = (4 * k + c) * 24
            f1[k, c] = pairs[at : at + 24]

    clear_edges(xc, 24)
    clear_edges(xd, 24)
    scales(f1, inv1, 0.25)
    first_sweep(xc, f1, inv1, 24)
    sweep(xc, xd, f1, inv1, 24, 0.25)
    restrict(xd, f1, rs1, gs1, 24, 0.25, 4, 8)
    for k in range(K):
        x1_out[k] = xd[k + 1, :, 12:28, :]
    for k in range(PLANES):
        f1_out[k] = f1[k, :, 4:20, :]
    pairs = exact_dot(gs1[...], pair_matrix(256))
    for k in range(PLANES):
        for c in range(2):
            at = (2 * k + c) * 8
            f2_out[k, c] = pairs[at : at + 8]


def middle_kernel(own, on, off, x2_out, f2, chunk, xa, xb, inv, rs, gs):
    even = lax.axis_index("gx") % 2 == 0

    def assemble(up, down):
        for k in range(PLANES):
            f2[k, :, 0:1, :] = jnp.zeros((2, 1, 128), F32)
            f2[k, :, 1:6, :] = up[k, :, 1:6, :]
            f2[k, :, 6:10, :] = own[k, :, 2:6, :]
            f2[k, :, 10:15, :] = down[k, :, 2:7, :]
            f2[k, :, 15:16, :] = jnp.zeros((2, 1, 128), F32)

    parity_copy(even, on, off, assemble)
    h = 0.25**2
    clear_edges(xa, 16)
    clear_edges(xb, 16)
    scales(f2, inv, h)
    first_sweep(xa, f2, inv, 16, True)
    sweep(xa, xb, f2, inv, 16, h, True)
    restrict(xb, f2, rs, gs, 16, h, 0, 8, True)
    for k in range(K):
        x2_out[k] = xb[k + 1, :, 8:24, :]
    pairs = exact_dot(gs[...], pair_matrix(256))
    rows = [pairs[8 * k + 3 : 8 * k + 5] for k in range(PLANES)]
    rows.append(jnp.zeros((2, 128), F32))
    piece = jnp.concatenate(rows, axis=0)

    def fill(i, carry):
        chunk[i] = piece
        return carry

    lax.fori_loop(0, chunk.shape[0], fill, 0)


def add_copies(x, coarse, es, at_row, n, rows, first, count):
    chunks = coarse.shape[1]
    for k in range(K):
        for c in range(chunks):
            es[(k * chunks + c) * n : (k * chunks + c) * n + n, :] = coarse[k + 1, c, 8 + at_row : 8 + at_row + n, :]
    wide = exact_dot(es[...], copy_matrix(256))
    skip = (2 * n - rows) // 4
    used = rows // 2
    for k in range(K):
        for c in range(chunks):
            base = (k * chunks + c) * n + skip
            for half in range(2):
                fc = 2 * c + half - first
                if 0 <= fc < count:
                    e = wide[base : base + used, 128 * half : 128 * half + 128]
                    for p in range(2):
                        x[k + 1, fc, pl.ds(8 + p, used, stride=2), :] += e


def coarse_kernel(
    same, other, x2_in, f2, x1_in, f1, x0_in, f0, guess, updated, new_defect,
    f3, xa, xb, inv3, rs3, gs3, f4, ya, yb, inv4, es2, xc, xd, inv2, es1, xe, xf, inv1, es0, xg, xh, inv0,
):
    gx = lax.axis_index("gx")
    tiles = 2 * same.shape[0]
    for t in range(TILES):
        tile = gx - SIDE + t
        valid = jnp.logical_and(tile >= 0, tile < tiles)
        chip = jnp.clip(tile, 0, tiles - 1) // 2
        piece = jnp.where(valid, (same if t % 2 else other)[chip], 0.0)
        for k in range(PLANES):
            f3[k, 0, 2 * t : 2 * t + 2, :] = piece[2 * k : 2 * k + 2]
    for k in range(PLANES):
        f3[k, 0, 2 * TILES : 48, :] = jnp.zeros((48 - 2 * TILES, 128), F32)
    h = 0.25**3
    clear_edges(xa, 48)
    clear_edges(xb, 48)
    scales(f3, inv3, h)
    first_sweep(xa, f3, inv3, 48, True)
    sweep(xa, xb, f3, inv3, 48, h, True)
    restrict(xb, f3, rs3, gs3, 48, h, 0, 24, True)
    pairs = exact_dot(gs3[...], pair_matrix(128))
    for k in range(PLANES):
        f4[k, 0] = pairs[24 * k : 24 * k + 24]

    h = 0.25**4
    clear_edges(ya, 24)
    clear_edges(yb, 24)
    scales(f4, inv4, h)
    first_sweep(ya, f4, inv4, 24, True)
    for _ in range(3):
        sweep(ya, yb, f4, inv4, 24, h, True)
        sweep(yb, ya, f4, inv4, 24, h, True)
    sweep(ya, yb, f4, inv4, 24, h, True)

    h = 0.25**3
    for k in range(K):
        wide = exact_dot(yb[k + 1, 0, 8:32, :], copy_matrix(128))
        for p in range(2):
            xb[k + 1, 0, pl.ds(8 + p, 24, stride=2), :] += wide
    sweep(xb, xa, f3, inv3, 48, h, True)
    sweep(xa, xb, f3, inv3, 48, h, True)

    h = 0.25**2
    clear_edges(xc, 16)
    clear_edges(xd, 16)
    scales(f2, inv2, h)
    for k in range(K):
        xc[k + 1, :, 8:24, :] = x2_in[k]
    add_copies(xc, xb, es2, 19, 8, 16, 0, 2)
    sweep(xc, xd, f2, inv2, 16, h, True)
    sweep(xd, xc, f2, inv2, 16, h, True)

    h = 0.25
    clear_edges(xe, 16)
    clear_edges(xf, 16)
    scales(f1, inv1, h)
    for k in range(K):
        xe[k + 1, :, 8:24, :] = x1_in[k]
    add_copies(xe, xc, es1, 4, 8, 16, 0, 4)
    sweep(xe, xf, f1, inv1, 16, h)
    sweep(xf, xe, f1, inv1, 16, h)

    clear_edges(xg, 24)
    clear_edges(xh, 24)
    scales(f0, inv0, 1.0)
    for k in range(K):
        xg[k + 1, :, 8:32, :] = x0_in[k]
    add_copies(xg, xe, es0, 0, 16, 24, 1, 6)
    sweep(xg, xh, f0, inv0, 24, 1.0)
    sweep(xh, xg, f0, inv0, 24, 1.0)

    def finish(k):
        for c, (v, hs, vs) in enumerate(stencil(xg, k, 16, 12)):
            if 1 <= c <= 4:
                vc = f0[VC, c, 4:20, :]
                center = 4.0 + 2.0 * vc + f0[BT, c, 4:20, :]
                cols = slice(128 * (c - 1), 128 * c)
                new_defect[k, :, cols] = f0[k, c, 4:20, :] - center * v + hs + vc * vs
                updated[k, :, cols] = guess[k, :, cols] + v

    each_plane(finish)


def call(kernel, name, outs, scratch, *operands):
    spec = pl.BlockSpec(memory_space=pltpu.VMEM)
    return pl.pallas_call(
        kernel,
        name=name,
        out_shape=[jax.ShapeDtypeStruct(s, F32) for s in outs],
        in_specs=[spec] * len(operands),
        out_specs=[spec] * len(outs),
        scratch_shapes=[pltpu.VMEM(s, F32) for s in scratch],
        compiler_params=pltpu.CompilerParams(vmem_limit_bytes=48 * 1024 * 1024),
    )(*operands)


def field(chunks, rows):
    return (K + 2, chunks, rows + 16, 128)


def shards(right_side, guess, vertical, breaking):
    nx, ny = lax.axis_size("gx"), lax.axis_size("gy")
    chip = [(i, i ^ 1) for i in range(nx)]
    gap = [(i, i + 1) for i in range(1, nx - 1, 2)]
    gap = gap + [(b, a) for a, b in gap]
    rows = [(16, 512)]

    f_own, to_left, to_right = call(
        pack_kernel, "pack", [(K, 4, 16, 128), (Y_ROWS, 128), (Y_ROWS, 128)], [], right_side, guess, vertical, breaking
    )
    from_right = lax.ppermute(to_left, "gy", [(j + 1, j) for j in range(ny - 1)])
    from_left = lax.ppermute(to_right, "gy", [(j, j + 1) for j in range(ny - 1)])
    (q,) = call(widen_kernel, "widen", [(PLANES + 2, 8, 16, 128)], [], f_own, guess, vertical, breaking, from_left, from_right)
    off = lax.ppermute(q, "gx", gap)
    on = lax.ppermute(q, "gx", chip)
    x0, f0, x1, f1, f2_own = call(
        fine_kernel,
        "fine",
        [(K, 6, 24, 128), (PLANES, 6, 24, 128), (K, 4, 16, 128), (PLANES, 4, 16, 128), (PLANES, 2, 8, 128)],
        [
            (PLANES, 8, 48, 128), field(8, 48), field(8, 48), (8, 48, 128), (8, 64, 128), (PLANES * 4 * 24, 256),
            (PLANES, 4, 24, 128), field(4, 24), field(4, 24), (4, 24, 128), (4, 40, 128), (PLANES * 2 * 8, 256),
        ],
        q, on, off,
    )
    off = lax.ppermute(f2_own, "gx", gap)
    on = lax.ppermute(f2_own, "gx", chip)
    x2, f2, chunk = call(
        middle_kernel,
        "middle",
        [(K, 2, 16, 128), (PLANES, 2, 16, 128), (nx // 2, 24, 128)],
        [field(2, 16), field(2, 16), (2, 16, 128), (2, 32, 128), (PLANES * 8, 256)],
        f2_own, on, off,
    )
    same = lax.all_to_all(
        chunk, "gx", 0, 0, axis_index_groups=[list(range(0, nx, 2)), list(range(1, nx, 2))], tiled=True
    )
    other = lax.ppermute(same, "gx", chip)
    return tuple(
        call(
            coarse_kernel,
            "coarse",
            [(K, 16, 512), (K, 16, 512)],
            [
                (PLANES, 1, 48, 128), field(1, 48), field(1, 48), (1, 48, 128), (1, 64, 128), (PLANES * 24, 128),
                (PLANES, 1, 24, 128), field(1, 24), field(1, 24), (1, 24, 128),
                (K * 8, 128), field(2, 16), field(2, 16), (2, 16, 128),
                (K * 2 * 8, 128), field(4, 16), field(4, 16), (4, 16, 128),
                (K * 4 * 16, 128), field(6, 24), field(6, 24), (6, 24, 128),
            ],
            same, other, x2, f2, x1, f1, x0, f0, guess,
        )
    )


def solution(mesh):
    in_specs = (P(None, "gx", "gy"), P(None, "gx", "gy"), P("gx", "gy"), P("gx", "gy"))
    out_specs = (P(None, "gx", "gy"), P(None, "gx", "gy"))
    return jax.shard_map(shards, mesh=mesh, in_specs=in_specs, out_specs=out_specs, check_vma=False)
```

time: 634 us -> 92.8 us (0.15)
  the two profiles are of different devices: /device:TPU:231 before, /device:TPU:25 now
where the time goes in v1:
time: 92.8 us; the launch traced here: 92.3 us
  blocking collectives  27.2 us (29%)
  starting transfers between devices  24.3 us (26%)
  Pallas kernels  19.6 us (21%)
  waiting for transfers between devices  17 us (18%)
  local copies, waits for them, and re-layouts  3.43 us (4%)
    all_to_all x1, blocking collectives, shards(): lax.all_to_all(chunk, 'gx', 0, 0, axis_index_groups=[list(range(0, nx, 2)...  27.2 us
    pallas_call x5, Pallas kernels, call(): pl.pallas_call(kernel, name=name, out_shape=[jax.ShapeDtypeStruct(s, F32)...  19.6 us
    ppermute x1, waiting for transfers between devices, shards(): off = lax.ppermute(q, 'gx', gap)  8.43 us
    ppermute x1, starting transfers between devices, shards(): other = lax.ppermute(same, 'gx', chip)  5.62 us
    ppermute x1, waiting for transfers between devices, shards(): lax.ppermute(to_left, 'gy', [(j + 1, j) for j in range(ny - 1)])  5.01 us
    ppermute x1, starting transfers between devices, shards(): off = lax.ppermute(q, 'gx', gap)  4.87 us
    ppermute x1, starting transfers between devices, shards(): lax.ppermute(to_right, 'gy', [(j, j + 1) for j in range(ny - 1)])  4.42 us
    ppermute x1, starting transfers between devices, shards(): off = lax.ppermute(f2_own, 'gx', gap)  3.64 us
  transfers between devices with their start and end apart: 7, of which 6 were waited for; matrix products, arithmetic and copies ran while one was open for 0% of the time, Pallas kernels for 0%

profile of v1, /device:TPU:25, one launch (start us, length us, event | category | flops | bytes accessed | tf_op | source)
XLA Modules:
  0.0 92.3 jit_solution(6003611052076776083)
XLA Ops:
  0.6 0.0 copy-start
  0.6 1.0 %copy-done = f32[9,16,512]{2,1,0:T(8,128)S(1)} copy-done((f32[9,16,512]{2,1,0:T(8,128)S(1)}, f32[9,16,512]{2,1,0:T(8,128)}, u32[]{:S(2)}) %copy-start) | copy-done | bytes 294936
  1.6 0.0 copy-start.2
  1.6 1.0 %copy-done.2 = f32[9,16,512]{2,1,0:T(8,128)S(1)} copy-done((f32[9,16,512]{2,1,0:T(8,128)S(1)}, f32[9,16,512]{2,1,0:T(8,128)}, u32[]{:S(2)}) %copy-start.2) | copy-done | bytes 294936
  2.6 0.0 copy-start.3
  2.6 0.8 copy-done.3
  3.3 0.0 copy-start.4
  3.3 0.8 copy-done.4
  4.1 0.0 copy-start.1
  4.1 0.7 pack.1
  4.8 4.4 %collective-permute-start = (f32[328,128]{1,0:T(8,128)S(1)}, f32[328,128]{1,0:T(8,128)S(1)}, u32[]{:S(2)}, u32[]{:S(2)}) collective-permute-start(f32[328,128]{1,0:T(8,128)S(1)} %get-tuple-element.14), channel_id=1, source_target_pairs={{0,1},{1,2},{2,3},{3,4},{4,5},{5,6},{6,7},{8,9},{9,10},{10,11},{11... | collective-permute-start | bytes 503816 | tf_op jit(solution)/shard_map/ppermute | solution.py:489
  9.2 1.9 %collective-permute-start.1 = (f32[328,128]{1,0:T(8,128)S(1)}, f32[328,128]{1,0:T(8,128)S(1)}, u32[]{:S(2)}, u32[]{:S(2)}) collective-permute-start(f32[328,128]{1,0:T(8,128)S(1)} %get-tuple-element.15), channel_id=1, source_target_pairs={{1,0},{2,1},{3,2},{4,3},{5,4},{6,5},{7,6},{9,8},{10,9},{11,10},{12... | collective-permute-start | bytes 503816 | tf_op jit(solution)/shard_map/ppermute | solution.py:488
  11.1 1.0 %collective-permute-done.from_left = f32[328,128]{1,0:T(8,128)S(1)} collective-permute-done((f32[328,128]{1,0:T(8,128)S(1)}, f32[328,128]{1,0:T(8,128)S(1)}, u32[]{:S(2)}, u32[]{:S(2)}) %collective-permute-start) | collective-permute-done | bytes 167968 | tf_op jit(solution)/shard_map/ppermute | solution.py:489
  12.2 5.0 %collective-permute-done.1.from_right = f32[328,128]{1,0:T(8,128)S(1)} collective-permute-done((f32[328,128]{1,0:T(8,128)S(1)}, f32[328,128]{1,0:T(8,128)S(1)}, u32[]{:S(2)}, u32[]{:S(2)}) %collective-permute-start.1) | collective-permute-done | bytes 167968 | tf_op jit(solution)/shard_map/ppermute | solution.py:488
  17.2 0.0 copy-done.1
  17.2 0.2 widen.1.q
  17.4 4.9 %collective-permute-start.3 = (f32[13,8,16,128]{3,2,1,0:T(8,128)S(1)}, f32[13,8,16,128]{3,2,1,0:T(8,128)S(1)}, u32[]{:S(2)}, u32[]{:S(2)}) collective-permute-start(f32[13,8,16,128]{3,2,1,0:T(8,128)S(1)} %widen.1.q), channel_id=1, source_target_pairs={{8,16},{24,32},{40,48},{56,64},{72,80},{88,96},{104,112},{120,128}... | collective-permute-start | bytes 2555912 | tf_op jit(solution)/shard_map/ppermute | solution.py:491
  22.3 1.9 %collective-permute-start.2 = (f32[13,8,16,128]{3,2,1,0:T(8,128)S(1)}, f32[13,8,16,128]{3,2,1,0:T(8,128)S(1)}, u32[]{:S(2)}, u32[]{:S(2)}) collective-permute-start(f32[13,8,16,128]{3,2,1,0:T(8,128)S(1)} %widen.1.q), channel_id=1, source_target_pairs={{0,8},{8,0},{16,24},{24,16},{32,40},{40,32},{48,56},{56,48},{64,72... | collective-permute-start | bytes 2555912 | tf_op jit(solution)/shard_map/ppermute | solution.py:492
  24.2 8.4 %collective-permute-done.3.off = f32[13,8,16,128]{3,2,1,0:T(8,128)S(1)} collective-permute-done((f32[13,8,16,128]{3,2,1,0:T(8,128)S(1)}, f32[13,8,16,128]{3,2,1,0:T(8,128)S(1)}, u32[]{:S(2)}, u32[]{:S(2)}) %collective-permute-start.3) | collective-permute-done | bytes 852000 | tf_op jit(solution)/shard_map/ppermute | solution.py:491
  32.6 0.0 collective-permute-done.2.on
  32.6 9.1 %fine.1 = (f32[9,6,24,128]{3,2,1,0:T(8,128)S(1)}, f32[11,6,24,128]{3,2,1,0:T(8,128)S(1)}, f32[9,4,16,128]{3,2,1,0:T(8,128)S(1)}, f32[11,4,16,128]{3,2,1,0:T(8,128)S(1)}, f32[11,2,8,128]{3,2,1,0:T(8,128)S(1)}) custom-call(f32[13,8,16,128]{3,2,1,0:T(8,128)S(1)} %widen.1.q, f32[13,8,16,128]{3,2,1,0:T(8,128)S(1)} %collective-permute-done.2.on, ...), custom_call_target="tpu_custom_call" | custom-call | tf_op jit(solution)/shard_map/fine/pallas_call | solution.py:463
  41.7 3.6 %collective-permute-start.5 = (f32[11,2,8,128]{3,2,1,0:T(8,128)S(1)}, f32[11,2,8,128]{3,2,1,0:T(8,128)S(1)}, u32[]{:S(2)}, u32[]{:S(2)}) collective-permute-start(f32[11,2,8,128]{3,2,1,0:T(8,128)S(1)} %get-tuple-element.16.own), channel_id=1, source_target_pairs={{8,16},{24,32},{40,48},{56,64},{72,80},{88,96},{104,112},{120,128}... | collective-permute-start | bytes 270344 | tf_op jit(solution)/shard_map/ppermute | solution.py:503
  45.4 1.9 %collective-permute-start.4 = (f32[11,2,8,128]{3,2,1,0:T(8,128)S(1)}, f32[11,2,8,128]{3,2,1,0:T(8,128)S(1)}, u32[]{:S(2)}, u32[]{:S(2)}) collective-permute-start(f32[11,2,8,128]{3,2,1,0:T(8,128)S(1)} %get-tuple-element.16.own), channel_id=1, source_target_pairs={{0,8},{8,0},{16,24},{24,16},{32,40},{40,32},{48,56},{56,48},{64,72... | collective-permute-start | bytes 270344 | tf_op jit(solution)/shard_map/ppermute | solution.py:504
  47.3 0.3 collective-permute-done.5.off
  47.6 1.0 %collective-permute-done.4.on = f32[11,2,8,128]{3,2,1,0:T(8,128)S(1)} collective-permute-done((f32[11,2,8,128]{3,2,1,0:T(8,128)S(1)}, f32[11,2,8,128]{3,2,1,0:T(8,128)S(1)}, u32[]{:S(2)}, u32[]{:S(2)}) %collective-permute-start.4) | collective-permute-done | bytes 90144 | tf_op jit(solution)/shard_map/ppermute | solution.py:504
  48.6 0.7 middle.1
  49.3 27.2 %all_to_all.5.same = f32[32,24,128]{2,1,0:T(8,128)S(1)} all-to-all(f32[32,24,128]{2,1,0:T(8,128)S(1)} %get-tuple-element.17), channel_id=1, replica_groups={{0,16,32,48,64,80,96,112,128,144,160,176,192,208,224,240,256,272,288,30..., dimensions={0} | all-to-all | bytes 786432 | tf_op jit(solution)/shard_map/all_to_all | solution.py:512
  76.5 5.6 %collective-permute-start.6 = (f32[32,24,128]{2,1,0:T(8,128)S(1)}, f32[32,24,128]{2,1,0:T(8,128)S(1)}, u32[]{:S(2)}, u32[]{:S(2)}) collective-permute-start(f32[32,24,128]{2,1,0:T(8,128)S(1)} %all_to_all.5.same), channel_id=1, source_target_pairs={{0,8},{8,0},{16,24},{24,16},{32,40},{40,32},{48,56},{56,48},{64,72... | collective-permute-start | bytes 1179656 | tf_op jit(solution)/shard_map/ppermute | solution.py:515
  82.1 1.3 %collective-permute-done.6.other = f32[32,24,128]{2,1,0:T(8,128)S(1)} collective-permute-done((f32[32,24,128]{2,1,0:T(8,128)S(1)}, f32[32,24,128]{2,1,0:T(8,128)S(1)}, u32[]{:S(2)}, u32[]{:S(2)}) %collective-permute-start.6) | collective-permute-done | bytes 393248 | tf_op jit(solution)/shard_map/ppermute | solution.py:515
  83.4 8.9 %coarse.1 = (f32[9,16,512]{2,1,0:T(8,128)}, f32[9,16,512]{2,1,0:T(8,128)}) custom-call(f32[32,24,128]{2,1,0:T(8,128)S(1)} %all_to_all.5.same, f32[32,24,128]{2,1,0:T(8,128)S(1)} %collective-permute-done.6.other, f32[9,2,16,128]{3,2,1,0:T(8,128)S(1)} %get-tuple-element.18.x2_in, f32[11,2,16,128]{3,2,1,0:T(8,128)S(1)} %get-tuple-element.19.f2, ...), custom_call_target="tpu_custom_call" | custom-call | tf_op jit(solution)/shard_map/coarse/pallas_call | solution.py:463
Async XLA Ops:
  0.6 1.0 %copy-start = (f32[9,16,512]{2,1,0:T(8,128)S(1)}, f32[9,16,512]{2,1,0:T(8,128)}, u32[]{:S(2)}) copy-start(f32[9,16,512]{2,1,0:T(8,128)} %guess.5) | copy-start | bytes 884740
  1.6 1.0 %copy-start.2 = (f32[9,16,512]{2,1,0:T(8,128)S(1)}, f32[9,16,512]{2,1,0:T(8,128)}, u32[]{:S(2)}) copy-start(f32[9,16,512]{2,1,0:T(8,128)} %right_side.1) | copy-start | bytes 884740
  2.6 0.8 copy-start.3
  3.3 0.8 copy-start.4
  4.1 13.1 %copy-start.1 = (f32[9,16,512]{2,1,0:T(8,128)S(1)}, f32[9,16,512]{2,1,0:T(8,128)}, u32[]{:S(2)}) copy-start(f32[9,16,512]{2,1,0:T(8,128)} %guess.5) | copy-start | bytes 884740
  4.8 7.4 %collective-permute-start = (f32[328,128]{1,0:T(8,128)S(1)}, f32[328,128]{1,0:T(8,128)S(1)}, u32[]{:S(2)}, u32[]{:S(2)}) collective-permute-start(f32[328,128]{1,0:T(8,128)S(1)} %get-tuple-element.14), channel_id=1, source_target_pairs={{0,1},{1,2},{2,3},{3,4},{4,5},{5,6},{6,7},{8,9},{9,10},{10,11},{11... | collective-permute-start | bytes 503816 | tf_op jit(solution)/shard_map/ppermute | solution.py:489
  9.2 7.9 %collective-permute-start.1 = (f32[328,128]{1,0:T(8,128)S(1)}, f32[328,128]{1,0:T(8,128)S(1)}, u32[]{:S(2)}, u32[]{:S(2)}) collective-permute-start(f32[328,128]{1,0:T(8,128)S(1)} %get-tuple-element.15), channel_id=1, source_target_pairs={{1,0},{2,1},{3,2},{4,3},{5,4},{6,5},{7,6},{9,8},{10,9},{11,10},{12... | collective-permute-start | bytes 503816 | tf_op jit(solution)/shard_map/ppermute | solution.py:488
  17.4 15.2 %collective-permute-start.3 = (f32[13,8,16,128]{3,2,1,0:T(8,128)S(1)}, f32[13,8,16,128]{3,2,1,0:T(8,128)S(1)}, u32[]{:S(2)}, u32[]{:S(2)}) collective-permute-start(f32[13,8,16,128]{3,2,1,0:T(8,128)S(1)} %widen.1.q), channel_id=1, source_target_pairs={{8,16},{24,32},{40,48},{56,64},{72,80},{88,96},{104,112},{120,128}... | collective-permute-start | bytes 2555912 | tf_op jit(solution)/shard_map/ppermute | solution.py:491
  22.3 10.4 %collective-permute-start.2 = (f32[13,8,16,128]{3,2,1,0:T(8,128)S(1)}, f32[13,8,16,128]{3,2,1,0:T(8,128)S(1)}, u32[]{:S(2)}, u32[]{:S(2)}) collective-permute-start(f32[13,8,16,128]{3,2,1,0:T(8,128)S(1)} %widen.1.q), channel_id=1, source_target_pairs={{0,8},{8,0},{16,24},{24,16},{32,40},{40,32},{48,56},{56,48},{64,72... | collective-permute-start | bytes 2555912 | tf_op jit(solution)/shard_map/ppermute | solution.py:492
  41.7 5.8 %collective-permute-start.5 = (f32[11,2,8,128]{3,2,1,0:T(8,128)S(1)}, f32[11,2,8,128]{3,2,1,0:T(8,128)S(1)}, u32[]{:S(2)}, u32[]{:S(2)}) collective-permute-start(f32[11,2,8,128]{3,2,1,0:T(8,128)S(1)} %get-tuple-element.16.own), channel_id=1, source_target_pairs={{8,16},{24,32},{40,48},{56,64},{72,80},{88,96},{104,112},{120,128}... | collective-permute-start | bytes 270344 | tf_op jit(solution)/shard_map/ppermute | solution.py:503
  45.4 3.2 %collective-permute-start.4 = (f32[11,2,8,128]{3,2,1,0:T(8,128)S(1)}, f32[11,2,8,128]{3,2,1,0:T(8,128)S(1)}, u32[]{:S(2)}, u32[]{:S(2)}) collective-permute-start(f32[11,2,8,128]{3,2,1,0:T(8,128)S(1)} %get-tuple-element.16.own), channel_id=1, source_target_pairs={{0,8},{8,0},{16,24},{24,16},{32,40},{40,32},{48,56},{56,48},{64,72... | collective-permute-start | bytes 270344 | tf_op jit(solution)/shard_map/ppermute | solution.py:504
  76.5 7.0 %collective-permute-start.6 = (f32[32,24,128]{2,1,0:T(8,128)S(1)}, f32[32,24,128]{2,1,0:T(8,128)S(1)}, u32[]{:S(2)}, u32[]{:S(2)}) collective-permute-start(f32[32,24,128]{2,1,0:T(8,128)S(1)} %all_to_all.5.same), channel_id=1, source_target_pairs={{0,8},{8,0},{16,24},{24,16},{32,40},{40,32},{48,56},{56,48},{64,72... | collective-permute-start | bytes 1179656 | tf_op jit(solution)/shard_map/ppermute | solution.py:515

commit v2 on v1

v2 whole, which is shorter than its diff:
```python
import jax
import jax.numpy as jnp
from jax import lax
from jax.experimental import pallas as pl
from jax.experimental.pallas import tpu as pltpu
from jax.sharding import PartitionSpec as P

K = 9
PLANES = K + 2
VC, BT = K, K + 1
TILES = 23
SIDE = TILES // 2
damping = 0.8
keep = 0.2
break_gain = 0.05
F32 = jnp.float32
BF16 = jnp.bfloat16

COLS_AT = 24 * PLANES
TOP_AT = COLS_AT + 16
BOTTOM_AT = TOP_AT + 16
FAR_AT = BOTTOM_AT + 16
Y_ROWS = FAR_AT + 16

SHORT_AT = 8 * PLANES
GUESS_AT = SHORT_AT + 5 * PLANES
X_ROWS = GUESS_AT + K


def lanes(rows):
    return lax.broadcasted_iota(jnp.int32, (rows, 128), 1)


def shifted(chunks):
    lane = lanes(chunks[0].shape[0])
    right = [pltpu.roll(v, 1, 1) for v in chunks]
    left = [pltpu.roll(v, 127, 1) for v in chunks]
    n = len(chunks)
    before = [jnp.where(lane == 0, right[c - 1], right[c]) if c else right[c] for c in range(n)]
    after = [jnp.where(lane == 127, left[c + 1], left[c]) if c < n - 1 else left[c] for c in range(n)]
    return before, after


def stencil(x, k, rows, at):
    count = x.shape[1]
    here = pl.ds(at, rows)
    v = [x[k + 1, c, here, :] for c in range(count)]
    before, after = shifted(v)
    out = []
    for c in range(count):
        hs = (x[k + 1, c, pl.ds(at - 1, rows), :] + x[k + 1, c, pl.ds(at + 1, rows), :]) + (before[c] + after[c])
        vs = x[k, c, here, :] + x[k + 2, c, here, :]
        out.append((v[c], hs, vs))
    return out


def clear_edges(x, rows):
    count, total = x.shape[1], x.shape[2]
    for k in (0, K + 1):
        x[k] = jnp.zeros((count, total, 128), F32)
    for k in range(1, K + 1):
        x[k, :, 0:8, :] = jnp.zeros((count, 8, 128), F32)
        x[k, :, 8 + rows : total, :] = jnp.zeros((count, total - 8 - rows, 128), F32)


def scales(f, inv, ratio, h):
    for c in range(f.shape[1]):
        vc = f[VC, c]
        center = 4.0 * h + 2.0 * vc + f[BT, c]
        inv[c] = jnp.where(vc > 0.0, damping / center, 0.0)
        if ratio is not None:
            ratio[c] = center * (1.0 / damping)


def first_sweep(x, f, inv, rows):
    for k in range(K):
        for c in range(f.shape[1]):
            x[k + 1, c, pl.ds(8, rows), :] = inv[c] * f[k, c]


def times(h, value):
    return value if h == 1.0 else h * value


def second_sweep(x, y, f, inv, rows, h):
    for k in range(K):
        for c, (v, hs, vs) in enumerate(stencil(x, k, rows, 8)):
            y[k + 1, c, pl.ds(8, rows), :] = (1.0 + keep) * v + inv[c] * (times(h, hs) + f[VC, c] * vs)


def sweep(x, y, f, inv, rows, h):
    for k in range(K):
        for c, (v, hs, vs) in enumerate(stencil(x, k, rows, 8)):
            y[k + 1, c, pl.ds(8, rows), :] = keep * v + inv[c] * (f[k, c] + times(h, hs) + f[VC, c] * vs)


def pair_matrix(inputs):
    i = lax.broadcasted_iota(jnp.int32, (inputs, 128), 0)
    j = lax.broadcasted_iota(jnp.int32, (inputs, 128), 1)
    return jnp.where((i == 2 * j) | (i == 2 * j + 1), 0.25, 0.0).astype(BF16)


def fold_matrix(inputs):
    i = lax.broadcasted_iota(jnp.int32, (inputs, 128), 0)
    d = i - 2 * lax.broadcasted_iota(jnp.int32, (inputs, 128), 1)
    inner = jnp.where((d == 0) | (d == 1), 0.375, 0.0)
    return jnp.where((d == -1) | (d == 2), 0.125, inner).astype(BF16)


def copy_matrix(outputs):
    i = lax.broadcasted_iota(jnp.int32, (128, outputs), 0)
    j = lax.broadcasted_iota(jnp.int32, (128, outputs), 1)
    return jnp.where((j == 2 * i) | (j == 2 * i + 1), 1.0, 0.0).astype(BF16)


def exact_dot(values, matrix, parts=3):
    total = None
    for _ in range(parts):
        part = values.astype(BF16)
        values = values - part.astype(F32)
        product = jnp.dot(part, matrix, preferred_element_type=F32)
        total = product if total is None else total + product
    return total


def restrict(x, f, inv, ratio, rs, gs, coarse, rows, h, base, n):
    count = f.shape[1]
    pairs = max(count // 2, 1)
    width = gs.shape[-1]
    lane = lanes(n)
    rs[:, 0:8, :] = jnp.zeros((count, 8, 128), F32)
    rs[:, 8 + rows : 16 + rows, :] = jnp.zeros((count, 8, 128), F32)

    def part(slot, c):
        return gs[slot, (c // 2) * n : (c // 2) * n + n, 128 * (c % 2) : 128 * (c % 2) + 128]

    def put(slot, c, value):
        gs[slot, (c // 2) * n : (c // 2) * n + n, 128 * (c % 2) : 128 * (c % 2) + 128] = value

    def residual(k, slot):
        for c, (v, hs, vs) in enumerate(stencil(x, k, rows, 8)):
            around = inv[c] * (f[k, c] + times(h, hs) + f[VC, c] * vs)
            rs[c, 8 : 8 + rows, :] = ratio[c] * (around - damping * v)
        for c in range(count):

            def pick(start):
                return rs[c, pl.ds(8 + base + start, n, stride=2), :]

            put(slot, c, (pick(-1) + 3.0 * (pick(0) + pick(1)) + pick(2)) * 0.125)

    def emit(k, slot, values):
        for j in range(pairs):
            value = values[j * n : j * n + n]
            if j > 0:
                value = value + jnp.where(lane == 0, 0.125 * pltpu.roll(part(slot, 2 * j - 1), 1, 1), 0.0)
            if j < pairs - 1:
                value = value + jnp.where(lane == 127, 0.125 * pltpu.roll(part(slot, 2 * j + 2), 127, 1), 0.0)
            coarse[k, j] = value

    matrix = fold_matrix(width)
    for k in range(K):
        residual(k, k)
    size = pairs * n
    values = exact_dot(gs[...].reshape(K * size, width), matrix, 2)
    for k in range(K):
        emit(k, k, values[k * size : k * size + size])
    for slot, k in enumerate((VC, BT)):
        for c in range(count):
            put(slot, c, f[k, c, pl.ds(base, n, stride=2), :] + f[k, c, pl.ds(base + 1, n, stride=2), :])
    values = exact_dot(gs[0:2].reshape(2 * pairs * n, width), pair_matrix(width))
    for slot, k in enumerate((VC, BT)):
        for j in range(pairs):
            at = (slot * pairs + j) * n
            coarse[k, j] = values[at : at + n]


def parity_copy(even, on, off, assemble):
    @pl.when(even)
    def _():
        assemble(off, on)

    @pl.when(jnp.logical_not(even))
    def _():
        assemble(on, off)


def own_defect(right_side, guess, vc, bt, k, left, right):
    v = guess[k]
    row = lax.broadcasted_iota(jnp.int32, v.shape, 0)
    col = lax.broadcasted_iota(jnp.int32, v.shape, 1)
    hs = jnp.where(row > 0, pltpu.roll(v, 1, 0), 0.0) + jnp.where(row < 15, pltpu.roll(v, 15, 0), 0.0)
    hs = hs + jnp.where(col > 0, pltpu.roll(v, 1, 1), left) + jnp.where(col < 511, pltpu.roll(v, 511, 1), right)
    vs = guess[1] if k == 0 else guess[K - 2] if k == K - 1 else guess[k - 1] + guess[k + 1]
    return right_side[k] - (4.0 + 2.0 * vc + bt) * v + hs + vc * vs


def pack_kernel(rs_in, g_in, vc_in, br_in, to_left, to_right, right_side, guess, vertical, breaking, sems):
    pairs = ((vc_in, vertical), (br_in, breaking), (g_in, guess), (rs_in, right_side))
    copies = [pltpu.make_async_copy(a, b, sems.at[i]) for i, (a, b) in enumerate(pairs)]
    for copy in copies:
        copy.start()
    for copy in copies:
        copy.wait()
    lane = lanes(16)
    lane8 = lanes(8)
    vc = vertical[...]
    bt = break_gain * breaking[...].astype(F32)

    def pack(plane, field):
        near, far = field[:, 0:128], field[:, 128:256]
        to_left[24 * plane : 24 * plane + 16, :] = near
        to_left[24 * plane + 16 : 24 * plane + 24, :] = jnp.where(
            lane8 < 64, far[0:8], pltpu.roll(far[8:16], 64, 1)
        )
        near, far = field[:, 384:512], field[:, 256:384]
        to_right[24 * plane : 24 * plane + 16, :] = near
        to_right[24 * plane + 16 : 24 * plane + 24, :] = jnp.where(
            lane8 >= 64, far[0:8], pltpu.roll(far[8:16], 64, 1)
        )

    first = jnp.zeros((16, 128), F32)
    last = jnp.zeros((16, 128), F32)
    to_left[TOP_AT:Y_ROWS, :] = jnp.zeros((Y_ROWS - TOP_AT, 128), F32)
    to_right[TOP_AT:Y_ROWS, :] = jnp.zeros((Y_ROWS - TOP_AT, 128), F32)
    lane1 = lanes(1)
    for k in range(K):
        v = guess[k]
        f = own_defect(right_side, guess, vc, bt, k, 0.0, 0.0)
        pack(k, f)
        first = jnp.where(lane == k, jnp.broadcast_to(v[:, 0:1], (16, 128)), first)
        last = jnp.where(lane == k, jnp.broadcast_to(v[:, 511:512], (16, 128)), last)
        top, bottom = v[0:1], v[15:16]
        to_left[TOP_AT + k : TOP_AT + k + 1, :] = top[:, 0:128]
        to_left[BOTTOM_AT + k : BOTTOM_AT + k + 1, :] = bottom[:, 0:128]
        to_left[FAR_AT + k : FAR_AT + k + 1, :] = jnp.where(
            lane1 < 64, top[:, 128:256], pltpu.roll(bottom[:, 128:256], 64, 1)
        )
        to_right[TOP_AT + k : TOP_AT + k + 1, :] = top[:, 384:512]
        to_right[BOTTOM_AT + k : BOTTOM_AT + k + 1, :] = bottom[:, 384:512]
        to_right[FAR_AT + k : FAR_AT + k + 1, :] = jnp.where(
            lane1 >= 64, top[:, 256:384], pltpu.roll(bottom[:, 256:384], 64, 1)
        )
    pack(VC, vc)
    pack(BT, bt)
    to_left[COLS_AT : COLS_AT + 16, :] = first
    to_right[COLS_AT : COLS_AT + 16, :] = last


def widen_kernel(right_side, guess, vertical, breaking, from_left, from_right, q, to_on, to_off):
    lane = lanes(16)
    lane8 = lanes(8)
    lane1 = lanes(1)
    left_cols = from_left[COLS_AT : COLS_AT + 16, :]
    right_cols = from_right[COLS_AT : COLS_AT + 16, :]
    vc = vertical[...]
    bt = break_gain * breaking[...].astype(F32)
    for k in range(PLANES):
        far = from_left[24 * k + 16 : 24 * k + 24, :]
        q[k, 0, 0:8, :] = jnp.where(lane8 >= 64, far, 0.0)
        q[k, 0, 8:16, :] = jnp.where(lane8 >= 64, pltpu.roll(far, 64, 1), 0.0)
        far = from_right[24 * k + 16 : 24 * k + 24, :]
        q[k, 7, 0:8, :] = jnp.where(lane8 < 64, far, 0.0)
        q[k, 7, 8:16, :] = jnp.where(lane8 < 64, pltpu.roll(far, 64, 1), 0.0)
        near_left = from_left[24 * k : 24 * k + 16, :]
        near_right = from_right[24 * k : 24 * k + 16, :]
        if k < K:
            v = guess[k]
            first = jnp.broadcast_to(v[:, 0:1], (16, 128))
            last = jnp.broadcast_to(v[:, 511:512], (16, 128))
            q[k, 1] = near_left + jnp.where(lane == 127, first, 0.0)
            q[k, 6] = near_right + jnp.where(lane == 0, last, 0.0)
            own = own_defect(right_side, guess, vc, bt, k, left_cols[:, k : k + 1], right_cols[:, k : k + 1])
        else:
            q[k, 1] = near_left
            q[k, 6] = near_right
            own = vc if k == VC else bt
        for c in range(4):
            q[k, 2 + c] = own[:, 128 * c : 128 * c + 128]
    for plane, row, near_at in ((PLANES, 0, TOP_AT), (PLANES + 1, 15, BOTTOM_AT)):
        for c in range(8):
            q[plane, c] = jnp.zeros((16, 128), F32)
        for k in range(K):
            at = slice(k, k + 1)
            v = guess[k, row : row + 1, :]
            for c in range(4):
                q[plane, 2 + c, at, :] = v[:, 128 * c : 128 * c + 128]
            q[plane, 1, at, :] = from_left[near_at + k : near_at + k + 1, :]
            q[plane, 6, at, :] = from_right[near_at + k : near_at + k + 1, :]
            far_left = from_left[FAR_AT + k : FAR_AT + k + 1, :]
            far_right = from_right[FAR_AT + k : FAR_AT + k + 1, :]
            if plane == PLANES + 1:
                far_left = pltpu.roll(far_left, 64, 1)
                far_right = pltpu.roll(far_right, 64, 1)
            q[plane, 0, at, :] = jnp.where(lane1 >= 64, far_left, 0.0)
            q[plane, 7, at, :] = jnp.where(lane1 < 64, far_right, 0.0)


    def fill(buffer, long, short, plane):
        for c in range(7):
            for k in range(PLANES):
                piece = jnp.where(lane < 64, q[k, 7], q[k, 0]) if c == 0 else q[k, c]
                buffer[c, 8 * k : 8 * k + 8, :] = piece[long : long + 8]
                buffer[c, SHORT_AT + 5 * k : SHORT_AT + 5 * k + 5, :] = piece[short : short + 5]
            piece = jnp.where(lane < 64, q[plane, 7], q[plane, 0]) if c == 0 else q[plane, c]
            buffer[c, GUESS_AT : GUESS_AT + K, :] = piece[0:K]

    def fill_both(to_up, to_down):
        fill(to_up, 0, 8, PLANES)
        fill(to_down, 8, 3, PLANES + 1)

    parity_copy(lax.axis_index("gx") % 2 == 0, to_on, to_off, fill_both)


def fine_kernel(q, off, on, x0_out, f0_out, x1_out, f1_out, f2_out, f, xa, xb, inv, ratio, rs, gs, f1, xc, xd, inv1, ratio1, rs1, gs1):
    even = lax.axis_index("gx") % 2 == 0

    def assemble(up, down):
        lane = lanes(8)

        def piece(buffer, c, at, n):
            value = buffer[min(c % 7, c), at : at + n, :]
            if c == 0:
                return jnp.where(lane[0:n] >= 64, value, 0.0)
            return jnp.where(lane[0:n] < 64, value, 0.0) if c == 7 else value

        for c in range(8):
            for k in range(PLANES):
                short = SHORT_AT + 5 * k
                f[k, c, 0:3, :] = jnp.zeros((3, 128), F32)
                f[k, c, 3:8, :] = piece(up, c, short, 5)
                f[k, c, 8:16, :] = piece(up, c, 8 * k, 8)
                f[k, c, 16:32, :] = q[k, c]
                f[k, c, 32:40, :] = piece(down, c, 8 * k, 8)
                f[k, c, 40:45, :] = piece(down, c, short, 5)
                f[k, c, 45:48, :] = jnp.zeros((3, 128), F32)
            for k in range(K):
                row = slice(k, k + 1)
                f[k, c, 15:16, :] += q[PLANES, c, row, :]
                f[k, c, 16:17, :] += piece(up, c, GUESS_AT + k, 1)
                f[k, c, 31:32, :] += piece(down, c, GUESS_AT + k, 1)
                f[k, c, 32:33, :] += q[PLANES + 1, c, row, :]

    parity_copy(even, on, off, assemble)
    clear_edges(xa, 48)
    clear_edges(xb, 48)
    scales(f, inv, ratio, 1.0)
    first_sweep(xa, f, inv, 48)
    second_sweep(xa, xb, f, inv, 48, 1.0)
    restrict(xb, f, inv, ratio, rs, gs, f1, 48, 1.0, 0, 24)
    for k in range(K):
        x0_out[k] = xb[k + 1, 1:7, 20:44, :]
    for k in range(PLANES):
        f0_out[k] = f[k, 1:7, 12:36, :]

    clear_edges(xc, 24)
    clear_edges(xd, 24)
    scales(f1, inv1, ratio1, 0.25)
    first_sweep(xc, f1, inv1, 24)
    second_sweep(xc, xd, f1, inv1, 24, 0.25)
    restrict(xd, f1, inv1, ratio1, rs1, gs1, f2_out, 24, 0.25, 4, 8)
    for k in range(K):
        x1_out[k] = xd[k + 1, :, 12:28, :]
    for k in range(PLANES):
        f1_out[k] = f1[k, :, 4:20, :]


def middle_kernel(own, on, off, x2_out, f2, chunk, xa, xb, inv, ratio, rs, gs, f3):
    even = lax.axis_index("gx") % 2 == 0

    def assemble(up, down):
        for k in range(PLANES):
            f2[k, :, 0:1, :] = jnp.zeros((2, 1, 128), F32)
            f2[k, :, 1:6, :] = up[k, :, 1:6, :]
            f2[k, :, 6:10, :] = own[k, :, 2:6, :]
            f2[k, :, 10:15, :] = down[k, :, 2:7, :]
            f2[k, :, 15:16, :] = jnp.zeros((2, 1, 128), F32)

    parity_copy(even, on, off, assemble)
    h = 0.25**2
    clear_edges(xa, 16)
    clear_edges(xb, 16)
    scales(f2, inv, ratio, h)
    first_sweep(xa, f2, inv, 16)
    second_sweep(xa, xb, f2, inv, 16, h)
    restrict(xb, f2, inv, ratio, rs, gs, f3, 16, h, 0, 8)
    for k in range(K):
        x2_out[k] = xb[k + 1, :, 8:24, :]
    rows = [f3[k, 0, 3:5, :] for k in range(PLANES)]
    rows.append(jnp.zeros((2, 128), F32))
    piece = jnp.concatenate(rows, axis=0)

    def fill(i, carry):
        chunk[i] = piece
        return carry

    lax.fori_loop(0, chunk.shape[0], fill, 0)


def add_copies(x, coarse, es, at_row, n, rows, first, count):
    chunks = coarse.shape[1]
    for k in range(K):
        for c in range(chunks):
            es[(k * chunks + c) * n : (k * chunks + c) * n + n, :] = coarse[k + 1, c, 8 + at_row : 8 + at_row + n, :]
    wide = exact_dot(es[...], copy_matrix(256))
    skip = (2 * n - rows) // 4
    used = rows // 2
    for k in range(K):
        for c in range(chunks):
            base = (k * chunks + c) * n + skip
            for half in range(2):
                fc = 2 * c + half - first
                if 0 <= fc < count:
                    e = wide[base : base + used, 128 * half : 128 * half + 128]
                    for p in range(2):
                        x[k + 1, fc, pl.ds(8 + p, used, stride=2), :] += e


def coarse_kernel(
    same, other, x2_in, f2, x1_in, f1, x0_in, f0, guess, updated, new_defect,
    f3, xa, xb, inv3, ratio3, rs3, gs3, f4, ya, yb, inv4, es3, es2, xc, xd, inv2, es1, xe, xf, inv1, es0, xg, xh, inv0,
):
    gx = lax.axis_index("gx")
    tiles = 2 * same.shape[0]
    for t in range(TILES):
        tile = gx - SIDE + t
        valid = jnp.logical_and(tile >= 0, tile < tiles)
        chip = jnp.clip(tile, 0, tiles - 1) // 2
        piece = jnp.where(valid, (same if t % 2 else other)[chip], 0.0)
        for k in range(PLANES):
            f3[k, 0, 2 * t : 2 * t + 2, :] = piece[2 * k : 2 * k + 2]
    for k in range(PLANES):
        f3[k, 0, 2 * TILES : 48, :] = jnp.zeros((48 - 2 * TILES, 128), F32)
    h = 0.25**3
    clear_edges(xa, 48)
    clear_edges(xb, 48)
    scales(f3, inv3, ratio3, h)
    first_sweep(xa, f3, inv3, 48)
    second_sweep(xa, xb, f3, inv3, 48, h)
    restrict(xb, f3, inv3, ratio3, rs3, gs3, f4, 48, h, 0, 24)

    h = 0.25**4
    clear_edges(ya, 24)
    clear_edges(yb, 24)
    scales(f4, inv4, None, h)
    first_sweep(ya, f4, inv4, 24)
    second_sweep(ya, yb, f4, inv4, 24, h)
    for _ in range(3):
        sweep(yb, ya, f4, inv4, 24, h)
        sweep(ya, yb, f4, inv4, 24, h)

    h = 0.25**3
    for k in range(K):
        es3[24 * k : 24 * k + 24, :] = yb[k + 1, 0, 8:32, :]
    wide = exact_dot(es3[...], copy_matrix(128))
    for k in range(K):
        for p in range(2):
            xb[k + 1, 0, pl.ds(8 + p, 24, stride=2), :] += wide[24 * k : 24 * k + 24]
    sweep(xb, xa, f3, inv3, 48, h)
    sweep(xa, xb, f3, inv3, 48, h)

    h = 0.25**2
    clear_edges(xc, 16)
    clear_edges(xd, 16)
    scales(f2, inv2, None, h)
    for k in range(K):
        xc[k + 1, :, 8:24, :] = x2_in[k]
    add_copies(xc, xb, es2, 19, 8, 16, 0, 2)
    sweep(xc, xd, f2, inv2, 16, h)
    sweep(xd, xc, f2, inv2, 16, h)

    h = 0.25
    clear_edges(xe, 16)
    clear_edges(xf, 16)
    scales(f1, inv1, None, h)
    for k in range(K):
        xe[k + 1, :, 8:24, :] = x1_in[k]
    add_copies(xe, xc, es1, 4, 8, 16, 0, 4)
    sweep(xe, xf, f1, inv1, 16, h)
    sweep(xf, xe, f1, inv1, 16, h)

    clear_edges(xg, 24)
    clear_edges(xh, 24)
    scales(f0, inv0, None, 1.0)
    for k in range(K):
        xg[k + 1, :, 8:32, :] = x0_in[k]
    add_copies(xg, xe, es0, 0, 16, 24, 1, 6)
    sweep(xg, xh, f0, inv0, 24, 1.0)
    sweep(xh, xg, f0, inv0, 24, 1.0)

    for k in range(K):
        for c, (v, hs, vs) in enumerate(stencil(xg, k, 16, 12)):
            if 1 <= c <= 4:
                vc = f0[VC, c, 4:20, :]
                center = 4.0 + 2.0 * vc + f0[BT, c, 4:20, :]
                cols = slice(128 * (c - 1), 128 * c)
                new_defect[k, :, cols] = f0[k, c, 4:20, :] - center * v + hs + vc * vs
                updated[k, :, cols] = guess[k, :, cols] + v


def call(kernel, name, outs, scratch, *operands, space=pltpu.VMEM, mib=48):
    spec = pl.BlockSpec(memory_space=pltpu.VMEM)
    return pl.pallas_call(
        kernel,
        name=name,
        out_shape=[jax.ShapeDtypeStruct(s, F32) for s in outs],
        in_specs=[pl.BlockSpec(memory_space=space)] * len(operands),
        out_specs=[spec] * len(outs),
        scratch_shapes=[pltpu.VMEM(s, F32) if isinstance(s, tuple) else s for s in scratch],
        compiler_params=pltpu.CompilerParams(vmem_limit_bytes=mib * 1024 * 1024),
    )(*operands)


def field(chunks, rows):
    return (K + 2, chunks, rows + 16, 128)


def shards(right_side, guess, vertical, breaking):
    nx, ny = lax.axis_size("gx"), lax.axis_size("gy")
    chip = [(i, i ^ 1) for i in range(nx)]
    gap = [(i, i + 1) for i in range(1, nx - 1, 2)]
    gap = gap + [(b, a) for a, b in gap]

    to_left, to_right = call(
        pack_kernel,
        "pack",
        [(Y_ROWS, 128), (Y_ROWS, 128)],
        [(K, 16, 512), (K, 16, 512), (16, 512), pltpu.VMEM((16, 512), jnp.int32), pltpu.SemaphoreType.DMA((4,))],
        right_side, guess, vertical, breaking,
        space=pltpu.HBM,
        mib=62,
    )
    from_right = lax.ppermute(to_left, "gy", [(j + 1, j) for j in range(ny - 1)])
    from_left = lax.ppermute(to_right, "gy", [(j, j + 1) for j in range(ny - 1)])
    q, to_on, to_off = call(
        widen_kernel,
        "widen",
        [(PLANES + 2, 8, 16, 128), (7, X_ROWS, 128), (7, X_ROWS, 128)],
        [],
        right_side, guess, vertical, breaking, from_left, from_right,
    )
    off = lax.ppermute(to_off, "gx", gap)
    on = lax.ppermute(to_on, "gx", chip)
    x0, f0, x1, f1, f2_own = call(
        fine_kernel,
        "fine",
        [(K, 6, 24, 128), (PLANES, 6, 24, 128), (K, 4, 16, 128), (PLANES, 4, 16, 128), (PLANES, 2, 8, 128)],
        [
            (PLANES, 8, 48, 128), field(8, 48), field(8, 48), (8, 48, 128), (8, 48, 128), (8, 64, 128), (K, 4 * 24, 256),
            (PLANES, 4, 24, 128), field(4, 24), field(4, 24), (4, 24, 128), (4, 24, 128), (4, 40, 128), (K, 2 * 8, 256),
        ],
        q, off, on,
    )
    off = lax.ppermute(f2_own, "gx", gap)
    on = lax.ppermute(f2_own, "gx", chip)
    x2, f2, chunk = call(
        middle_kernel,
        "middle",
        [(K, 2, 16, 128), (PLANES, 2, 16, 128), (nx // 2, 24, 128)],
        [field(2, 16), field(2, 16), (2, 16, 128), (2, 16, 128), (2, 32, 128), (K, 8, 256), (PLANES, 1, 8, 128)],
        f2_own, on, off,
    )
    same = lax.all_to_all(
        chunk, "gx", 0, 0, axis_index_groups=[list(range(0, nx, 2)), list(range(1, nx, 2))], tiled=True
    )
    other = lax.ppermute(same, "gx", chip)
    return tuple(
        call(
            coarse_kernel,
            "coarse",
            [(K, 16, 512), (K, 16, 512)],
            [
                (PLANES, 1, 48, 128), field(1, 48), field(1, 48), (1, 48, 128), (1, 48, 128), (1, 64, 128), (K, 24, 128),
                (PLANES, 1, 24, 128), field(1, 24), field(1, 24), (1, 24, 128), (K * 24, 128),
                (K * 8, 128), field(2, 16), field(2, 16), (2, 16, 128),
                (K * 2 * 8, 128), field(4, 16), field(4, 16), (4, 16, 128),
                (K * 4 * 16, 128), field(6, 24), field(6, 24), (6, 24, 128),
            ],
            same, other, x2, f2, x1, f1, x0, f0, guess,
        )
    )


def solution(mesh):
    in_specs = (P(None, "gx", "gy"), P(None, "gx", "gy"), P("gx", "gy"), P("gx", "gy"))
    out_specs = (P(None, "gx", "gy"), P(None, "gx", "gy"))
    return jax.shard_map(shards, mesh=mesh, in_specs=in_specs, out_specs=out_specs, check_vma=False)
```

time: 92.8 us -> 79.7 us (0.86)
  Pallas kernels: 19.6 us -> 13.1 us
  local copies, waits for them, and re-layouts: 3.43 us -> 0.02 us
  waiting for transfers between devices: 17 us -> 13.9 us
    pallas_call x5, Pallas kernels: 19.6 us -> 13.1 us  [call(): pl.pallas_call(kernel, name=name, out_shape=[jax.ShapeDtypeStruct(s, F32)...]
    unnamed x10 -> x8, local copies, waits for them, and re-layouts: 3.43 us -> 0.02 us
    ppermute x2, waiting for transfers between devices: 8.44 us -> 5.14 us  [the longest x1 5.14 us: shards(): off = lax.ppermute(to_off, 'gx', gap)]
where the time goes in v2:
time: 79.7 us; the launch traced here: 79.4 us
  blocking collectives  27.2 us (34%)
  starting transfers between devices  24.3 us (30%)
  waiting for transfers between devices  13.9 us (17%)
  Pallas kernels  13.1 us (16%)
    all_to_all x1, blocking collectives, shards(): lax.all_to_all(chunk, 'gx', 0, 0, axis_index_groups=[list(range(0, nx, 2)...  27.2 us
    pallas_call x5, Pallas kernels, call(): pl.pallas_call(kernel, name=name, out_shape=[jax.ShapeDtypeStruct(s, F32)...  13.1 us
    ppermute x1, starting transfers between devices, shards(): other = lax.ppermute(same, 'gx', chip)  5.62 us
    ppermute x1, waiting for transfers between devices, shards(): off = lax.ppermute(to_off, 'gx', gap)  5.14 us
    ppermute x1, waiting for transfers between devices, shards(): lax.ppermute(to_left, 'gy', [(j + 1, j) for j in range(ny - 1)])  4.9 us
    ppermute x1, starting transfers between devices, shards(): off = lax.ppermute(to_off, 'gx', gap)  4.85 us
    ppermute x1, starting transfers between devices, shards(): lax.ppermute(to_right, 'gy', [(j, j + 1) for j in range(ny - 1)])  4.41 us
    ppermute x1, starting transfers between devices, shards(): off = lax.ppermute(f2_own, 'gx', gap)  3.69 us
  transfers between devices with their start and end apart: 7, of which 6 were waited for; matrix products, arithmetic and copies ran while one was open for 0% of the time, Pallas kernels for 0%

profile of v2, /device:TPU:25, one launch (start us, length us, event | category | flops | bytes accessed | tf_op | source)
XLA Modules:
  0.0 79.4 jit_solution(2427729533156979600)
XLA Ops:
  0.6 0.0 copy-start
  0.6 0.0 copy-start.3
  0.7 0.0 copy-start.2
  0.7 0.0 copy-start.1
  0.7 2.6 %pack.1 = (f32[328,128]{1,0:T(8,128)}, f32[328,128]{1,0:T(8,128)}) custom-call(f32[9,16,512]{2,1,0:T(8,128)} %right_side.1, f32[9,16,512]{2,1,0:T(8,128)} %guess.3, f32[16,512]{1,0:T(8,128)} %vertical.1, s32[16,512]{1,0:T(8,128)} %breaking.1), custom_call_target="tpu_custom_call" | custom-call | tf_op jit(solution)/shard_map/pack/pallas_call | solution.py:502
  3.3 4.4 %collective-permute-start = (f32[328,128]{1,0:T(8,128)}, f32[328,128]{1,0:T(8,128)S(1)}, u32[]{:S(2)}, u32[]{:S(2)}) collective-permute-start(f32[328,128]{1,0:T(8,128)} %get-tuple-element.15), channel_id=1, source_target_pairs={{0,1},{1,2},{2,3},{3,4},{4,5},{5,6},{6,7},{8,9},{9,10},{10,11},{11... | collective-permute-start | bytes 503816 | tf_op jit(solution)/shard_map/ppermute | solution.py:533
  7.7 1.9 %collective-permute-start.1 = (f32[328,128]{1,0:T(8,128)}, f32[328,128]{1,0:T(8,128)S(1)}, u32[]{:S(2)}, u32[]{:S(2)}) collective-permute-start(f32[328,128]{1,0:T(8,128)} %get-tuple-element.16), channel_id=1, source_target_pairs={{1,0},{2,1},{3,2},{4,3},{5,4},{6,5},{7,6},{9,8},{10,9},{11,10},{12... | collective-permute-start | bytes 503816 | tf_op jit(solution)/shard_map/ppermute | solution.py:532
  9.6 1.3 %collective-permute-done.from_left = f32[328,128]{1,0:T(8,128)S(1)} collective-permute-done((f32[328,128]{1,0:T(8,128)}, f32[328,128]{1,0:T(8,128)S(1)}, u32[]{:S(2)}, u32[]{:S(2)}) %collective-permute-start) | collective-permute-done | bytes 167968 | tf_op jit(solution)/shard_map/ppermute | solution.py:533
  11.0 4.9 %collective-permute-done.1.from_right = f32[328,128]{1,0:T(8,128)S(1)} collective-permute-done((f32[328,128]{1,0:T(8,128)}, f32[328,128]{1,0:T(8,128)S(1)}, u32[]{:S(2)}, u32[]{:S(2)}) %collective-permute-start.1) | collective-permute-done | bytes 167968 | tf_op jit(solution)/shard_map/ppermute | solution.py:532
  15.9 0.0 copy-done
  15.9 0.0 copy-done.3
  15.9 0.0 copy-done.2
  15.9 0.0 copy-done.1
  15.9 0.5 widen.1
  16.4 4.9 %collective-permute-start.2 = (f32[7,152,128]{2,1,0:T(8,128)S(1)}, f32[7,152,128]{2,1,0:T(8,128)S(1)}, u32[]{:S(2)}, u32[]{:S(2)}) collective-permute-start(f32[7,152,128]{2,1,0:T(8,128)S(1)} %get-tuple-element.18), channel_id=1, source_target_pairs={{8,16},{24,32},{40,48},{56,64},{72,80},{88,96},{104,112},{120,128}... | collective-permute-start | bytes 1634312 | tf_op jit(solution)/shard_map/ppermute | solution.py:541
  21.3 1.9 %collective-permute-start.3 = (f32[7,152,128]{2,1,0:T(8,128)S(1)}, f32[7,152,128]{2,1,0:T(8,128)S(1)}, u32[]{:S(2)}, u32[]{:S(2)}) collective-permute-start(f32[7,152,128]{2,1,0:T(8,128)S(1)} %get-tuple-element.19), channel_id=1, source_target_pairs={{0,8},{8,0},{16,24},{24,16},{32,40},{40,32},{48,56},{56,48},{64,72... | collective-permute-start | bytes 1634312 | tf_op jit(solution)/shard_map/ppermute | solution.py:542
  23.2 5.1 %collective-permute-done.2.off = f32[7,152,128]{2,1,0:T(8,128)S(1)} collective-permute-done((f32[7,152,128]{2,1,0:T(8,128)S(1)}, f32[7,152,128]{2,1,0:T(8,128)S(1)}, u32[]{:S(2)}, u32[]{:S(2)}) %collective-permute-start.2) | collective-permute-done | bytes 544800 | tf_op jit(solution)/shard_map/ppermute | solution.py:541
  28.3 0.0 collective-permute-done.3.on
  28.3 4.7 %fine.1 = (f32[9,6,24,128]{3,2,1,0:T(8,128)S(1)}, f32[11,6,24,128]{3,2,1,0:T(8,128)S(1)}, f32[9,4,16,128]{3,2,1,0:T(8,128)S(1)}, f32[11,4,16,128]{3,2,1,0:T(8,128)S(1)}, f32[11,2,8,128]{3,2,1,0:T(8,128)S(1)}) custom-call(f32[13,8,16,128]{3,2,1,0:T(8,128)S(1)} %get-tuple-element.17.q, f32[7,152,128]{2,1,0:T(8,128)S(1)} %collective-permute-done.2.off, ...), custom_call_target="tpu_custom_call" | custom-call | tf_op jit(solution)/shard_map/fine/pallas_call | solution.py:502
  33.0 3.7 %collective-permute-start.5 = (f32[11,2,8,128]{3,2,1,0:T(8,128)S(1)}, f32[11,2,8,128]{3,2,1,0:T(8,128)S(1)}, u32[]{:S(2)}, u32[]{:S(2)}) collective-permute-start(f32[11,2,8,128]{3,2,1,0:T(8,128)S(1)} %get-tuple-element.20.own), channel_id=1, source_target_pairs={{8,16},{24,32},{40,48},{56,64},{72,80},{88,96},{104,112},{120,128}... | collective-permute-start | bytes 270344 | tf_op jit(solution)/shard_map/ppermute | solution.py:553
  36.7 1.9 %collective-permute-start.4 = (f32[11,2,8,128]{3,2,1,0:T(8,128)S(1)}, f32[11,2,8,128]{3,2,1,0:T(8,128)S(1)}, u32[]{:S(2)}, u32[]{:S(2)}) collective-permute-start(f32[11,2,8,128]{3,2,1,0:T(8,128)S(1)} %get-tuple-element.20.own), channel_id=1, source_target_pairs={{0,8},{8,0},{16,24},{24,16},{32,40},{40,32},{48,56},{56,48},{64,72... | collective-permute-start | bytes 270344 | tf_op jit(solution)/shard_map/ppermute | solution.py:554
  38.7 0.3 collective-permute-done.5.off
  38.9 1.0 %collective-permute-done.4.on = f32[11,2,8,128]{3,2,1,0:T(8,128)S(1)} collective-permute-done((f32[11,2,8,128]{3,2,1,0:T(8,128)S(1)}, f32[11,2,8,128]{3,2,1,0:T(8,128)S(1)}, u32[]{:S(2)}, u32[]{:S(2)}) %collective-permute-start.4) | collective-permute-done | bytes 90144 | tf_op jit(solution)/shard_map/ppermute | solution.py:554
  39.9 0.6 middle.1
  40.6 27.2 %all_to_all.5.same = f32[32,24,128]{2,1,0:T(8,128)S(1)} all-to-all(f32[32,24,128]{2,1,0:T(8,128)S(1)} %get-tuple-element.21), channel_id=1, replica_groups={{0,16,32,48,64,80,96,112,128,144,160,176,192,208,224,240,256,272,288,30..., dimensions={0} | all-to-all | bytes 786432 | tf_op jit(solution)/shard_map/all_to_all | solution.py:562
  67.8 5.6 %collective-permute-start.6 = (f32[32,24,128]{2,1,0:T(8,128)S(1)}, f32[32,24,128]{2,1,0:T(8,128)S(1)}, u32[]{:S(2)}, u32[]{:S(2)}) collective-permute-start(f32[32,24,128]{2,1,0:T(8,128)S(1)} %all_to_all.5.same), channel_id=1, source_target_pairs={{0,8},{8,0},{16,24},{24,16},{32,40},{40,32},{48,56},{56,48},{64,72... | collective-permute-start | bytes 1179656 | tf_op jit(solution)/shard_map/ppermute | solution.py:565
  73.4 1.3 %collective-permute-done.6.other = f32[32,24,128]{2,1,0:T(8,128)S(1)} collective-permute-done((f32[32,24,128]{2,1,0:T(8,128)S(1)}, f32[32,24,128]{2,1,0:T(8,128)S(1)}, u32[]{:S(2)}, u32[]{:S(2)}) %collective-permute-start.6) | collective-permute-done | bytes 393248 | tf_op jit(solution)/shard_map/ppermute | solution.py:565
  74.7 4.7 %coarse.1 = (f32[9,16,512]{2,1,0:T(8,128)}, f32[9,16,512]{2,1,0:T(8,128)}) custom-call(f32[32,24,128]{2,1,0:T(8,128)S(1)} %all_to_all.5.same, f32[32,24,128]{2,1,0:T(8,128)S(1)} %collective-permute-done.6.other, f32[9,2,16,128]{3,2,1,0:T(8,128)S(1)} %get-tuple-element.22.x2_in, f32[11,2,16,128]{3,2,1,0:T(8,128)S(1)} %get-tuple-element.23.f2, ...), custom_call_target="tpu_custom_call" | custom-call | tf_op jit(solution)/shard_map/coarse/pallas_call | solution.py:502
Async XLA Ops:
  0.6 15.2 %copy-start = (f32[9,16,512]{2,1,0:T(8,128)S(1)}, f32[9,16,512]{2,1,0:T(8,128)}, u32[]{:S(2)}) copy-start(f32[9,16,512]{2,1,0:T(8,128)} %guess.3) | copy-start | bytes 884740
  0.6 15.2 %copy-start.3 = (s32[16,512]{1,0:T(8,128)S(1)}, s32[16,512]{1,0:T(8,128)}, u32[]{:S(2)}) copy-start(s32[16,512]{1,0:T(8,128)} %breaking.1) | copy-start | bytes 98308
  0.7 15.2 %copy-start.2 = (f32[16,512]{1,0:T(8,128)S(1)}, f32[16,512]{1,0:T(8,128)}, u32[]{:S(2)}) copy-start(f32[16,512]{1,0:T(8,128)} %vertical.1) | copy-start | bytes 98308
  0.7 15.2 %copy-start.1 = (f32[9,16,512]{2,1,0:T(8,128)S(1)}, f32[9,16,512]{2,1,0:T(8,128)}, u32[]{:S(2)}) copy-start(f32[9,16,512]{2,1,0:T(8,128)} %right_side.1) | copy-start | bytes 884740
  3.3 7.7 %collective-permute-start = (f32[328,128]{1,0:T(8,128)}, f32[328,128]{1,0:T(8,128)S(1)}, u32[]{:S(2)}, u32[]{:S(2)}) collective-permute-start(f32[328,128]{1,0:T(8,128)} %get-tuple-element.15), channel_id=1, source_target_pairs={{0,1},{1,2},{2,3},{3,4},{4,5},{5,6},{6,7},{8,9},{9,10},{10,11},{11... | collective-permute-start | bytes 503816 | tf_op jit(solution)/shard_map/ppermute | solution.py:533
  7.7 8.2 %collective-permute-start.1 = (f32[328,128]{1,0:T(8,128)}, f32[328,128]{1,0:T(8,128)S(1)}, u32[]{:S(2)}, u32[]{:S(2)}) collective-permute-start(f32[328,128]{1,0:T(8,128)} %get-tuple-element.16), channel_id=1, source_target_pairs={{1,0},{2,1},{3,2},{4,3},{5,4},{6,5},{7,6},{9,8},{10,9},{11,10},{12... | collective-permute-start | bytes 503816 | tf_op jit(solution)/shard_map/ppermute | solution.py:532
  16.4 11.9 %collective-permute-start.2 = (f32[7,152,128]{2,1,0:T(8,128)S(1)}, f32[7,152,128]{2,1,0:T(8,128)S(1)}, u32[]{:S(2)}, u32[]{:S(2)}) collective-permute-start(f32[7,152,128]{2,1,0:T(8,128)S(1)} %get-tuple-element.18), channel_id=1, source_target_pairs={{8,16},{24,32},{40,48},{56,64},{72,80},{88,96},{104,112},{120,128}... | collective-permute-start | bytes 1634312 | tf_op jit(solution)/shard_map/ppermute | solution.py:541
  21.3 7.1 %collective-permute-start.3 = (f32[7,152,128]{2,1,0:T(8,128)S(1)}, f32[7,152,128]{2,1,0:T(8,128)S(1)}, u32[]{:S(2)}, u32[]{:S(2)}) collective-permute-start(f32[7,152,128]{2,1,0:T(8,128)S(1)} %get-tuple-element.19), channel_id=1, source_target_pairs={{0,8},{8,0},{16,24},{24,16},{32,40},{40,32},{48,56},{56,48},{64,72... | collective-permute-start | bytes 1634312 | tf_op jit(solution)/shard_map/ppermute | solution.py:542
  33.0 5.9 %collective-permute-start.5 = (f32[11,2,8,128]{3,2,1,0:T(8,128)S(1)}, f32[11,2,8,128]{3,2,1,0:T(8,128)S(1)}, u32[]{:S(2)}, u32[]{:S(2)}) collective-permute-start(f32[11,2,8,128]{3,2,1,0:T(8,128)S(1)} %get-tuple-element.20.own), channel_id=1, source_target_pairs={{8,16},{24,32},{40,48},{56,64},{72,80},{88,96},{104,112},{120,128}... | collective-permute-start | bytes 270344 | tf_op jit(solution)/shard_map/ppermute | solution.py:553
  36.7 3.2 %collective-permute-start.4 = (f32[11,2,8,128]{3,2,1,0:T(8,128)S(1)}, f32[11,2,8,128]{3,2,1,0:T(8,128)S(1)}, u32[]{:S(2)}, u32[]{:S(2)}) collective-permute-start(f32[11,2,8,128]{3,2,1,0:T(8,128)S(1)} %get-tuple-element.20.own), channel_id=1, source_target_pairs={{0,8},{8,0},{16,24},{24,16},{32,40},{40,32},{48,56},{56,48},{64,72... | collective-permute-start | bytes 270344 | tf_op jit(solution)/shard_map/ppermute | solution.py:554
  67.8 7.0 %collective-permute-start.6 = (f32[32,24,128]{2,1,0:T(8,128)S(1)}, f32[32,24,128]{2,1,0:T(8,128)S(1)}, u32[]{:S(2)}, u32[]{:S(2)}) collective-permute-start(f32[32,24,128]{2,1,0:T(8,128)S(1)} %all_to_all.5.same), channel_id=1, source_target_pairs={{0,8},{8,0},{16,24},{24,16},{32,40},{40,32},{48,56},{56,48},{64,72... | collective-permute-start | bytes 1179656 | tf_op jit(solution)/shard_map/ppermute | solution.py:565

commit v3 on v2

--- a/solution.py
+++ b/solution.py
@@ -10,6 +10,8 @@
 VC, BT = K, K + 1
 TILES = 23
 SIDE = TILES // 2
+PLANE = 8
+EXTRA = SIDE - PLANE
 damping = 0.8
 keep = 0.2
 break_gain = 0.05
@@ -194,7 +196,7 @@
     return right_side[k] - (4.0 + 2.0 * vc + bt) * v + hs + vc * vs
 
 
-def pack_kernel(rs_in, g_in, vc_in, br_in, to_left, to_right, right_side, guess, vertical, breaking, sems):
+def pack_kernel(rs_in, g_in, vc_in, br_in, to_inside, to_across, right_side, guess, vertical, breaking, sems):
     pairs = ((vc_in, vertical), (br_in, breaking), (g_in, guess), (rs_in, right_side))
     copies = [pltpu.make_async_copy(a, b, sems.at[i]) for i, (a, b) in enumerate(pairs)]
     for copy in copies:
@@ -206,94 +208,101 @@
     vc = vertical[...]
     bt = break_gain * breaking[...].astype(F32)
 
-    def pack(plane, field):
-        near, far = field[:, 0:128], field[:, 128:256]
-        to_left[24 * plane : 24 * plane + 16, :] = near
-        to_left[24 * plane + 16 : 24 * plane + 24, :] = jnp.where(
-            lane8 < 64, far[0:8], pltpu.roll(far[8:16], 64, 1)
-        )
-        near, far = field[:, 384:512], field[:, 256:384]
-        to_right[24 * plane : 24 * plane + 16, :] = near
-        to_right[24 * plane + 16 : 24 * plane + 24, :] = jnp.where(
-            lane8 >= 64, far[0:8], pltpu.roll(far[8:16], 64, 1)
-        )
-
-    first = jnp.zeros((16, 128), F32)
-    last = jnp.zeros((16, 128), F32)
-    to_left[TOP_AT:Y_ROWS, :] = jnp.zeros((Y_ROWS - TOP_AT, 128), F32)
-    to_right[TOP_AT:Y_ROWS, :] = jnp.zeros((Y_ROWS - TOP_AT, 128), F32)
-    lane1 = lanes(1)
-    for k in range(K):
-        v = guess[k]
-        f = own_defect(right_side, guess, vc, bt, k, 0.0, 0.0)
-        pack(k, f)
-        first = jnp.where(lane == k, jnp.broadcast_to(v[:, 0:1], (16, 128)), first)
-        last = jnp.where(lane == k, jnp.broadcast_to(v[:, 511:512], (16, 128)), last)
-        top, bottom = v[0:1], v[15:16]
-        to_left[TOP_AT + k : TOP_AT + k + 1, :] = top[:, 0:128]
-        to_left[BOTTOM_AT + k : BOTTOM_AT + k + 1, :] = bottom[:, 0:128]
-        to_left[FAR_AT + k : FAR_AT + k + 1, :] = jnp.where(
-            lane1 < 64, top[:, 128:256], pltpu.roll(bottom[:, 128:256], 64, 1)
-        )
-        to_right[TOP_AT + k : TOP_AT + k + 1, :] = top[:, 384:512]
-        to_right[BOTTOM_AT + k : BOTTOM_AT + k + 1, :] = bottom[:, 384:512]
-        to_right[FAR_AT + k : FAR_AT + k + 1, :] = jnp.where(
-            lane1 >= 64, top[:, 256:384], pltpu.roll(bottom[:, 256:384], 64, 1)
-        )
-    pack(VC, vc)
-    pack(BT, bt)
-    to_left[COLS_AT : COLS_AT + 16, :] = first
-    to_right[COLS_AT : COLS_AT + 16, :] = last
-
-
-def widen_kernel(right_side, guess, vertical, breaking, from_left, from_right, q, to_on, to_off):
+    def pack_all(to_right, to_left):
+        def pack(plane, field):
+            near, far = field[:, 0:128], field[:, 128:256]
+            to_left[24 * plane : 24 * plane + 16, :] = near
+            to_left[24 * plane + 16 : 24 * plane + 24, :] = jnp.where(
+                lane8 < 64, far[0:8], pltpu.roll(far[8:16], 64, 1)
+            )
+            near, far = field[:, 384:512], field[:, 256:384]
+            to_right[24 * plane : 24 * plane + 16, :] = near
+            to_right[24 * plane + 16 : 24 * plane + 24, :] = jnp.where(
+                lane8 >= 64, far[0:8], pltpu.roll(far[8:16], 64, 1)
+            )
+
+        first = jnp.zeros((16, 128), F32)
+        last = jnp.zeros((16, 128), F32)
+        to_left[TOP_AT:Y_ROWS, :] = jnp.zeros((Y_ROWS - TOP_AT, 128), F32)
+        to_right[TOP_AT:Y_ROWS, :] = jnp.zeros((Y_ROWS - TOP_AT, 128), F32)
+        lane1 = lanes(1)
+        for k in range(K):
+            v = guess[k]
+            f = own_defect(right_side, guess, vc, bt, k, 0.0, 0.0)
+            pack(k, f)
+            first = jnp.where(lane == k, jnp.broadcast_to(v[:, 0:1], (16, 128)), first)
+            last = jnp.where(lane == k, jnp.broadcast_to(v[:, 511:512], (16, 128)), last)
+            top, bottom = v[0:1], v[15:16]
+            to_left[TOP_AT + k : TOP_AT + k + 1, :] = top[:, 0:128]
+            to_left[BOTTOM_AT + k : BOTTOM_AT + k + 1, :] = bottom[:, 0:128]
+            to_left[FAR_AT + k : FAR_AT + k + 1, :] = jnp.where(
+                lane1 < 64, top[:, 128:256], pltpu.roll(bottom[:, 128:256], 64, 1)
+            )
+            to_right[TOP_AT + k : TOP_AT + k + 1, :] = top[:, 384:512]
+            to_right[BOTTOM_AT + k : BOTTOM_AT + k + 1, :] = bottom[:, 384:512]
+            to_right[FAR_AT + k : FAR_AT + k + 1, :] = jnp.where(
+                lane1 >= 64, top[:, 256:384], pltpu.roll(bottom[:, 256:384], 64, 1)
+            )
+        pack(VC, vc)
+        pack(BT, bt)
+        to_left[COLS_AT : COLS_AT + 16, :] = first
+        to_right[COLS_AT : COLS_AT + 16, :] = last
+
+    parity_copy(lax.axis_index("gy") % 2 == 0, to_inside, to_across, lambda left, right: pack_all(right, left))
+
+
+def widen_kernel(right_side, guess, vertical, breaking, across, inside, q, to_on, to_off):
     lane = lanes(16)
-    lane8 = lanes(8)
-    lane1 = lanes(1)
-    left_cols = from_left[COLS_AT : COLS_AT + 16, :]
-    right_cols = from_right[COLS_AT : COLS_AT + 16, :]
-    vc = vertical[...]
-    bt = break_gain * breaking[...].astype(F32)
-    for k in range(PLANES):
-        far = from_left[24 * k + 16 : 24 * k + 24, :]
-        q[k, 0, 0:8, :] = jnp.where(lane8 >= 64, far, 0.0)
-        q[k, 0, 8:16, :] = jnp.where(lane8 >= 64, pltpu.roll(far, 64, 1), 0.0)
-        far = from_right[24 * k + 16 : 24 * k + 24, :]
-        q[k, 7, 0:8, :] = jnp.where(lane8 < 64, far, 0.0)
-        q[k, 7, 8:16, :] = jnp.where(lane8 < 64, pltpu.roll(far, 64, 1), 0.0)
-        near_left = from_left[24 * k : 24 * k + 16, :]
-        near_right = from_right[24 * k : 24 * k + 16, :]
-        if k < K:
-            v = guess[k]
-            first = jnp.broadcast_to(v[:, 0:1], (16, 128))
-            last = jnp.broadcast_to(v[:, 511:512], (16, 128))
-            q[k, 1] = near_left + jnp.where(lane == 127, first, 0.0)
-            q[k, 6] = near_right + jnp.where(lane == 0, last, 0.0)
-            own = own_defect(right_side, guess, vc, bt, k, left_cols[:, k : k + 1], right_cols[:, k : k + 1])
-        else:
-            q[k, 1] = near_left
-            q[k, 6] = near_right
-            own = vc if k == VC else bt
-        for c in range(4):
-            q[k, 2 + c] = own[:, 128 * c : 128 * c + 128]
-    for plane, row, near_at in ((PLANES, 0, TOP_AT), (PLANES + 1, 15, BOTTOM_AT)):
-        for c in range(8):
-            q[plane, c] = jnp.zeros((16, 128), F32)
-        for k in range(K):
-            at = slice(k, k + 1)
-            v = guess[k, row : row + 1, :]
+
+    def assemble(from_left, from_right):
+        lane = lanes(16)
+        lane8 = lanes(8)
+        lane1 = lanes(1)
+        left_cols = from_left[COLS_AT : COLS_AT + 16, :]
+        right_cols = from_right[COLS_AT : COLS_AT + 16, :]
+        vc = vertical[...]
+        bt = break_gain * breaking[...].astype(F32)
+        for k in range(PLANES):
+            far = from_left[24 * k + 16 : 24 * k + 24, :]
+            q[k, 0, 0:8, :] = jnp.where(lane8 >= 64, far, 0.0)
+            q[k, 0, 8:16, :] = jnp.where(lane8 >= 64, pltpu.roll(far, 64, 1), 0.0)
+            far = from_right[24 * k + 16 : 24 * k + 24, :]
+            q[k, 7, 0:8, :] = jnp.where(lane8 < 64, far, 0.0)
+            q[k, 7, 8:16, :] = jnp.where(lane8 < 64, pltpu.roll(far, 64, 1), 0.0)
+            near_left = from_left[24 * k : 24 * k + 16, :]
+            near_right = from_right[24 * k : 24 * k + 16, :]
+            if k < K:
+                v = guess[k]
+                first = jnp.broadcast_to(v[:, 0:1], (16, 128))
+                last = jnp.broadcast_to(v[:, 511:512], (16, 128))
+                q[k, 1] = near_left + jnp.where(lane == 127, first, 0.0)
+                q[k, 6] = near_right + jnp.where(lane == 0, last, 0.0)
+                own = own_defect(right_side, guess, vc, bt, k, left_cols[:, k : k + 1], right_cols[:, k : k + 1])
+            else:
+                q[k, 1] = near_left
+                q[k, 6] = near_right
+                own = vc if k == VC else bt
             for c in range(4):
-                q[plane, 2 + c, at, :] = v[:, 128 * c : 128 * c + 128]
-            q[plane, 1, at, :] = from_left[near_at + k : near_at + k + 1, :]
-            q[plane, 6, at, :] = from_right[near_at + k : near_at + k + 1, :]
-            far_left = from_left[FAR_AT + k : FAR_AT + k + 1, :]
-            far_right = from_right[FAR_AT + k : FAR_AT + k + 1, :]
-            if plane == PLANES + 1:
-                far_left = pltpu.roll(far_left, 64, 1)
-                far_right = pltpu.roll(far_right, 64, 1)
-            q[plane, 0, at, :] = jnp.where(lane1 >= 64, far_left, 0.0)
-            q[plane, 7, at, :] = jnp.where(lane1 < 64, far_right, 0.0)
-
+                q[k, 2 + c] = own[:, 128 * c : 128 * c + 128]
+        for plane, row, near_at in ((PLANES, 0, TOP_AT), (PLANES + 1, 15, BOTTOM_AT)):
+            for c in range(8):
+                q[plane, c] = jnp.zeros((16, 128), F32)
+            for k in range(K):
+                at = slice(k, k + 1)
+                v = guess[k, row : row + 1, :]
+                for c in range(4):
+                    q[plane, 2 + c, at, :] = v[:, 128 * c : 128 * c + 128]
+                q[plane, 1, at, :] = from_left[near_at + k : near_at + k + 1, :]
+                q[plane, 6, at, :] = from_right[near_at + k : near_at + k + 1, :]
+                far_left = from_left[FAR_AT + k : FAR_AT + k + 1, :]
+                far_right = from_right[FAR_AT + k : FAR_AT + k + 1, :]
+                if plane == PLANES + 1:
+                    far_left = pltpu.roll(far_left, 64, 1)
+                    far_right = pltpu.roll(far_right, 64, 1)
+                q[plane, 0, at, :] = jnp.where(lane1 >= 64, far_left, 0.0)
+                q[plane, 7, at, :] = jnp.where(lane1 < 64, far_right, 0.0)
+
+    parity_copy(lax.axis_index("gy") % 2 == 0, inside, across, assemble)
 
     def fill(buffer, long, short, plane):
         for c in range(7):
@@ -415,17 +424,44 @@
                         x[k + 1, fc, pl.ds(8 + p, used, stride=2), :] += e
 
 
+def edge_kernel(plane, copy, edge):
+    copy[...] = plane[...]
+    first = lax.axis_index("gx") % PLANE < PLANE // 2
+
+    @pl.when(first)
+    def _():
+        edge[...] = plane[PLANE - EXTRA : PLANE]
+
+    @pl.when(jnp.logical_not(first))
+    def _():
+        edge[...] = plane[0:EXTRA]
+
+
 def coarse_kernel(
-    same, other, x2_in, f2, x1_in, f1, x0_in, f0, guess, updated, new_defect,
-    f3, xa, xb, inv3, ratio3, rs3, gs3, f4, ya, yb, inv4, es3, es2, xc, xd, inv2, es1, xe, xf, inv1, es0, xg, xh, inv0,
+    plane, beyond, before, after, x2_in, f2, x1_in, f1, x0_in, f0, guess, updated, new_defect,
+    window, f3, xa, xb, inv3, ratio3, rs3, gs3, f4, ya, yb, inv4, es3, es2, xc, xd, inv2, es1, xe, xf, inv1, es0, xg, xh, inv0,
 ):
     gx = lax.axis_index("gx")
-    tiles = 2 * same.shape[0]
+    tiles = lax.axis_size("gx")
+    place = gx % PLANE
+    above, below = EXTRA, EXTRA + 2 * PLANE
+
+    window[above : above + PLANE] = before[...]
+    window[above + PLANE : below] = plane[...]
+    window[below : below + PLANE] = after[...]
+
+    @pl.when(place < PLANE // 2)
+    def _():
+        window[0:EXTRA] = beyond[...]
+
+    @pl.when(place >= PLANE // 2)
+    def _():
+        window[below + PLANE : below + PLANE + EXTRA] = beyond[...]
+
     for t in range(TILES):
         tile = gx - SIDE + t
         valid = jnp.logical_and(tile >= 0, tile < tiles)
-        chip = jnp.clip(tile, 0, tiles - 1) // 2
-        piece = jnp.where(valid, (same if t % 2 else other)[chip], 0.0)
+        piece = jnp.where(valid, window[place + t], 0.0)
         for k in range(PLANES):
             f3[k, 0, 2 * t : 2 * t + 2, :] = piece[2 * k : 2 * k + 2]
     for k in range(PLANES):
@@ -520,7 +556,7 @@
     gap = [(i, i + 1) for i in range(1, nx - 1, 2)]
     gap = gap + [(b, a) for a, b in gap]
 
-    to_left, to_right = call(
+    to_inside, to_across = call(
         pack_kernel,
         "pack",
         [(Y_ROWS, 128), (Y_ROWS, 128)],
@@ -529,14 +565,16 @@
         space=pltpu.HBM,
         mib=62,
     )
-    from_right = lax.ppermute(to_left, "gy", [(j + 1, j) for j in range(ny - 1)])
-    from_left = lax.ppermute(to_right, "gy", [(j, j + 1) for j in range(ny - 1)])
+    inside = [(j, j ^ 1) for j in range(ny)]
+    across = [(j, j + 1) for j in range(1, ny - 1, 2)]
+    across = lax.ppermute(to_across, "gy", across + [(b, a) for a, b in across])
+    inside = lax.ppermute(to_inside, "gy", inside)
     q, to_on, to_off = call(
         widen_kernel,
         "widen",
         [(PLANES + 2, 8, 16, 128), (7, X_ROWS, 128), (7, X_ROWS, 128)],
         [],
-        right_side, guess, vertical, breaking, from_left, from_right,
+        right_side, guess, vertical, breaking, across, inside,
     )
     off = lax.ppermute(to_off, "gx", gap)
     on = lax.ppermute(to_on, "gx", chip)
@@ -555,27 +593,32 @@
     x2, f2, chunk = call(
         middle_kernel,
         "middle",
-        [(K, 2, 16, 128), (PLANES, 2, 16, 128), (nx // 2, 24, 128)],
+        [(K, 2, 16, 128), (PLANES, 2, 16, 128), (PLANE, 24, 128)],
         [field(2, 16), field(2, 16), (2, 16, 128), (2, 16, 128), (2, 32, 128), (K, 8, 256), (PLANES, 1, 8, 128)],
         f2_own, on, off,
     )
-    same = lax.all_to_all(
-        chunk, "gx", 0, 0, axis_index_groups=[list(range(0, nx, 2)), list(range(1, nx, 2))], tiled=True
-    )
-    other = lax.ppermute(same, "gx", chip)
+    groups = [list(range(i, i + PLANE)) for i in range(0, nx, PLANE)]
+    plane = lax.all_to_all(chunk, "gx", 0, 0, axis_index_groups=groups, tiled=True)
+    plane, edge = call(edge_kernel, "edge", [(PLANE, 24, 128), (EXTRA, 24, 128)], [], plane)
+    far = [(i, i + 2 * PLANE) for i in range(nx - 2 * PLANE) if i % PLANE < EXTRA]
+    far += [(i, i - 2 * PLANE) for i in range(2 * PLANE, nx) if i % PLANE >= PLANE - EXTRA]
+    beyond = lax.ppermute(edge, "gx", far)
+    before = lax.ppermute(plane, "gx", [(i, i + PLANE) for i in range(nx - PLANE)])
+    after = lax.ppermute(plane, "gx", [(i + PLANE, i) for i in range(nx - PLANE)])
     return tuple(
         call(
             coarse_kernel,
             "coarse",
             [(K, 16, 512), (K, 16, 512)],
             [
+                (2 * EXTRA + 3 * PLANE, 24, 128),
                 (PLANES, 1, 48, 128), field(1, 48), field(1, 48), (1, 48, 128), (1, 48, 128), (1, 64, 128), (K, 24, 128),
                 (PLANES, 1, 24, 128), field(1, 24), field(1, 24), (1, 24, 128), (K * 24, 128),
                 (K * 8, 128), field(2, 16), field(2, 16), (2, 16, 128),
                 (K * 2 * 8, 128), field(4, 16), field(4, 16), (4, 16, 128),
                 (K * 4 * 16, 128), field(6, 24), field(6, 24), (6, 24, 128),
             ],
-            same, other, x2, f2, x1, f1, x0, f0, guess,
+            plane, beyond, before, after, x2, f2, x1, f1, x0, f0, guess,
         )
     )
 

time: 79.7 us -> 73.6 us (0.923)
  the two profiles are of different devices: /device:TPU:25 before, /device:TPU:88 now
where the time goes in v3:
time: 73.6 us; the launch traced here: 73.2 us
  starting transfers between devices  31.5 us (43%)
  waiting for transfers between devices  19 us (26%)
  Pallas kernels  13.1 us (18%)
  blocking collectives  8.83 us (12%)
  between operations  0.79 us (1%)
    pallas_call x6, Pallas kernels, call(): pl.pallas_call(kernel, name=name, out_shape=[jax.ShapeDtypeStruct(s, F32)...  13.1 us
    ppermute x1, starting transfers between devices, shards(): beyond = lax.ppermute(edge, 'gx', far)  9.36 us
    all_to_all x1, blocking collectives, shards(): lax.all_to_all(chunk, 'gx', 0, 0, axis_index_groups=groups, tiled=True)  8.83 us
    ppermute x1, waiting for transfers between devices, shards(): off = lax.ppermute(to_off, 'gx', gap)  7.39 us
    ppermute x1, starting transfers between devices, shards(): across = lax.ppermute(to_across, 'gy', across + [(b, a) for a, b in across])  4.69 us
    ppermute x1, starting transfers between devices, shards(): lax.ppermute(plane, 'gx', [(i, i + PLANE) for i in range(nx - PLANE)])  4.27 us
    ppermute x1, waiting for transfers between devices, shards(): off = lax.ppermute(f2_own, 'gx', gap)  4.07 us
    ppermute x1, starting transfers between devices, shards(): on = lax.ppermute(to_on, 'gx', chip)  3.42 us
  transfers between devices with their start and end apart: 9, of which 5 were waited for; matrix products, arithmetic and copies ran while one was open for 0% of the time, Pallas kernels for 0%

profile of v3, /device:TPU:88, one launch (start us, length us, event | category | flops | bytes accessed | tf_op | source)
XLA Modules:
  0.0 73.2 jit_solution(13502541316721037590)
XLA Ops:
  0.6 0.0 copy-start
  0.6 0.0 copy-start.3
  0.7 0.0 copy-start.2
  0.7 0.0 copy-start.1
  0.7 2.6 %pack.1 = (f32[328,128]{1,0:T(8,128)}, f32[328,128]{1,0:T(8,128)}) custom-call(f32[9,16,512]{2,1,0:T(8,128)} %right_side.1, f32[9,16,512]{2,1,0:T(8,128)} %guess.3, f32[16,512]{1,0:T(8,128)} %vertical.1, s32[16,512]{1,0:T(8,128)} %breaking.1), custom_call_target="tpu_custom_call" | custom-call | tf_op jit(solution)/shard_map/pack/pallas_call | solution.py:538
  3.3 4.7 %collective-permute-start = (f32[328,128]{1,0:T(8,128)}, f32[328,128]{1,0:T(8,128)S(1)}, u32[]{:S(2)}, u32[]{:S(2)}) collective-permute-start(f32[328,128]{1,0:T(8,128)} %get-tuple-element.17), channel_id=1, source_target_pairs={{1,2},{3,4},{5,6},{2,1},{4,3},{6,5},{9,10},{11,12},{13,14},{10,9},... | collective-permute-start | bytes 503816 | tf_op jit(solution)/shard_map/ppermute | solution.py:570
  8.0 1.9 %collective-permute-start.1 = (f32[328,128]{1,0:T(8,128)}, f32[328,128]{1,0:T(8,128)S(1)}, u32[]{:S(2)}, u32[]{:S(2)}) collective-permute-start(f32[328,128]{1,0:T(8,128)} %get-tuple-element.18), channel_id=1, source_target_pairs={{0,1},{1,0},{2,3},{3,2},{4,5},{5,4},{6,7},{7,6},{8,9},{9,8},{10,11... | collective-permute-start | bytes 503816 | tf_op jit(solution)/shard_map/ppermute | solution.py:571
  9.9 2.7 %collective-permute-done.across = f32[328,128]{1,0:T(8,128)S(1)} collective-permute-done((f32[328,128]{1,0:T(8,128)}, f32[328,128]{1,0:T(8,128)S(1)}, u32[]{:S(2)}, u32[]{:S(2)}) %collective-permute-start) | collective-permute-done | bytes 167968 | tf_op jit(solution)/shard_map/ppermute | solution.py:570
  12.7 3.2 %collective-permute-done.1.inside = f32[328,128]{1,0:T(8,128)S(1)} collective-permute-done((f32[328,128]{1,0:T(8,128)}, f32[328,128]{1,0:T(8,128)S(1)}, u32[]{:S(2)}, u32[]{:S(2)}) %collective-permute-start.1) | collective-permute-done | bytes 167968 | tf_op jit(solution)/shard_map/ppermute | solution.py:571
  15.9 0.0 copy-done
  15.9 0.0 copy-done.3
  15.9 0.0 copy-done.2
  15.9 0.0 copy-done.1
  15.9 0.5 widen.1
  16.4 2.0 %collective-permute-start.2 = (f32[7,152,128]{2,1,0:T(8,128)S(1)}, f32[7,152,128]{2,1,0:T(8,128)S(1)}, u32[]{:S(2)}, u32[]{:S(2)}) collective-permute-start(f32[7,152,128]{2,1,0:T(8,128)S(1)} %get-tuple-element.20), channel_id=1, source_target_pairs={{8,16},{24,32},{40,48},{56,64},{72,80},{88,96},{104,112},{120,128}... | collective-permute-start | bytes 1634312 | tf_op jit(solution)/shard_map/ppermute | solution.py:579
  18.4 3.4 %collective-permute-start.3 = (f32[7,152,128]{2,1,0:T(8,128)S(1)}, f32[7,152,128]{2,1,0:T(8,128)S(1)}, u32[]{:S(2)}, u32[]{:S(2)}) collective-permute-start(f32[7,152,128]{2,1,0:T(8,128)S(1)} %get-tuple-element.21), channel_id=1, source_target_pairs={{0,8},{8,0},{16,24},{24,16},{32,40},{40,32},{48,56},{56,48},{64,72... | collective-permute-start | bytes 1634312 | tf_op jit(solution)/shard_map/ppermute | solution.py:580
  21.9 7.4 %collective-permute-done.2.off = f32[7,152,128]{2,1,0:T(8,128)S(1)} collective-permute-done((f32[7,152,128]{2,1,0:T(8,128)S(1)}, f32[7,152,128]{2,1,0:T(8,128)S(1)}, u32[]{:S(2)}, u32[]{:S(2)}) %collective-permute-start.2) | collective-permute-done | bytes 544800 | tf_op jit(solution)/shard_map/ppermute | solution.py:579
  29.3 0.0 collective-permute-done.3.on
  29.3 4.7 %fine.1 = (f32[9,6,24,128]{3,2,1,0:T(8,128)S(1)}, f32[11,6,24,128]{3,2,1,0:T(8,128)S(1)}, f32[9,4,16,128]{3,2,1,0:T(8,128)S(1)}, f32[11,4,16,128]{3,2,1,0:T(8,128)S(1)}, f32[11,2,8,128]{3,2,1,0:T(8,128)S(1)}) custom-call(f32[13,8,16,128]{3,2,1,0:T(8,128)S(1)} %get-tuple-element.19.q, f32[7,152,128]{2,1,0:T(8,128)S(1)} %collective-permute-done.2.off, ...), custom_call_target="tpu_custom_call" | custom-call | tf_op jit(solution)/shard_map/fine/pallas_call | solution.py:538
  34.0 2.0 %collective-permute-start.5 = (f32[11,2,8,128]{3,2,1,0:T(8,128)S(1)}, f32[11,2,8,128]{3,2,1,0:T(8,128)S(1)}, u32[]{:S(2)}, u32[]{:S(2)}) collective-permute-start(f32[11,2,8,128]{3,2,1,0:T(8,128)S(1)} %get-tuple-element.22.own), channel_id=1, source_target_pairs={{8,16},{24,32},{40,48},{56,64},{72,80},{88,96},{104,112},{120,128}... | collective-permute-start | bytes 270344 | tf_op jit(solution)/shard_map/ppermute | solution.py:591
  36.0 1.9 %collective-permute-start.4 = (f32[11,2,8,128]{3,2,1,0:T(8,128)S(1)}, f32[11,2,8,128]{3,2,1,0:T(8,128)S(1)}, u32[]{:S(2)}, u32[]{:S(2)}) collective-permute-start(f32[11,2,8,128]{3,2,1,0:T(8,128)S(1)} %get-tuple-element.22.own), channel_id=1, source_target_pairs={{0,8},{8,0},{16,24},{24,16},{32,40},{40,32},{48,56},{56,48},{64,72... | collective-permute-start | bytes 270344 | tf_op jit(solution)/shard_map/ppermute | solution.py:592
  37.9 4.1 %collective-permute-done.5.off = f32[11,2,8,128]{3,2,1,0:T(8,128)S(1)} collective-permute-done((f32[11,2,8,128]{3,2,1,0:T(8,128)S(1)}, f32[11,2,8,128]{3,2,1,0:T(8,128)S(1)}, u32[]{:S(2)}, u32[]{:S(2)}) %collective-permute-start.5) | collective-permute-done | bytes 90144 | tf_op jit(solution)/shard_map/ppermute | solution.py:591
  42.0 0.0 collective-permute-done.4.on
  42.0 0.5 middle.1
  42.5 8.8 %all_to_all.5.plane = f32[8,24,128]{2,1,0:T(8,128)S(1)} all-to-all(f32[8,24,128]{2,1,0:T(8,128)S(1)} %get-tuple-element.23), channel_id=1, replica_groups={{0,8,16,24,32,40,48,56},{64,72,80,88,96,104,112,120},{128,136,144,152,1..., dimensions={0} | all-to-all | bytes 196608 | tf_op jit(solution)/shard_map/all_to_all | solution.py:601
  51.4 1.9 %collective-permute-start.8 = (f32[8,24,128]{2,1,0:T(8,128)S(1)}, f32[8,24,128]{2,1,0:T(8,128)S(1)}, u32[]{:S(2)}, u32[]{:S(2)}) collective-permute-start(f32[8,24,128]{2,1,0:T(8,128)S(1)} %get-tuple-element.24.plane), channel_id=1, source_target_pairs={{64,0},{72,8},{80,16},{88,24},{96,32},{104,40},{112,48},{120,56},{... | collective-permute-start | bytes 294920 | tf_op jit(solution)/shard_map/ppermute | solution.py:607
  53.3 4.3 %collective-permute-start.7 = (f32[8,24,128]{2,1,0:T(8,128)S(1)}, f32[8,24,128]{2,1,0:T(8,128)S(1)}, u32[]{:S(2)}, u32[]{:S(2)}) collective-permute-start(f32[8,24,128]{2,1,0:T(8,128)S(1)} %get-tuple-element.24.plane), channel_id=1, source_target_pairs={{0,64},{8,72},{16,80},{24,88},{32,96},{40,104},{48,112},{56,120},{... | collective-permute-start | bytes 294920 | tf_op jit(solution)/shard_map/ppermute | solution.py:606
  57.6 9.4 %collective-permute-start.6 = (f32[3,24,128]{2,1,0:T(8,128)S(1)}, f32[3,24,128]{2,1,0:T(8,128)S(1)}, u32[]{:S(2)}, u32[]{:S(2)}) collective-permute-start(f32[3,24,128]{2,1,0:T(8,128)S(1)} %get-tuple-element.25), channel_id=1, source_target_pairs={{0,128},{8,136},{16,144},{64,192},{72,200},{80,208},{128,256},{136... | collective-permute-start | bytes 110600 | tf_op jit(solution)/shard_map/ppermute | solution.py:605
  66.9 1.6 %collective-permute-done.6.beyond = f32[3,24,128]{2,1,0:T(8,128)S(1)} collective-permute-done((f32[3,24,128]{2,1,0:T(8,128)S(1)}, f32[3,24,128]{2,1,0:T(8,128)S(1)}, u32[]{:S(2)}, u32[]{:S(2)}) %collective-permute-start.6) | collective-permute-done | bytes 36896 | tf_op jit(solution)/shard_map/ppermute | solution.py:605
  68.5 0.0 collective-permute-done.8.after
  68.5 0.0 collective-permute-done.7.before
  68.5 4.7 %coarse.1 = (f32[9,16,512]{2,1,0:T(8,128)}, f32[9,16,512]{2,1,0:T(8,128)}) custom-call(f32[8,24,128]{2,1,0:T(8,128)S(1)} %get-tuple-element.24.plane, f32[3,24,128]{2,1,0:T(8,128)S(1)} %collective-permute-done.6.beyond, f32[8,24,128]{2,1,0:T(8,128)S(1)} %collective-permute-done.7.before, f32[8,24,128]{2,1,0:T(8,128)S(1)} %collective-permute-done.8.after, ...), custom_call_target="tpu_custom_call" | custom-call | tf_op jit(solution)/shard_map/coarse/pallas_call | solution.py:538
  (1 shorter events, 0.0 us)
Async XLA Ops:
  0.6 15.2 %copy-start = (f32[9,16,512]{2,1,0:T(8,128)S(1)}, f32[9,16,512]{2,1,0:T(8,128)}, u32[]{:S(2)}) copy-start(f32[9,16,512]{2,1,0:T(8,128)} %guess.3) | copy-start | bytes 884740
  0.6 15.2 %copy-start.3 = (s32[16,512]{1,0:T(8,128)S(1)}, s32[16,512]{1,0:T(8,128)}, u32[]{:S(2)}) copy-start(s32[16,512]{1,0:T(8,128)} %breaking.1) | copy-start | bytes 98308
  0.7 15.2 %copy-start.2 = (f32[16,512]{1,0:T(8,128)S(1)}, f32[16,512]{1,0:T(8,128)}, u32[]{:S(2)}) copy-start(f32[16,512]{1,0:T(8,128)} %vertical.1) | copy-start | bytes 98308
  0.7 15.2 %copy-start.1 = (f32[9,16,512]{2,1,0:T(8,128)S(1)}, f32[9,16,512]{2,1,0:T(8,128)}, u32[]{:S(2)}) copy-start(f32[9,16,512]{2,1,0:T(8,128)} %right_side.1) | copy-start | bytes 884740
  3.3 9.3 %collective-permute-start = (f32[328,128]{1,0:T(8,128)}, f32[328,128]{1,0:T(8,128)S(1)}, u32[]{:S(2)}, u32[]{:S(2)}) collective-permute-start(f32[328,128]{1,0:T(8,128)} %get-tuple-element.17), channel_id=1, source_target_pairs={{1,2},{3,4},{5,6},{2,1},{4,3},{6,5},{9,10},{11,12},{13,14},{10,9},... | collective-permute-start | bytes 503816 | tf_op jit(solution)/shard_map/ppermute | solution.py:570
  8.0 7.9 %collective-permute-start.1 = (f32[328,128]{1,0:T(8,128)}, f32[328,128]{1,0:T(8,128)S(1)}, u32[]{:S(2)}, u32[]{:S(2)}) collective-permute-start(f32[328,128]{1,0:T(8,128)} %get-tuple-element.18), channel_id=1, source_target_pairs={{0,1},{1,0},{2,3},{3,2},{4,5},{5,4},{6,7},{7,6},{8,9},{9,8},{10,11... | collective-permute-start | bytes 503816 | tf_op jit(solution)/shard_map/ppermute | solution.py:571
  16.4 12.8 %collective-permute-start.2 = (f32[7,152,128]{2,1,0:T(8,128)S(1)}, f32[7,152,128]{2,1,0:T(8,128)S(1)}, u32[]{:S(2)}, u32[]{:S(2)}) collective-permute-start(f32[7,152,128]{2,1,0:T(8,128)S(1)} %get-tuple-element.20), channel_id=1, source_target_pairs={{8,16},{24,32},{40,48},{56,64},{72,80},{88,96},{104,112},{120,128}... | collective-permute-start | bytes 1634312 | tf_op jit(solution)/shard_map/ppermute | solution.py:579
  18.4 10.8 %collective-permute-start.3 = (f32[7,152,128]{2,1,0:T(8,128)S(1)}, f32[7,152,128]{2,1,0:T(8,128)S(1)}, u32[]{:S(2)}, u32[]{:S(2)}) collective-permute-start(f32[7,152,128]{2,1,0:T(8,128)S(1)} %get-tuple-element.21), channel_id=1, source_target_pairs={{0,8},{8,0},{16,24},{24,16},{32,40},{40,32},{48,56},{56,48},{64,72... | collective-permute-start | bytes 1634312 | tf_op jit(solution)/shard_map/ppermute | solution.py:580
  34.0 8.0 %collective-permute-start.5 = (f32[11,2,8,128]{3,2,1,0:T(8,128)S(1)}, f32[11,2,8,128]{3,2,1,0:T(8,128)S(1)}, u32[]{:S(2)}, u32[]{:S(2)}) collective-permute-start(f32[11,2,8,128]{3,2,1,0:T(8,128)S(1)} %get-tuple-element.22.own), channel_id=1, source_target_pairs={{8,16},{24,32},{40,48},{56,64},{72,80},{88,96},{104,112},{120,128}... | collective-permute-start | bytes 270344 | tf_op jit(solution)/shard_map/ppermute | solution.py:591
  36.0 6.0 %collective-permute-start.4 = (f32[11,2,8,128]{3,2,1,0:T(8,128)S(1)}, f32[11,2,8,128]{3,2,1,0:T(8,128)S(1)}, u32[]{:S(2)}, u32[]{:S(2)}) collective-permute-start(f32[11,2,8,128]{3,2,1,0:T(8,128)S(1)} %get-tuple-element.22.own), channel_id=1, source_target_pairs={{0,8},{8,0},{16,24},{24,16},{32,40},{40,32},{48,56},{56,48},{64,72... | collective-permute-start | bytes 270344 | tf_op jit(solution)/shard_map/ppermute | solution.py:592
  51.4 17.2 %collective-permute-start.8 = (f32[8,24,128]{2,1,0:T(8,128)S(1)}, f32[8,24,128]{2,1,0:T(8,128)S(1)}, u32[]{:S(2)}, u32[]{:S(2)}) collective-permute-start(f32[8,24,128]{2,1,0:T(8,128)S(1)} %get-tuple-element.24.plane), channel_id=1, source_target_pairs={{64,0},{72,8},{80,16},{88,24},{96,32},{104,40},{112,48},{120,56},{... | collective-permute-start | bytes 294920 | tf_op jit(solution)/shard_map/ppermute | solution.py:607
  53.3 15.3 %collective-permute-start.7 = (f32[8,24,128]{2,1,0:T(8,128)S(1)}, f32[8,24,128]{2,1,0:T(8,128)S(1)}, u32[]{:S(2)}, u32[]{:S(2)}) collective-permute-start(f32[8,24,128]{2,1,0:T(8,128)S(1)} %get-tuple-element.24.plane), channel_id=1, source_target_pairs={{0,64},{8,72},{16,80},{24,88},{32,96},{40,104},{48,112},{56,120},{... | collective-permute-start | bytes 294920 | tf_op jit(solution)/shard_map/ppermute | solution.py:606
  57.6 11.0 %collective-permute-start.6 = (f32[3,24,128]{2,1,0:T(8,128)S(1)}, f32[3,24,128]{2,1,0:T(8,128)S(1)}, u32[]{:S(2)}, u32[]{:S(2)}) collective-permute-start(f32[3,24,128]{2,1,0:T(8,128)S(1)} %get-tuple-element.25), channel_id=1, source_target_pairs={{0,128},{8,136},{16,144},{64,192},{72,200},{80,208},{128,256},{136... | collective-permute-start | bytes 110600 | tf_op jit(solution)/shard_map/ppermute | solution.py:605

commit v4 on v3

--- a/solution.py
+++ b/solution.py
@@ -251,7 +251,7 @@
     parity_copy(lax.axis_index("gy") % 2 == 0, to_inside, to_across, lambda left, right: pack_all(right, left))
 
 
-def widen_kernel(right_side, guess, vertical, breaking, across, inside, q, to_on, to_off):
+def widen_kernel(right_side, guess, vertical, breaking, inside, across, q, to_on, to_off):
     lane = lanes(16)
 
     def assemble(from_left, from_right):
@@ -574,7 +574,7 @@
         "widen",
         [(PLANES + 2, 8, 16, 128), (7, X_ROWS, 128), (7, X_ROWS, 128)],
         [],
-        right_side, guess, vertical, breaking, across, inside,
+        right_side, guess, vertical, breaking, inside, across,
     )
     off = lax.ppermute(to_off, "gx", gap)
     on = lax.ppermute(to_on, "gx", chip)

time: 73.6 us -> 72.7 us (0.988)
  the two profiles are of different devices: /device:TPU:88 before, /device:TPU:96 now
where the time goes in v4:
time: 72.7 us; the launch traced here: 72.3 us
  starting transfers between devices  29.6 us (41%)
  waiting for transfers between devices  20 us (28%)
  Pallas kernels  13.1 us (18%)
  blocking collectives  8.81 us (12%)
  between operations  0.79 us (1%)
    pallas_call x6, Pallas kernels, call(): pl.pallas_call(kernel, name=name, out_shape=[jax.ShapeDtypeStruct(s, F32)...  13.1 us
    ppermute x1, starting transfers between devices, shards(): beyond = lax.ppermute(edge, 'gx', far)  9.36 us
    all_to_all x1, blocking collectives, shards(): lax.all_to_all(chunk, 'gx', 0, 0, axis_index_groups=groups, tiled=True)  8.81 us
    ppermute x1, waiting for transfers between devices, shards(): off = lax.ppermute(to_off, 'gx', gap)  7.39 us
    ppermute x1, starting transfers between devices, shards(): lax.ppermute(plane, 'gx', [(i, i + PLANE) for i in range(nx - PLANE)])  4.28 us
    ppermute x1, waiting for transfers between devices, shards(): off = lax.ppermute(f2_own, 'gx', gap)  4.07 us
    ppermute x1, waiting for transfers between devices, shards(): across = lax.ppermute(to_across, 'gy', across + [(b, a) for a, b in across])  3.53 us
    ppermute x1, starting transfers between devices, shards(): on = lax.ppermute(to_on, 'gx', chip)  3.42 us
  transfers between devices with their start and end apart: 9, of which 5 were waited for; matrix products, arithmetic and copies ran while one was open for 0% of the time, Pallas kernels for 0%

profile of v4, /device:TPU:96, one launch (start us, length us, event | category | flops | bytes accessed | tf_op | source)
XLA Modules:
  0.0 72.3 jit_solution(2623412591044382498)
XLA Ops:
  0.6 0.0 copy-start
  0.6 0.0 copy-start.3
  0.7 0.0 copy-start.2
  0.7 0.0 copy-start.1
  0.7 2.6 %pack.1 = (f32[328,128]{1,0:T(8,128)}, f32[328,128]{1,0:T(8,128)}) custom-call(f32[9,16,512]{2,1,0:T(8,128)} %right_side.1, f32[9,16,512]{2,1,0:T(8,128)} %guess.3, f32[16,512]{1,0:T(8,128)} %vertical.1, s32[16,512]{1,0:T(8,128)} %breaking.1), custom_call_target="tpu_custom_call" | custom-call | tf_op jit(solution)/shard_map/pack/pallas_call | solution.py:538
  3.3 2.6 %collective-permute-start = (f32[328,128]{1,0:T(8,128)}, f32[328,128]{1,0:T(8,128)S(1)}, u32[]{:S(2)}, u32[]{:S(2)}) collective-permute-start(f32[328,128]{1,0:T(8,128)} %get-tuple-element.17), channel_id=1, source_target_pairs={{0,1},{1,0},{2,3},{3,2},{4,5},{5,4},{6,7},{7,6},{8,9},{9,8},{10,11... | collective-permute-start | bytes 503816 | tf_op jit(solution)/shard_map/ppermute | solution.py:571
  5.9 2.1 %collective-permute-start.1 = (f32[328,128]{1,0:T(8,128)}, f32[328,128]{1,0:T(8,128)S(1)}, u32[]{:S(2)}, u32[]{:S(2)}) collective-permute-start(f32[328,128]{1,0:T(8,128)} %get-tuple-element.18), channel_id=1, source_target_pairs={{1,2},{3,4},{5,6},{2,1},{4,3},{6,5},{9,10},{11,12},{13,14},{10,9},... | collective-permute-start | bytes 503816 | tf_op jit(solution)/shard_map/ppermute | solution.py:570
  8.0 3.4 %collective-permute-done.inside = f32[328,128]{1,0:T(8,128)S(1)} collective-permute-done((f32[328,128]{1,0:T(8,128)}, f32[328,128]{1,0:T(8,128)S(1)}, u32[]{:S(2)}, u32[]{:S(2)}) %collective-permute-start) | collective-permute-done | bytes 167968 | tf_op jit(solution)/shard_map/ppermute | solution.py:571
  11.4 3.5 %collective-permute-done.1.across = f32[328,128]{1,0:T(8,128)S(1)} collective-permute-done((f32[328,128]{1,0:T(8,128)}, f32[328,128]{1,0:T(8,128)S(1)}, u32[]{:S(2)}, u32[]{:S(2)}) %collective-permute-start.1) | collective-permute-done | bytes 167968 | tf_op jit(solution)/shard_map/ppermute | solution.py:570
  15.0 0.0 copy-done
  15.0 0.0 copy-done.3
  15.0 0.0 copy-done.2
  15.0 0.0 copy-done.1
  15.0 0.5 widen.1
  15.5 2.0 %collective-permute-start.2 = (f32[7,152,128]{2,1,0:T(8,128)S(1)}, f32[7,152,128]{2,1,0:T(8,128)S(1)}, u32[]{:S(2)}, u32[]{:S(2)}) collective-permute-start(f32[7,152,128]{2,1,0:T(8,128)S(1)} %get-tuple-element.20), channel_id=1, source_target_pairs={{8,16},{24,32},{40,48},{56,64},{72,80},{88,96},{104,112},{120,128}... | collective-permute-start | bytes 1634312 | tf_op jit(solution)/shard_map/ppermute | solution.py:579
  17.6 3.4 %collective-permute-start.3 = (f32[7,152,128]{2,1,0:T(8,128)S(1)}, f32[7,152,128]{2,1,0:T(8,128)S(1)}, u32[]{:S(2)}, u32[]{:S(2)}) collective-permute-start(f32[7,152,128]{2,1,0:T(8,128)S(1)} %get-tuple-element.21), channel_id=1, source_target_pairs={{0,8},{8,0},{16,24},{24,16},{32,40},{40,32},{48,56},{56,48},{64,72... | collective-permute-start | bytes 1634312 | tf_op jit(solution)/shard_map/ppermute | solution.py:580
  21.0 7.4 %collective-permute-done.2.off = f32[7,152,128]{2,1,0:T(8,128)S(1)} collective-permute-done((f32[7,152,128]{2,1,0:T(8,128)S(1)}, f32[7,152,128]{2,1,0:T(8,128)S(1)}, u32[]{:S(2)}, u32[]{:S(2)}) %collective-permute-start.2) | collective-permute-done | bytes 544800 | tf_op jit(solution)/shard_map/ppermute | solution.py:579
  28.4 0.0 collective-permute-done.3.on
  28.4 4.7 %fine.1 = (f32[9,6,24,128]{3,2,1,0:T(8,128)S(1)}, f32[11,6,24,128]{3,2,1,0:T(8,128)S(1)}, f32[9,4,16,128]{3,2,1,0:T(8,128)S(1)}, f32[11,4,16,128]{3,2,1,0:T(8,128)S(1)}, f32[11,2,8,128]{3,2,1,0:T(8,128)S(1)}) custom-call(f32[13,8,16,128]{3,2,1,0:T(8,128)S(1)} %get-tuple-element.19.q, f32[7,152,128]{2,1,0:T(8,128)S(1)} %collective-permute-done.2.off, ...), custom_call_target="tpu_custom_call" | custom-call | tf_op jit(solution)/shard_map/fine/pallas_call | solution.py:538
  33.1 2.0 %collective-permute-start.5 = (f32[11,2,8,128]{3,2,1,0:T(8,128)S(1)}, f32[11,2,8,128]{3,2,1,0:T(8,128)S(1)}, u32[]{:S(2)}, u32[]{:S(2)}) collective-permute-start(f32[11,2,8,128]{3,2,1,0:T(8,128)S(1)} %get-tuple-element.22.own), channel_id=1, source_target_pairs={{8,16},{24,32},{40,48},{56,64},{72,80},{88,96},{104,112},{120,128}... | collective-permute-start | bytes 270344 | tf_op jit(solution)/shard_map/ppermute | solution.py:591
  35.1 1.9 %collective-permute-start.4 = (f32[11,2,8,128]{3,2,1,0:T(8,128)S(1)}, f32[11,2,8,128]{3,2,1,0:T(8,128)S(1)}, u32[]{:S(2)}, u32[]{:S(2)}) collective-permute-start(f32[11,2,8,128]{3,2,1,0:T(8,128)S(1)} %get-tuple-element.22.own), channel_id=1, source_target_pairs={{0,8},{8,0},{16,24},{24,16},{32,40},{40,32},{48,56},{56,48},{64,72... | collective-permute-start | bytes 270344 | tf_op jit(solution)/shard_map/ppermute | solution.py:592
  37.0 4.1 %collective-permute-done.5.off = f32[11,2,8,128]{3,2,1,0:T(8,128)S(1)} collective-permute-done((f32[11,2,8,128]{3,2,1,0:T(8,128)S(1)}, f32[11,2,8,128]{3,2,1,0:T(8,128)S(1)}, u32[]{:S(2)}, u32[]{:S(2)}) %collective-permute-start.5) | collective-permute-done | bytes 90144 | tf_op jit(solution)/shard_map/ppermute | solution.py:591
  41.1 0.0 collective-permute-done.4.on
  41.1 0.5 middle.1
  41.6 8.8 %all_to_all.5.plane = f32[8,24,128]{2,1,0:T(8,128)S(1)} all-to-all(f32[8,24,128]{2,1,0:T(8,128)S(1)} %get-tuple-element.23), channel_id=1, replica_groups={{0,8,16,24,32,40,48,56},{64,72,80,88,96,104,112,120},{128,136,144,152,1..., dimensions={0} | all-to-all | bytes 196608 | tf_op jit(solution)/shard_map/all_to_all | solution.py:601
  50.4 1.9 %collective-permute-start.8 = (f32[8,24,128]{2,1,0:T(8,128)S(1)}, f32[8,24,128]{2,1,0:T(8,128)S(1)}, u32[]{:S(2)}, u32[]{:S(2)}) collective-permute-start(f32[8,24,128]{2,1,0:T(8,128)S(1)} %get-tuple-element.24.plane), channel_id=1, source_target_pairs={{64,0},{72,8},{80,16},{88,24},{96,32},{104,40},{112,48},{120,56},{... | collective-permute-start | bytes 294920 | tf_op jit(solution)/shard_map/ppermute | solution.py:607
  52.4 4.3 %collective-permute-start.7 = (f32[8,24,128]{2,1,0:T(8,128)S(1)}, f32[8,24,128]{2,1,0:T(8,128)S(1)}, u32[]{:S(2)}, u32[]{:S(2)}) collective-permute-start(f32[8,24,128]{2,1,0:T(8,128)S(1)} %get-tuple-element.24.plane), channel_id=1, source_target_pairs={{0,64},{8,72},{16,80},{24,88},{32,96},{40,104},{48,112},{56,120},{... | collective-permute-start | bytes 294920 | tf_op jit(solution)/shard_map/ppermute | solution.py:606
  56.7 9.4 %collective-permute-start.6 = (f32[3,24,128]{2,1,0:T(8,128)S(1)}, f32[3,24,128]{2,1,0:T(8,128)S(1)}, u32[]{:S(2)}, u32[]{:S(2)}) collective-permute-start(f32[3,24,128]{2,1,0:T(8,128)S(1)} %get-tuple-element.25), channel_id=1, source_target_pairs={{0,128},{8,136},{16,144},{64,192},{72,200},{80,208},{128,256},{136... | collective-permute-start | bytes 110600 | tf_op jit(solution)/shard_map/ppermute | solution.py:605
  66.0 1.6 %collective-permute-done.6.beyond = f32[3,24,128]{2,1,0:T(8,128)S(1)} collective-permute-done((f32[3,24,128]{2,1,0:T(8,128)S(1)}, f32[3,24,128]{2,1,0:T(8,128)S(1)}, u32[]{:S(2)}, u32[]{:S(2)}) %collective-permute-start.6) | collective-permute-done | bytes 36896 | tf_op jit(solution)/shard_map/ppermute | solution.py:605
  67.6 0.0 collective-permute-done.8.after
  67.6 0.0 collective-permute-done.7.before
  67.7 4.7 %coarse.1 = (f32[9,16,512]{2,1,0:T(8,128)}, f32[9,16,512]{2,1,0:T(8,128)}) custom-call(f32[8,24,128]{2,1,0:T(8,128)S(1)} %get-tuple-element.24.plane, f32[3,24,128]{2,1,0:T(8,128)S(1)} %collective-permute-done.6.beyond, f32[8,24,128]{2,1,0:T(8,128)S(1)} %collective-permute-done.7.before, f32[8,24,128]{2,1,0:T(8,128)S(1)} %collective-permute-done.8.after, ...), custom_call_target="tpu_custom_call" | custom-call | tf_op jit(solution)/shard_map/coarse/pallas_call | solution.py:538
  (1 shorter events, 0.0 us)
Async XLA Ops:
  0.6 14.3 %copy-start = (f32[9,16,512]{2,1,0:T(8,128)S(1)}, f32[9,16,512]{2,1,0:T(8,128)}, u32[]{:S(2)}) copy-start(f32[9,16,512]{2,1,0:T(8,128)} %guess.3) | copy-start | bytes 884740
  0.6 14.3 %copy-start.3 = (s32[16,512]{1,0:T(8,128)S(1)}, s32[16,512]{1,0:T(8,128)}, u32[]{:S(2)}) copy-start(s32[16,512]{1,0:T(8,128)} %breaking.1) | copy-start | bytes 98308
  0.7 14.3 %copy-start.2 = (f32[16,512]{1,0:T(8,128)S(1)}, f32[16,512]{1,0:T(8,128)}, u32[]{:S(2)}) copy-start(f32[16,512]{1,0:T(8,128)} %vertical.1) | copy-start | bytes 98308
  0.7 14.3 %copy-start.1 = (f32[9,16,512]{2,1,0:T(8,128)S(1)}, f32[9,16,512]{2,1,0:T(8,128)}, u32[]{:S(2)}) copy-start(f32[9,16,512]{2,1,0:T(8,128)} %right_side.1) | copy-start | bytes 884740
  3.3 8.1 %collective-permute-start = (f32[328,128]{1,0:T(8,128)}, f32[328,128]{1,0:T(8,128)S(1)}, u32[]{:S(2)}, u32[]{:S(2)}) collective-permute-start(f32[328,128]{1,0:T(8,128)} %get-tuple-element.17), channel_id=1, source_target_pairs={{0,1},{1,0},{2,3},{3,2},{4,5},{5,4},{6,7},{7,6},{8,9},{9,8},{10,11... | collective-permute-start | bytes 503816 | tf_op jit(solution)/shard_map/ppermute | solution.py:571
  5.9 9.1 %collective-permute-start.1 = (f32[328,128]{1,0:T(8,128)}, f32[328,128]{1,0:T(8,128)S(1)}, u32[]{:S(2)}, u32[]{:S(2)}) collective-permute-start(f32[328,128]{1,0:T(8,128)} %get-tuple-element.18), channel_id=1, source_target_pairs={{1,2},{3,4},{5,6},{2,1},{4,3},{6,5},{9,10},{11,12},{13,14},{10,9},... | collective-permute-start | bytes 503816 | tf_op jit(solution)/shard_map/ppermute | solution.py:570
  15.5 12.8 %collective-permute-start.2 = (f32[7,152,128]{2,1,0:T(8,128)S(1)}, f32[7,152,128]{2,1,0:T(8,128)S(1)}, u32[]{:S(2)}, u32[]{:S(2)}) collective-permute-start(f32[7,152,128]{2,1,0:T(8,128)S(1)} %get-tuple-element.20), channel_id=1, source_target_pairs={{8,16},{24,32},{40,48},{56,64},{72,80},{88,96},{104,112},{120,128}... | collective-permute-start | bytes 1634312 | tf_op jit(solution)/shard_map/ppermute | solution.py:579
  17.6 10.8 %collective-permute-start.3 = (f32[7,152,128]{2,1,0:T(8,128)S(1)}, f32[7,152,128]{2,1,0:T(8,128)S(1)}, u32[]{:S(2)}, u32[]{:S(2)}) collective-permute-start(f32[7,152,128]{2,1,0:T(8,128)S(1)} %get-tuple-element.21), channel_id=1, source_target_pairs={{0,8},{8,0},{16,24},{24,16},{32,40},{40,32},{48,56},{56,48},{64,72... | collective-permute-start | bytes 1634312 | tf_op jit(solution)/shard_map/ppermute | solution.py:580
  33.1 8.0 %collective-permute-start.5 = (f32[11,2,8,128]{3,2,1,0:T(8,128)S(1)}, f32[11,2,8,128]{3,2,1,0:T(8,128)S(1)}, u32[]{:S(2)}, u32[]{:S(2)}) collective-permute-start(f32[11,2,8,128]{3,2,1,0:T(8,128)S(1)} %get-tuple-element.22.own), channel_id=1, source_target_pairs={{8,16},{24,32},{40,48},{56,64},{72,80},{88,96},{104,112},{120,128}... | collective-permute-start | bytes 270344 | tf_op jit(solution)/shard_map/ppermute | solution.py:591
  35.1 6.0 %collective-permute-start.4 = (f32[11,2,8,128]{3,2,1,0:T(8,128)S(1)}, f32[11,2,8,128]{3,2,1,0:T(8,128)S(1)}, u32[]{:S(2)}, u32[]{:S(2)}) collective-permute-start(f32[11,2,8,128]{3,2,1,0:T(8,128)S(1)} %get-tuple-element.22.own), channel_id=1, source_target_pairs={{0,8},{8,0},{16,24},{24,16},{32,40},{40,32},{48,56},{56,48},{64,72... | collective-permute-start | bytes 270344 | tf_op jit(solution)/shard_map/ppermute | solution.py:592
  50.4 17.2 %collective-permute-start.8 = (f32[8,24,128]{2,1,0:T(8,128)S(1)}, f32[8,24,128]{2,1,0:T(8,128)S(1)}, u32[]{:S(2)}, u32[]{:S(2)}) collective-permute-start(f32[8,24,128]{2,1,0:T(8,128)S(1)} %get-tuple-element.24.plane), channel_id=1, source_target_pairs={{64,0},{72,8},{80,16},{88,24},{96,32},{104,40},{112,48},{120,56},{... | collective-permute-start | bytes 294920 | tf_op jit(solution)/shard_map/ppermute | solution.py:607
  52.4 15.3 %collective-permute-start.7 = (f32[8,24,128]{2,1,0:T(8,128)S(1)}, f32[8,24,128]{2,1,0:T(8,128)S(1)}, u32[]{:S(2)}, u32[]{:S(2)}) collective-permute-start(f32[8,24,128]{2,1,0:T(8,128)S(1)} %get-tuple-element.24.plane), channel_id=1, source_target_pairs={{0,64},{8,72},{16,80},{24,88},{32,96},{40,104},{48,112},{56,120},{... | collective-permute-start | bytes 294920 | tf_op jit(solution)/shard_map/ppermute | solution.py:606
  56.7 11.0 %collective-permute-start.6 = (f32[3,24,128]{2,1,0:T(8,128)S(1)}, f32[3,24,128]{2,1,0:T(8,128)S(1)}, u32[]{:S(2)}, u32[]{:S(2)}) collective-permute-start(f32[3,24,128]{2,1,0:T(8,128)S(1)} %get-tuple-element.25), channel_id=1, source_target_pairs={{0,128},{8,136},{16,144},{64,192},{72,200},{80,208},{128,256},{136... | collective-permute-start | bytes 110600 | tf_op jit(solution)/shard_map/ppermute | solution.py:605

commit v5 on v4

--- a/solution.py
+++ b/solution.py
@@ -20,9 +20,9 @@
 
 COLS_AT = 24 * PLANES
 TOP_AT = COLS_AT + 16
-BOTTOM_AT = TOP_AT + 16
-FAR_AT = BOTTOM_AT + 16
-Y_ROWS = FAR_AT + 16
+BOTTOM_AT = TOP_AT + K
+FAR_AT = BOTTOM_AT + K
+Y_ROWS = FAR_AT + K + 5
 
 SHORT_AT = 8 * PLANES
 GUESS_AT = SHORT_AT + 5 * PLANES

time: 72.7 us -> 72.6 us (level)
  no operation moved by 1% of the time
where the time goes in v5:
time: 72.6 us; the launch traced here: 72.2 us
  starting transfers between devices  29.6 us (41%)
  waiting for transfers between devices  19.8 us (27%)
  Pallas kernels  13.1 us (18%)
  blocking collectives  8.82 us (12%)
  between operations  0.79 us (1%)
    pallas_call x6, Pallas kernels, call(): pl.pallas_call(kernel, name=name, out_shape=[jax.ShapeDtypeStruct(s, F32)...  13.1 us
    ppermute x1, starting transfers between devices, shards(): beyond = lax.ppermute(edge, 'gx', far)  9.37 us
    all_to_all x1, blocking collectives, shards(): lax.all_to_all(chunk, 'gx', 0, 0, axis_index_groups=groups, tiled=True)  8.82 us
    ppermute x1, waiting for transfers between devices, shards(): off = lax.ppermute(to_off, 'gx', gap)  7.39 us
    ppermute x1, starting transfers between devices, shards(): lax.ppermute(plane, 'gx', [(i, i + PLANE) for i in range(nx - PLANE)])  4.28 us
    ppermute x1, waiting for transfers between devices, shards(): off = lax.ppermute(f2_own, 'gx', gap)  4.07 us
    ppermute x1, waiting for transfers between devices, shards(): across = lax.ppermute(to_across, 'gy', across + [(b, a) for a, b in across])  3.53 us
    ppermute x1, starting transfers between devices, shards(): on = lax.ppermute(to_on, 'gx', chip)  3.42 us
  transfers between devices with their start and end apart: 9, of which 5 were waited for; matrix products, arithmetic and copies ran while one was open for 0% of the time, Pallas kernels for 0%

profile of v5, /device:TPU:96, one launch (start us, length us, event | category | flops | bytes accessed | tf_op | source)
XLA Modules:
  0.0 72.2 jit_solution(3644900780011560124)
XLA Ops:
  0.6 0.0 copy-start
  0.6 0.0 copy-start.3
  0.7 0.0 copy-start.2
  0.7 0.0 copy-start.1
  0.7 2.6 %pack.1 = (f32[312,128]{1,0:T(8,128)}, f32[312,128]{1,0:T(8,128)}) custom-call(f32[9,16,512]{2,1,0:T(8,128)} %right_side.1, f32[9,16,512]{2,1,0:T(8,128)} %guess.3, f32[16,512]{1,0:T(8,128)} %vertical.1, s32[16,512]{1,0:T(8,128)} %breaking.1), custom_call_target="tpu_custom_call" | custom-call | tf_op jit(solution)/shard_map/pack/pallas_call | solution.py:538
  3.3 2.6 %collective-permute-start = (f32[312,128]{1,0:T(8,128)}, f32[312,128]{1,0:T(8,128)S(1)}, u32[]{:S(2)}, u32[]{:S(2)}) collective-permute-start(f32[312,128]{1,0:T(8,128)} %get-tuple-element.17), channel_id=1, source_target_pairs={{0,1},{1,0},{2,3},{3,2},{4,5},{5,4},{6,7},{7,6},{8,9},{9,8},{10,11... | collective-permute-start | bytes 479240 | tf_op jit(solution)/shard_map/ppermute | solution.py:571
  5.9 2.1 %collective-permute-start.1 = (f32[312,128]{1,0:T(8,128)}, f32[312,128]{1,0:T(8,128)S(1)}, u32[]{:S(2)}, u32[]{:S(2)}) collective-permute-start(f32[312,128]{1,0:T(8,128)} %get-tuple-element.18), channel_id=1, source_target_pairs={{1,2},{3,4},{5,6},{2,1},{4,3},{6,5},{9,10},{11,12},{13,14},{10,9},... | collective-permute-start | bytes 479240 | tf_op jit(solution)/shard_map/ppermute | solution.py:570
  8.0 3.2 %collective-permute-done.inside = f32[312,128]{1,0:T(8,128)S(1)} collective-permute-done((f32[312,128]{1,0:T(8,128)}, f32[312,128]{1,0:T(8,128)S(1)}, u32[]{:S(2)}, u32[]{:S(2)}) %collective-permute-start) | collective-permute-done | bytes 159776 | tf_op jit(solution)/shard_map/ppermute | solution.py:571
  11.3 3.5 %collective-permute-done.1.across = f32[312,128]{1,0:T(8,128)S(1)} collective-permute-done((f32[312,128]{1,0:T(8,128)}, f32[312,128]{1,0:T(8,128)S(1)}, u32[]{:S(2)}, u32[]{:S(2)}) %collective-permute-start.1) | collective-permute-done | bytes 159776 | tf_op jit(solution)/shard_map/ppermute | solution.py:570
  14.8 0.0 copy-done
  14.8 0.0 copy-done.3
  14.8 0.0 copy-done.2
  14.8 0.0 copy-done.1
  14.8 0.5 widen.1
  15.4 2.0 %collective-permute-start.2 = (f32[7,152,128]{2,1,0:T(8,128)S(1)}, f32[7,152,128]{2,1,0:T(8,128)S(1)}, u32[]{:S(2)}, u32[]{:S(2)}) collective-permute-start(f32[7,152,128]{2,1,0:T(8,128)S(1)} %get-tuple-element.20), channel_id=1, source_target_pairs={{8,16},{24,32},{40,48},{56,64},{72,80},{88,96},{104,112},{120,128}... | collective-permute-start | bytes 1634312 | tf_op jit(solution)/shard_map/ppermute | solution.py:579
  17.4 3.4 %collective-permute-start.3 = (f32[7,152,128]{2,1,0:T(8,128)S(1)}, f32[7,152,128]{2,1,0:T(8,128)S(1)}, u32[]{:S(2)}, u32[]{:S(2)}) collective-permute-start(f32[7,152,128]{2,1,0:T(8,128)S(1)} %get-tuple-element.21), channel_id=1, source_target_pairs={{0,8},{8,0},{16,24},{24,16},{32,40},{40,32},{48,56},{56,48},{64,72... | collective-permute-start | bytes 1634312 | tf_op jit(solution)/shard_map/ppermute | solution.py:580
  20.8 7.4 %collective-permute-done.2.off = f32[7,152,128]{2,1,0:T(8,128)S(1)} collective-permute-done((f32[7,152,128]{2,1,0:T(8,128)S(1)}, f32[7,152,128]{2,1,0:T(8,128)S(1)}, u32[]{:S(2)}, u32[]{:S(2)}) %collective-permute-start.2) | collective-permute-done | bytes 544800 | tf_op jit(solution)/shard_map/ppermute | solution.py:579
  28.2 0.0 collective-permute-done.3.on
  28.2 4.7 %fine.1 = (f32[9,6,24,128]{3,2,1,0:T(8,128)S(1)}, f32[11,6,24,128]{3,2,1,0:T(8,128)S(1)}, f32[9,4,16,128]{3,2,1,0:T(8,128)S(1)}, f32[11,4,16,128]{3,2,1,0:T(8,128)S(1)}, f32[11,2,8,128]{3,2,1,0:T(8,128)S(1)}) custom-call(f32[13,8,16,128]{3,2,1,0:T(8,128)S(1)} %get-tuple-element.19.q, f32[7,152,128]{2,1,0:T(8,128)S(1)} %collective-permute-done.2.off, ...), custom_call_target="tpu_custom_call" | custom-call | tf_op jit(solution)/shard_map/fine/pallas_call | solution.py:538
  32.9 2.0 %collective-permute-start.5 = (f32[11,2,8,128]{3,2,1,0:T(8,128)S(1)}, f32[11,2,8,128]{3,2,1,0:T(8,128)S(1)}, u32[]{:S(2)}, u32[]{:S(2)}) collective-permute-start(f32[11,2,8,128]{3,2,1,0:T(8,128)S(1)} %get-tuple-element.22.own), channel_id=1, source_target_pairs={{8,16},{24,32},{40,48},{56,64},{72,80},{88,96},{104,112},{120,128}... | collective-permute-start | bytes 270344 | tf_op jit(solution)/shard_map/ppermute | solution.py:591
  34.9 1.9 %collective-permute-start.4 = (f32[11,2,8,128]{3,2,1,0:T(8,128)S(1)}, f32[11,2,8,128]{3,2,1,0:T(8,128)S(1)}, u32[]{:S(2)}, u32[]{:S(2)}) collective-permute-start(f32[11,2,8,128]{3,2,1,0:T(8,128)S(1)} %get-tuple-element.22.own), channel_id=1, source_target_pairs={{0,8},{8,0},{16,24},{24,16},{32,40},{40,32},{48,56},{56,48},{64,72... | collective-permute-start | bytes 270344 | tf_op jit(solution)/shard_map/ppermute | solution.py:592
  36.8 4.1 %collective-permute-done.5.off = f32[11,2,8,128]{3,2,1,0:T(8,128)S(1)} collective-permute-done((f32[11,2,8,128]{3,2,1,0:T(8,128)S(1)}, f32[11,2,8,128]{3,2,1,0:T(8,128)S(1)}, u32[]{:S(2)}, u32[]{:S(2)}) %collective-permute-start.5) | collective-permute-done | bytes 90144 | tf_op jit(solution)/shard_map/ppermute | solution.py:591
  40.9 0.0 collective-permute-done.4.on
  40.9 0.5 middle.1
  41.4 8.8 %all_to_all.5.plane = f32[8,24,128]{2,1,0:T(8,128)S(1)} all-to-all(f32[8,24,128]{2,1,0:T(8,128)S(1)} %get-tuple-element.23), channel_id=1, replica_groups={{0,8,16,24,32,40,48,56},{64,72,80,88,96,104,112,120},{128,136,144,152,1..., dimensions={0} | all-to-all | bytes 196608 | tf_op jit(solution)/shard_map/all_to_all | solution.py:601
  50.3 1.9 %collective-permute-start.8 = (f32[8,24,128]{2,1,0:T(8,128)S(1)}, f32[8,24,128]{2,1,0:T(8,128)S(1)}, u32[]{:S(2)}, u32[]{:S(2)}) collective-permute-start(f32[8,24,128]{2,1,0:T(8,128)S(1)} %get-tuple-element.24.plane), channel_id=1, source_target_pairs={{64,0},{72,8},{80,16},{88,24},{96,32},{104,40},{112,48},{120,56},{... | collective-permute-start | bytes 294920 | tf_op jit(solution)/shard_map/ppermute | solution.py:607
  52.2 4.3 %collective-permute-start.7 = (f32[8,24,128]{2,1,0:T(8,128)S(1)}, f32[8,24,128]{2,1,0:T(8,128)S(1)}, u32[]{:S(2)}, u32[]{:S(2)}) collective-permute-start(f32[8,24,128]{2,1,0:T(8,128)S(1)} %get-tuple-element.24.plane), channel_id=1, source_target_pairs={{0,64},{8,72},{16,80},{24,88},{32,96},{40,104},{48,112},{56,120},{... | collective-permute-start | bytes 294920 | tf_op jit(solution)/shard_map/ppermute | solution.py:606
  56.5 9.4 %collective-permute-start.6 = (f32[3,24,128]{2,1,0:T(8,128)S(1)}, f32[3,24,128]{2,1,0:T(8,128)S(1)}, u32[]{:S(2)}, u32[]{:S(2)}) collective-permute-start(f32[3,24,128]{2,1,0:T(8,128)S(1)} %get-tuple-element.25), channel_id=1, source_target_pairs={{0,128},{8,136},{16,144},{64,192},{72,200},{80,208},{128,256},{136... | collective-permute-start | bytes 110600 | tf_op jit(solution)/shard_map/ppermute | solution.py:605
  65.9 1.6 %collective-permute-done.6.beyond = f32[3,24,128]{2,1,0:T(8,128)S(1)} collective-permute-done((f32[3,24,128]{2,1,0:T(8,128)S(1)}, f32[3,24,128]{2,1,0:T(8,128)S(1)}, u32[]{:S(2)}, u32[]{:S(2)}) %collective-permute-start.6) | collective-permute-done | bytes 36896 | tf_op jit(solution)/shard_map/ppermute | solution.py:605
  67.5 0.0 collective-permute-done.8.after
  67.5 0.0 collective-permute-done.7.before
  67.5 4.7 %coarse.1 = (f32[9,16,512]{2,1,0:T(8,128)}, f32[9,16,512]{2,1,0:T(8,128)}) custom-call(f32[8,24,128]{2,1,0:T(8,128)S(1)} %get-tuple-element.24.plane, f32[3,24,128]{2,1,0:T(8,128)S(1)} %collective-permute-done.6.beyond, f32[8,24,128]{2,1,0:T(8,128)S(1)} %collective-permute-done.7.before, f32[8,24,128]{2,1,0:T(8,128)S(1)} %collective-permute-done.8.after, ...), custom_call_target="tpu_custom_call" | custom-call | tf_op jit(solution)/shard_map/coarse/pallas_call | solution.py:538
  (1 shorter events, 0.0 us)
Async XLA Ops:
  0.6 14.2 %copy-start = (f32[9,16,512]{2,1,0:T(8,128)S(1)}, f32[9,16,512]{2,1,0:T(8,128)}, u32[]{:S(2)}) copy-start(f32[9,16,512]{2,1,0:T(8,128)} %guess.3) | copy-start | bytes 884740
  0.6 14.2 %copy-start.3 = (s32[16,512]{1,0:T(8,128)S(1)}, s32[16,512]{1,0:T(8,128)}, u32[]{:S(2)}) copy-start(s32[16,512]{1,0:T(8,128)} %breaking.1) | copy-start | bytes 98308
  0.7 14.1 %copy-start.2 = (f32[16,512]{1,0:T(8,128)S(1)}, f32[16,512]{1,0:T(8,128)}, u32[]{:S(2)}) copy-start(f32[16,512]{1,0:T(8,128)} %vertical.1) | copy-start | bytes 98308
  0.7 14.1 %copy-start.1 = (f32[9,16,512]{2,1,0:T(8,128)S(1)}, f32[9,16,512]{2,1,0:T(8,128)}, u32[]{:S(2)}) copy-start(f32[9,16,512]{2,1,0:T(8,128)} %right_side.1) | copy-start | bytes 884740
  3.3 8.0 %collective-permute-start = (f32[312,128]{1,0:T(8,128)}, f32[312,128]{1,0:T(8,128)S(1)}, u32[]{:S(2)}, u32[]{:S(2)}) collective-permute-start(f32[312,128]{1,0:T(8,128)} %get-tuple-element.17), channel_id=1, source_target_pairs={{0,1},{1,0},{2,3},{3,2},{4,5},{5,4},{6,7},{7,6},{8,9},{9,8},{10,11... | collective-permute-start | bytes 479240 | tf_op jit(solution)/shard_map/ppermute | solution.py:571
  5.9 8.9 %collective-permute-start.1 = (f32[312,128]{1,0:T(8,128)}, f32[312,128]{1,0:T(8,128)S(1)}, u32[]{:S(2)}, u32[]{:S(2)}) collective-permute-start(f32[312,128]{1,0:T(8,128)} %get-tuple-element.18), channel_id=1, source_target_pairs={{1,2},{3,4},{5,6},{2,1},{4,3},{6,5},{9,10},{11,12},{13,14},{10,9},... | collective-permute-start | bytes 479240 | tf_op jit(solution)/shard_map/ppermute | solution.py:570
  15.4 12.8 %collective-permute-start.2 = (f32[7,152,128]{2,1,0:T(8,128)S(1)}, f32[7,152,128]{2,1,0:T(8,128)S(1)}, u32[]{:S(2)}, u32[]{:S(2)}) collective-permute-start(f32[7,152,128]{2,1,0:T(8,128)S(1)} %get-tuple-element.20), channel_id=1, source_target_pairs={{8,16},{24,32},{40,48},{56,64},{72,80},{88,96},{104,112},{120,128}... | collective-permute-start | bytes 1634312 | tf_op jit(solution)/shard_map/ppermute | solution.py:579
  17.4 10.8 %collective-permute-start.3 = (f32[7,152,128]{2,1,0:T(8,128)S(1)}, f32[7,152,128]{2,1,0:T(8,128)S(1)}, u32[]{:S(2)}, u32[]{:S(2)}) collective-permute-start(f32[7,152,128]{2,1,0:T(8,128)S(1)} %get-tuple-element.21), channel_id=1, source_target_pairs={{0,8},{8,0},{16,24},{24,16},{32,40},{40,32},{48,56},{56,48},{64,72... | collective-permute-start | bytes 1634312 | tf_op jit(solution)/shard_map/ppermute | solution.py:580
  32.9 8.0 %collective-permute-start.5 = (f32[11,2,8,128]{3,2,1,0:T(8,128)S(1)}, f32[11,2,8,128]{3,2,1,0:T(8,128)S(1)}, u32[]{:S(2)}, u32[]{:S(2)}) collective-permute-start(f32[11,2,8,128]{3,2,1,0:T(8,128)S(1)} %get-tuple-element.22.own), channel_id=1, source_target_pairs={{8,16},{24,32},{40,48},{56,64},{72,80},{88,96},{104,112},{120,128}... | collective-permute-start | bytes 270344 | tf_op jit(solution)/shard_map/ppermute | solution.py:591
  34.9 6.0 %collective-permute-start.4 = (f32[11,2,8,128]{3,2,1,0:T(8,128)S(1)}, f32[11,2,8,128]{3,2,1,0:T(8,128)S(1)}, u32[]{:S(2)}, u32[]{:S(2)}) collective-permute-start(f32[11,2,8,128]{3,2,1,0:T(8,128)S(1)} %get-tuple-element.22.own), channel_id=1, source_target_pairs={{0,8},{8,0},{16,24},{24,16},{32,40},{40,32},{48,56},{56,48},{64,72... | collective-permute-start | bytes 270344 | tf_op jit(solution)/shard_map/ppermute | solution.py:592
  50.3 17.2 %collective-permute-start.8 = (f32[8,24,128]{2,1,0:T(8,128)S(1)}, f32[8,24,128]{2,1,0:T(8,128)S(1)}, u32[]{:S(2)}, u32[]{:S(2)}) collective-permute-start(f32[8,24,128]{2,1,0:T(8,128)S(1)} %get-tuple-element.24.plane), channel_id=1, source_target_pairs={{64,0},{72,8},{80,16},{88,24},{96,32},{104,40},{112,48},{120,56},{... | collective-permute-start | bytes 294920 | tf_op jit(solution)/shard_map/ppermute | solution.py:607
  52.2 15.3 %collective-permute-start.7 = (f32[8,24,128]{2,1,0:T(8,128)S(1)}, f32[8,24,128]{2,1,0:T(8,128)S(1)}, u32[]{:S(2)}, u32[]{:S(2)}) collective-permute-start(f32[8,24,128]{2,1,0:T(8,128)S(1)} %get-tuple-element.24.plane), channel_id=1, source_target_pairs={{0,64},{8,72},{16,80},{24,88},{32,96},{40,104},{48,112},{56,120},{... | collective-permute-start | bytes 294920 | tf_op jit(solution)/shard_map/ppermute | solution.py:606
  56.5 11.0 %collective-permute-start.6 = (f32[3,24,128]{2,1,0:T(8,128)S(1)}, f32[3,24,128]{2,1,0:T(8,128)S(1)}, u32[]{:S(2)}, u32[]{:S(2)}) collective-permute-start(f32[3,24,128]{2,1,0:T(8,128)S(1)} %get-tuple-element.25), channel_id=1, source_target_pairs={{0,128},{8,136},{16,144},{64,192},{72,200},{80,208},{128,256},{136... | collective-permute-start | bytes 110600 | tf_op jit(solution)/shard_map/ppermute | solution.py:605
